TPU v7x, 32 devices: a whole 2x2x4 slice. The times are simulated.
32 devices in a mesh: row: 4 (over y, core), col: 8 (over z, x).
Axes of the slice: x: 2, y: 2, z: 4, core: 2. Of those that a mesh axis runs over, the one named last changes fastest.
Arguments:
- hidden_in: bfloat16 [16384, 1024], P(('row', 'col')), may hold values from -6 to 6
- cotangent: float32 [16384, 1024], P(('row', 'col')), may hold values from -6 to 6
- seq_lengths: int32 [16], replicated, may hold values from 1 to 1024, 10240 in all
- slot_of: int32 [16], replicated, may hold values from 0 to 15, each once
- project: bfloat16 [2, 1024, 3072], P(None, 'row', 'col'), may hold values from -0.1875 to 0.1875
- offsets: float32 [2, 2048], P(None, 'col'), may hold values from -1.5 to 1.5
- combiner: bfloat16 [2, 1024, 1024], P(None, 'col', 'row'), may hold values from -1.5 to 1.5
- recenter: float32 [2, 1024], replicated, may hold values from -1.5 to 1.5
- stretch: float32 [2, 1024], replicated, may hold values from 0.5 to 1.5
- displace: float32 [2, 1024], replicated, may hold values from -1.5 to 1.5
- expand: bfloat16 [2, 1024, 4096], P(None, 'row', 'col'), may hold values from -0.1875 to 0.1875
- uplift: float32 [2, 4096], P(None, 'col'), may hold values from -1.5 to 1.5
- shrink: bfloat16 [2, 4096, 1024], P(None, 'col', 'row'), may hold values from -0.09375 to 0.09375
- lowering: float32 [2, 1024], replicated, may hold values from -1.5 to 1.5
- restretch: float32 [2, 1024], replicated, may hold values from 0.5 to 1.5
- redisplace: float32 [2, 1024], replicated, may hold values from -1.5 to 1.5
Outputs:
- hidden_out: float32 [16384, 1024], P(('row', 'col'))
- hidden_grad: float32 [16384, 1024], P(('row', 'col'))
- project_grad: float32 [2, 1024, 3072], P(None, 'row', 'col')
- offsets_grad: float32 [2, 2048], P(None, 'col')
- combiner_grad: float32 [2, 1024, 1024], P(None, 'col', 'row')
- recenter_grad: float32 [2, 1024], replicated
- stretch_grad: float32 [2, 1024], replicated
- displace_grad: float32 [2, 1024], replicated
- expand_grad: float32 [2, 1024, 4096], P(None, 'row', 'col')
- uplift_grad: float32 [2, 4096], P(None, 'col')
- shrink_grad: float32 [2, 4096, 1024], P(None, 'col', 'row')
- lowering_grad: float32 [2, 1024], replicated
- restretch_grad: float32 [2, 1024], replicated
- redisplace_grad: float32 [2, 1024], replicated
Inputs may be any that keep to these rules, and one draw needn't show every extreme that they name: `slot_of`: slot j holds tokens j * 1024 to (j + 1) * 1024 - 1 and lies on row index j // 4; every slot holds exactly one sequence. `seq_lengths`: a sequence's live tokens stand at the start of its slot; the lengths sum to 10240.
All inputs are finite; a program needn't handle non-finite values.
Results may differ from a plain program's by a relative error of at most 0.03.
Values may be sent and summed in bfloat16 or wider, within the bound.
No kernel may reach another device: no remote copies, remote signals or barrier semaphores. Data moves between devices by JAX's collectives and lax.ppermute only.
A program may use at most 256 MiB of HBM per device.

v0:
```python
import math

import jax
import jax.numpy as jnp
from jax import lax
from jax.sharding import PartitionSpec as P

HEADS = 16
HEAD_DIM = 64
LAYERS = 2


EPSILON = 1e-12
NEGATIVE = -1e30
SQRT_HALF = 0.7071067811865476
ROOT_TWO_PI_INV = 0.3989422804014327


def features(value):
    return lax.all_gather(value, "col", axis=0, tiled=True)


def grad_features(value):
    return lax.all_gather(value, "col", axis=0, tiled=True)


def rows_of(weight):
    return lax.all_gather(weight, "row", axis=0, tiled=True)


def cols_of(weight):
    return lax.all_gather(weight, "row", axis=1, tiled=True)


def inputs_again(value):
    return lax.all_gather(value, "col", axis=0, tiled=True)


def rows_again(weight):
    return lax.all_gather(weight, "row", axis=0, tiled=True)


def cols_again(weight):
    return lax.all_gather(weight, "row", axis=1, tiled=True)


def settle(partial_value):
    return lax.psum_scatter(
        partial_value.astype(jnp.bfloat16), "col", scatter_dimension=0, tiled=True
    ).astype(jnp.float32)


def weight_grad(left, right):
    return lax.psum_scatter(
        lax.dot_general(
            left, right, (((0,), (0,)), ((), ())), preferred_element_type=jnp.float32
        ).astype(jnp.bfloat16),
        "row",
        scatter_dimension=0,
        tiled=True,
    ).astype(jnp.float32)


def contract_last(left, right):
    return lax.dot_general(
        left, right, (((1,), (1,)), ((), ())), preferred_element_type=jnp.float32
    )


def gelu_exact(value):
    return 0.5 * value * (1.0 + lax.erf(value * SQRT_HALF))


def gelu_slope(value):
    return (
        0.5 * (1.0 + lax.erf(value * SQRT_HALF))
        + value * jnp.exp(-0.5 * value * value) * ROOT_TWO_PI_INV
    )


def norm_forward(summed, gain, shift):
    center = jnp.mean(summed, axis=1, keepdims=True)
    offset = summed - center
    spread = jnp.mean(offset * offset, axis=1, keepdims=True)
    inverse = lax.rsqrt(spread + EPSILON)
    normal = offset * inverse
    return (normal * gain + shift, normal, inverse)


def norm_backward(upstream, normal, inverse, gain):
    scaled = upstream * gain
    first_mean = jnp.mean(scaled, axis=1, keepdims=True)
    second_mean = jnp.mean(scaled * normal, axis=1, keepdims=True)
    return inverse * (scaled - first_mean - normal * second_mean)


def attend_forward(queries, keys, values, lengths, factor):
    slot_rows, heads_here, head_size = (queries.shape[1], queries.shape[2], queries.shape[3])
    block_rows = min(512, slot_rows)
    block_count = slot_rows // block_rows

    def one_slot(pieces):
        slot_queries, slot_keys, slot_values, length = pieces
        usable = jnp.arange(slot_rows, dtype=jnp.int32) < length

        def one_block(block_queries):
            scores = (
                jnp.einsum(
                    "qhe,khe->hqk", block_queries, slot_keys, preferred_element_type=jnp.float32
                )
                * factor
            )
            scores = jnp.where(usable[None, None, :], scores, NEGATIVE)
            highest = jnp.max(scores, axis=2, keepdims=True)
            raised = jnp.exp(scores - highest)
            denominator = jnp.sum(raised, axis=2, keepdims=True)
            weights_low = (raised / denominator).astype(jnp.bfloat16)
            context = jnp.einsum(
                "hqk,khe->qhe", weights_low, slot_values, preferred_element_type=jnp.float32
            )
            return (context, highest[:, :, 0] + jnp.log(denominator[:, :, 0]))

        context, logsum = lax.map(
            one_block, slot_queries.reshape(block_count, block_rows, heads_here, head_size)
        )
        return (context.reshape(slot_rows, heads_here, head_size), logsum)

    return lax.map(one_slot, (queries, keys, values, lengths))


def attend_backward(queries, keys, values, lengths, logsum, grad_context, factor):
    slot_rows, heads_here, head_size = (queries.shape[1], queries.shape[2], queries.shape[3])
    block_rows = min(512, slot_rows)
    block_count = slot_rows // block_rows
    blocked = (block_count, block_rows, heads_here, head_size)

    def one_slot(pieces):
        slot_queries, slot_keys, slot_values, length, slot_logsum, slot_grad = pieces
        usable = jnp.arange(slot_rows, dtype=jnp.int32) < length

        def one_block(carry, parts):
            key_grad, value_grad = carry
            block_queries, block_logsum, block_grad = parts
            scores = (
                jnp.einsum(
                    "qhe,khe->hqk", block_queries, slot_keys, preferred_element_type=jnp.float32
                )
                * factor
            )
            probs = jnp.where(
                usable[None, None, :], jnp.exp(scores - block_logsum[:, :, None]), 0.0
            )
            probs_low = probs.astype(jnp.bfloat16)
            grad_probs = jnp.einsum(
                "qhe,khe->hqk", block_grad, slot_values, preferred_element_type=jnp.float32
            )
            weighted = jnp.sum(probs * grad_probs, axis=2, keepdims=True)
            grad_scores = (probs * (grad_probs - weighted)).astype(jnp.bfloat16)
            query_grad = (
                jnp.einsum(
                    "hqk,khe->qhe", grad_scores, slot_keys, preferred_element_type=jnp.float32
                )
                * factor
            )
            key_grad = (
                key_grad
                + jnp.einsum(
                    "hqk,qhe->khe", grad_scores, block_queries, preferred_element_type=jnp.float32
                )
                * factor
            )
            value_grad = value_grad + jnp.einsum(
                "hqk,qhe->khe", probs_low, block_grad, preferred_element_type=jnp.float32
            )
            return ((key_grad, value_grad), query_grad)

        start_grad = jnp.zeros((slot_rows, heads_here, head_size), jnp.float32)
        (key_grad, value_grad), query_grad = lax.scan(
            one_block,
            (start_grad, start_grad),
            (slot_queries.reshape(blocked), slot_logsum, slot_grad.reshape(blocked)),
        )
        return (query_grad.reshape(slot_rows, heads_here, head_size), key_grad, value_grad)

    return lax.map(one_slot, (queries, keys, values, lengths, logsum, grad_context))


def shards(
    hidden_in,
    cotangent,
    seq_lengths,
    slot_of,
    project,
    offsets,
    combiner,
    recenter,
    stretch,
    displace,
    expand,
    uplift,
    shrink,
    lowering,
    restretch,
    redisplace,
):
    slots_here = seq_lengths.shape[0] // lax.axis_size("row")
    group_rows = hidden_in.shape[0] * lax.axis_size("col")
    slot_rows = group_rows // slots_here
    heads_here = HEADS // lax.axis_size("col")
    factor = 1.0 / math.sqrt(HEAD_DIM)
    slot_ids = lax.axis_index("row") * slots_here + jnp.arange(slots_here, dtype=jnp.int32)
    owners = (slot_of[None, :] == slot_ids[:, None]).astype(jnp.int32)
    lengths_here = jnp.sum(owners * seq_lengths[None, :], axis=1)
    shaped = (slots_here, slot_rows, heads_here, HEAD_DIM)
    current = hidden_in.astype(jnp.float32)
    saved = []
    for layer_index in range(LAYERS):
        layer_input = current
        input_full = features(current.astype(jnp.bfloat16))
        project_full = rows_of(project[layer_index])
        mixed = jnp.dot(input_full, project_full, preferred_element_type=jnp.float32).reshape(
            group_rows, heads_here, 3, HEAD_DIM
        )
        paired = offsets[layer_index].reshape(heads_here, 2, HEAD_DIM)
        queries = (mixed[:, :, 0] + paired[:, 0]).astype(jnp.bfloat16).reshape(shaped)
        keys = mixed[:, :, 1].astype(jnp.bfloat16).reshape(shaped)
        values = (mixed[:, :, 2] + paired[:, 1]).astype(jnp.bfloat16).reshape(shaped)
        context, logsum = attend_forward(queries, keys, values, lengths_here, factor)
        context_low = context.reshape(group_rows, heads_here * HEAD_DIM).astype(jnp.bfloat16)
        combiner_full = cols_of(combiner[layer_index])
        branch = (
            settle(jnp.dot(context_low, combiner_full, preferred_element_type=jnp.float32))
            + recenter[layer_index]
        )
        normed, normal_one, inverse_one = norm_forward(
            layer_input + branch, stretch[layer_index], displace[layer_index]
        )
        normed_full = features(normed.astype(jnp.bfloat16))
        expand_full = rows_of(expand[layer_index])
        inner = (
            jnp.dot(normed_full, expand_full, preferred_element_type=jnp.float32)
            + uplift[layer_index]
        )
        active = gelu_exact(inner).astype(jnp.bfloat16)
        shrink_full = cols_of(shrink[layer_index])
        branch_two = (
            settle(jnp.dot(active, shrink_full, preferred_element_type=jnp.float32))
            + lowering[layer_index]
        )
        current, normal_two, inverse_two = norm_forward(
            normed + branch_two, restretch[layer_index], redisplace[layer_index]
        )
        saved.append(
            (
                layer_input,
                input_full,
                project_full,
                queries,
                keys,
                values,
                logsum,
                context_low,
                combiner_full,
                normal_one,
                inverse_one,
                normed,
                normed_full,
                expand_full,
                inner,
                active,
                shrink_full,
                normal_two,
                inverse_two,
            )
        )
    upstream = cotangent
    grads_project, grads_offsets, grads_combiner, grads_recenter = ([], [], [], [])
    grads_stretch, grads_displace, grads_expand, grads_uplift = ([], [], [], [])
    grads_shrink, grads_lowering, grads_restretch, grads_redisplace = ([], [], [], [])
    for layer_index in reversed(range(LAYERS)):
        (
            layer_input,
            input_full,
            project_full,
            queries,
            keys,
            values,
            logsum,
            context_low,
            combiner_full,
            normal_one,
            inverse_one,
            normed,
            normed_full,
            expand_full,
            inner,
            active,
            shrink_full,
            normal_two,
            inverse_two,
        ) = saved[layer_index]
        input_use = inputs_again(layer_input.astype(jnp.bfloat16))
        normed_use = inputs_again(normed.astype(jnp.bfloat16))
        project_use = rows_again(project[layer_index])
        expand_use = rows_again(expand[layer_index])
        combiner_use = cols_again(combiner[layer_index])
        shrink_use = cols_again(shrink[layer_index])
        grads_redisplace.append(jnp.sum(upstream, axis=0))
        grads_restretch.append(jnp.sum(upstream * normal_two, axis=0))
        grad_sum_two = norm_backward(upstream, normal_two, inverse_two, restretch[layer_index])
        grad_branch_two = grad_sum_two.astype(jnp.bfloat16)
        grads_lowering.append(jnp.sum(grad_branch_two.astype(jnp.float32), axis=0))
        branch_two_full = grad_features(grad_branch_two)
        grads_shrink.append(weight_grad(branch_two_full, active).T)
        grad_inner = (contract_last(branch_two_full, shrink_use) * gelu_slope(inner)).astype(
            jnp.bfloat16
        )
        grads_uplift.append(jnp.sum(grad_inner.astype(jnp.float32), axis=0))
        grads_expand.append(weight_grad(normed_use, grad_inner))
        grad_normed = grad_sum_two + settle(contract_last(grad_inner, expand_use))
        grads_displace.append(jnp.sum(grad_normed, axis=0))
        grads_stretch.append(jnp.sum(grad_normed * normal_one, axis=0))
        grad_sum_one = norm_backward(grad_normed, normal_one, inverse_one, stretch[layer_index])
        grad_branch = grad_sum_one.astype(jnp.bfloat16)
        grads_recenter.append(jnp.sum(grad_branch.astype(jnp.float32), axis=0))
        branch_full = grad_features(grad_branch)
        grads_combiner.append(weight_grad(branch_full, context_low).T)
        grad_context = contract_last(branch_full, combiner_use).astype(jnp.bfloat16).reshape(shaped)
        query_grad, key_grad, value_grad = attend_backward(
            queries, keys, values, lengths_here, logsum, grad_context, factor
        )
        query_low = query_grad.reshape(group_rows, heads_here, HEAD_DIM).astype(jnp.bfloat16)
        key_low = key_grad.reshape(group_rows, heads_here, HEAD_DIM).astype(jnp.bfloat16)
        value_low = value_grad.reshape(group_rows, heads_here, HEAD_DIM).astype(jnp.bfloat16)
        grad_triple = jnp.stack([query_low, key_low, value_low], axis=2).reshape(
            group_rows, heads_here * 3 * HEAD_DIM
        )
        bias_pair = jnp.stack(
            [
                jnp.sum(query_low.astype(jnp.float32), axis=0),
                jnp.sum(value_low.astype(jnp.float32), axis=0),
            ],
            axis=1,
        )
        grads_offsets.append(bias_pair.reshape(heads_here * 2 * HEAD_DIM))
        grads_project.append(weight_grad(input_use, grad_triple))
        upstream = grad_sum_one + settle(contract_last(grad_triple, project_use))

    def ordered(items):
        return jnp.stack(items[::-1], axis=0)

    small = lax.psum((ordered(grads_offsets), ordered(grads_uplift)), "row")
    norms = lax.psum(
        (
            ordered(grads_recenter),
            ordered(grads_stretch),
            ordered(grads_displace),
            ordered(grads_lowering),
            ordered(grads_restretch),
            ordered(grads_redisplace),
        ),
        ("row", "col"),
    )
    return (
        current,
        upstream,
        ordered(grads_project),
        small[0],
        ordered(grads_combiner),
        norms[0],
        norms[1],
        norms[2],
        ordered(grads_expand),
        small[1],
        ordered(grads_shrink),
        norms[3],
        norms[4],
        norms[5],
    )


def solution(mesh):
    in_specs = (
        P(("row", "col"), None),
        P(("row", "col"), None),
        P(),
        P(),
        P(None, "row", "col"),
        P(None, "col"),
        P(None, "col", "row"),
        P(),
        P(),
        P(),
        P(None, "row", "col"),
        P(None, "col"),
        P(None, "col", "row"),
        P(),
        P(),
        P(),
    )
    out_specs = (
        P(("row", "col"), None),
        P(("row", "col"), None),
        P(None, "row", "col"),
        P(None, "col"),
        P(None, "col", "row"),
        P(),
        P(),
        P(),
        P(None, "row", "col"),
        P(None, "col"),
        P(None, "col", "row"),
        P(),
        P(),
        P(),
    )
    return jax.shard_map(shards, mesh=mesh, in_specs=in_specs, out_specs=out_specs, check_vma=False)
```

profile of v0, /device:TPU:0, one launch (start us, length us, event | category | flops | bytes accessed | tf_op | source)
XLA Modules:
  0.0 2856.8 jit_solution(16989118500840584813)
XLA Ops:
  11.7 7.7 all-gather.1
  22.0 8.7 all-gather
  30.7 107.9 %all-gather.21.cloned.1.call-done = bf16[4096,1024]{1,0:T(8,128)(2,1)} async-done(((bf16[512,1024]{1,0:T(8,128)(2,1)}), bf16[4096,1024]{1,0:T(8,128)(2,1)}) %all-gather.21.cloned.1.call-update) | async-done | bytes 8388624 | tf_op jit(solution)/shard_map/all_gather | solution.py:20
  162.5 45.8 %while.109 = (s32[]{:T(128)}, bf16[4,1024,2,64]{3,2,1,0:T(2,128)(2,1)}, f32[4,2,2,512]{3,2,1,0:T(2,128)S(1)}, bf16[4,1024,2,64]{1,3,2,0:T(8,128)(2,1)}, bf16[4,1...) while((s32[]{:T(128)}, ...), condition=%wide.region_6.7_spmd, body=%wide.region_1.6_spmd.sunk | while | flops 281018368 | bytes 17486632 | solution.py:128
  164.4 8.0 while.116
  175.8 8.0 while.116
  187.3 8.0 while.116
  198.7 8.0 while.116
  213.9 6.8 convolution_convert_fusion.7
  224.5 143.7 %reduce-scatter.17.cloned.1.call-done = bf16[512,1024]{1,0:T(8,128)(2,1)} async-done(((bf16[4096,1024]{1,0:T(8,128)(2,1)}), bf16[512,1024]{1,0:T(8,128)(2,1)}) %reduce-scatter.17.cloned.1.call-update) | async-done | bytes 1048592 | tf_op jit(solution)/shard_map/reduce_scatter | solution.py:48
  375.0 122.0 %all-gather.23.cloned.1.call-done = bf16[4096,1024]{1,0:T(8,128)(2,1)} async-done(((bf16[512,1024]{1,0:T(8,128)(2,1)}), bf16[4096,1024]{1,0:T(8,128)(2,1)}) %all-gather.23.cloned.1.call-update) | async-done | bytes 8388624 | tf_op jit(solution)/shard_map/all_gather | solution.py:20
  497.0 11.0 multiply_convert_fusion.3
  514.0 10.3 convolution_convert_fusion.5
  526.8 144.6 %reduce-scatter.19.cloned.1.call-done = bf16[512,1024]{1,0:T(8,128)(2,1)} async-done(((bf16[4096,1024]{1,0:T(8,128)(2,1)}), bf16[512,1024]{1,0:T(8,128)(2,1)}) %reduce-scatter.19.cloned.1.call-update) | async-done | bytes 1048592 | tf_op jit(solution)/shard_map/reduce_scatter | solution.py:48
  676.5 6.2 all-gather.5
  682.8 8.7 all-gather.4
  691.5 109.0 %all-gather.25.cloned.1.call-done = bf16[4096,1024]{1,0:T(8,128)(2,1)} async-done(((bf16[512,1024]{1,0:T(8,128)(2,1)}), bf16[4096,1024]{1,0:T(8,128)(2,1)}) %all-gather.25.cloned.1.call-update) | async-done | bytes 8388624 | tf_op jit(solution)/shard_map/all_gather | solution.py:20
  828.3 45.7 %while.111 = (s32[]{:T(128)}, bf16[4,1024,2,64]{3,2,1,0:T(2,128)(2,1)}, f32[4,2,2,512]{3,2,1,0:T(2,128)S(1)}, bf16[4,1024,2,64]{1,3,2,0:T(8,128)(2,1)S(1)}, bf16...) while((s32[]{:T(128)}, ...), condition=%wide.region_18.19_spmd, body=%wide.region_13.18_spmd.sunk | while | flops 281018368 | bytes 17486632 | solution.py:128
  830.1 8.0 while.117
  841.5 8.0 while.117
  853.0 8.0 while.117
  864.4 8.0 while.117
  879.2 6.8 convolution_convert_fusion.6
  886.9 144.5 %reduce-scatter.21.cloned.1.call-done = bf16[512,1024]{1,0:T(8,128)(2,1)} async-done(((bf16[4096,1024]{1,0:T(8,128)(2,1)}), bf16[512,1024]{1,0:T(8,128)(2,1)}) %reduce-scatter.21.cloned.1.call-update) | async-done | bytes 1048592 | tf_op jit(solution)/shard_map/reduce_scatter | solution.py:48
  1036.8 12.5 all-gather.41.cloned.1.call-done
  1049.3 127.3 %all-gather.27.cloned.1.call-done = bf16[4096,1024]{1,0:T(8,128)(2,1)} async-done(((bf16[512,1024]{1,0:T(8,128)(2,1)}), bf16[4096,1024]{1,0:T(8,128)(2,1)}) %all-gather.27.cloned.1.call-update) | async-done | bytes 8388624 | tf_op jit(solution)/shard_map/all_gather | solution.py:20
  1176.6 11.3 multiply_convert_fusion.2
  1193.0 10.3 convolution_convert_fusion.4
  1203.4 149.1 %reduce-scatter.23.cloned.1.call-done = bf16[512,1024]{1,0:T(8,128)(2,1)} async-done(((bf16[4096,1024]{1,0:T(8,128)(2,1)}), bf16[512,1024]{1,0:T(8,128)(2,1)}) %reduce-scatter.23.cloned.1.call-update) | async-done | bytes 1048592 | tf_op jit(solution)/shard_map/reduce_scatter | solution.py:48
  1360.5 124.0 %all-gather.29.cloned.1.call-done = bf16[4096,1024]{1,0:T(8,128)(2,1)} async-done(((bf16[512,1024]{1,0:T(8,128)(2,1)}), bf16[4096,1024]{1,0:T(8,128)(2,1)}) %all-gather.29.cloned.1.call-update) | async-done | bytes 8388624 | tf_op jit(solution)/shard_map/all_gather | solution.py:24
  1484.5 12.5 convert_reduce_fusion
  1499.1 7.2 convolution_convert_fusion.3
  1506.4 145.2 %reduce-scatter.25.cloned.1.call-done = bf16[512,1024]{1,0:T(8,128)(2,1)} async-done(((bf16[4096,1024]{1,0:T(8,128)(2,1)}), bf16[512,1024]{1,0:T(8,128)(2,1)}) %reduce-scatter.25.cloned.1.call-update) | async-done | bytes 1048592 | tf_op jit(solution)/shard_map/reduce_scatter | solution.py:48
  1658.4 124.2 %all-gather.31.cloned.1.call-done = bf16[4096,1024]{1,0:T(8,128)(2,1)} async-done(((bf16[512,1024]{1,0:T(8,128)(2,1)}), bf16[4096,1024]{1,0:T(8,128)(2,1)}) %all-gather.31.cloned.1.call-update) | async-done | bytes 8388624 | tf_op jit(solution)/shard_map/all_gather | solution.py:24
  1782.5 6.7 convolution_convert_fusion.9
  1801.6 107.8 %while.113 = (s32[]{:T(128)}, bf16[4,1024,2,64]{3,2,1,0:T(2,128)(2,1)}, bf16[4,1024,2,64]{1,3,2,0:T(8,128)(2,1)}, bf16[4,1024,2,64]{1,3,2,0:T(8,128)(2,1)}, bf16...) while((s32[]{:T(128)}, ...), condition=%wide.region_34.35_spmd, body=%wide.region_30.34_spmd.sunk | while | flops 687538176 | bytes 86821440 | solution.py:185
  1805.7 18.3 while.118
  1832.7 18.3 while.118
  1859.6 18.3 while.118
  1886.5 18.3 while.118
  1925.9 7.2 convolution_convert_fusion.2
  1933.2 145.3 %reduce-scatter.27.cloned.1.call-done = bf16[512,1024]{1,0:T(8,128)(2,1)} async-done(((bf16[4096,1024]{1,0:T(8,128)(2,1)}), bf16[512,1024]{1,0:T(8,128)(2,1)}) %reduce-scatter.27.cloned.1.call-update) | async-done | bytes 1048592 | tf_op jit(solution)/shard_map/reduce_scatter | solution.py:48
  2085.2 124.1 %all-gather.33.cloned.1.call-done = bf16[4096,1024]{1,0:T(8,128)(2,1)} async-done(((bf16[512,1024]{1,0:T(8,128)(2,1)}), bf16[4096,1024]{1,0:T(8,128)(2,1)}) %all-gather.33.cloned.1.call-update) | async-done | bytes 8388624 | tf_op jit(solution)/shard_map/all_gather | solution.py:24
  2209.4 12.3 convert_reduce_fusion.1
  2223.7 7.3 convolution_convert_fusion.1
  2231.2 145.1 %reduce-scatter.29.cloned.1.call-done = bf16[512,1024]{1,0:T(8,128)(2,1)} async-done(((bf16[4096,1024]{1,0:T(8,128)(2,1)}), bf16[512,1024]{1,0:T(8,128)(2,1)}) %reduce-scatter.29.cloned.1.call-update) | async-done | bytes 1048592 | tf_op jit(solution)/shard_map/reduce_scatter | solution.py:48
  2383.5 10.2 convolution_convert_fusion.10
  2393.8 10.1 convolution_convert_fusion.11
  2404.3 10.1 convolution_convert_fusion.12
  2414.6 10.3 convolution_convert_fusion.13
  2425.0 6.9 convolution_convert_fusion.16
  2431.9 75.8 %all-gather.35.cloned.1.call-done = bf16[4096,1024]{1,0:T(8,128)(2,1)} async-done(((bf16[512,1024]{1,0:T(8,128)(2,1)}), bf16[4096,1024]{1,0:T(8,128)(2,1)}) %all-gather.35.cloned.1.call-update) | async-done | bytes 8388624 | tf_op jit(solution)/shard_map/all_gather | solution.py:24
  2507.7 6.6 convolution_convert_fusion.17
  2514.6 8.6 convolution_convert_fusion.14
  2535.9 111.4 %while.115 = (s32[]{:T(128)}, bf16[4,1024,2,64]{3,2,1,0:T(2,128)(2,1)}, bf16[4,1024,2,64]{1,3,2,0:T(8,128)(2,1)}, bf16[4,1024,2,64]{1,3,2,0:T(8,128)(2,1)}, bf16...) while((s32[]{:T(128)}, ...), condition=%wide.region_45.46_spmd, body=%wide.region_41.45_spmd.sunk | while | flops 687538176 | bytes 86821440 | solution.py:185
  2540.8 18.6 while.119
  2568.8 18.4 while.119
  2596.6 18.4 while.119
  2624.5 18.5 while.119
  2665.6 6.8 fusion.106
  2672.6 10.0 convolution_convert_fusion
  2697.2 43.6 %all-reduce = (f32[2,1024]{1,0:T(2,128)}, f32[2,1024]{1,0:T(2,128)}, f32[2,1024]{1,0:T(2,128)}, f32[2,1024]{1,0:T(2,128)}, f32[2,1024]{1,0:T(2,128)}, /*index=5*/f32[2,1024]{1,0:T(2,128)}) all-reduce(f32[2,1024]{1,0:T(2,128)S(1)} %pad_maximum_fusion.2, ...), channel_id=1, replica_groups=mesh['row'=4,'col'=8] {'row','col'}, use_global_device_ids=true, to_apply=%region_58.59 | all-reduce | flops 12288 | bytes 98304 | tf_op jit(solution)/shard_map/psum | solution.py:353
  2745.6 7.0 all-reduce.1
  2756.5 89.5 %reduce-scatter.31.cloned.1.call-done = bf16[512,1024]{1,0:T(8,128)(2,1)} async-done(((bf16[4096,1024]{1,0:T(8,128)(2,1)}), bf16[512,1024]{1,0:T(8,128)(2,1)}) %reduce-scatter.31.cloned.1.call-update) | async-done | bytes 1048592 | tf_op jit(solution)/shard_map/reduce_scatter | solution.py:48
  (964 shorter events, 531.7 us)
Async XLA Ops:
  8.0 130.6 %all-gather.21.cloned.1.call-start = ((), (), s32[]{:S(2)}) async-start(), calls=%async_computation.16 | async-start | bytes 9437184 | tf_op jit(solution)/shard_map/all_gather | solution.py:20
  8.7 359.4 %reduce-scatter.17.cloned.1.call-start = ((), (), s32[]{:S(2)}) async-start(), calls=%async_computation.17 | async-start | bytes 9437184 | tf_op jit(solution)/shard_map/reduce_scatter | solution.py:48
  30.7 113.9 %copy-start.44 = (bf16[1,1024,384]{2,1,0:T(8,128)(2,1)}, bf16[1,1024,384]{2,1,0:T(8,128)(2,1)S(1)}, u32[]{:S(2)}) copy-start(bf16[1,1024,384]{2,1,0:T(8,128)(2,1)S(1)} %all-gather) | copy-start | bytes 2359300
  208.3 12.4 copy-start.25
  208.3 12.4 copy-start.53
  220.8 147.4 %copy-start.13 = (bf16[512,1024]{1,0:T(8,128)(2,1)S(1)}, bf16[512,1024]{1,0:T(8,128)(2,1)}, u32[]{:S(2)}) copy-start(bf16[512,1024]{1,0:T(8,128)(2,1)} %param.32) | copy-start | bytes 3145732
  220.9 154.1 %all-gather.37.cloned.1.call-start = ((), (), s32[]{:S(2)}) async-start(), calls=%async_computation.40 | async-start | bytes 1310720 | tf_op jit(solution)/shard_map/all_gather | solution.py:28
  222.7 274.4 %all-gather.23.cloned.1.call-start = ((), (), s32[]{:S(2)}) async-start(), calls=%async_computation.18 | async-start | bytes 9437184 | tf_op jit(solution)/shard_map/all_gather | solution.py:20
  223.3 448.1 %copy-start.51 = (f32[1,1024]{1,0:T(1,128)}, f32[1,1024]{1,0:T(1,128)S(1)}, u32[]{:S(2)}) copy-start(f32[1,1024]{1,0:T(1,128)S(1)} %get-tuple-element.995) | copy-start | bytes 12292
  223.9 447.5 %copy-start.54 = (f32[1,1024]{1,0:T(1,128)}, f32[1,1024]{1,0:T(1,128)S(1)}, u32[]{:S(2)}) copy-start(f32[1,1024]{1,0:T(1,128)S(1)} %get-tuple-element.992) | copy-start | bytes 12292
  369.9 301.5 %copy-start.60 = (f32[512]{0:T(512)}, f32[512]{0:T(512)S(1)}, u32[]{:S(2)}) copy-start(f32[512]{0:T(512)S(1)} %broadcast_multiply_fusion.11) | copy-start | bytes 6148
  371.8 299.6 %copy-start.65 = (f32[512]{0:T(512)}, f32[512]{0:T(512)S(1)}, u32[]{:S(2)}) copy-start(f32[512]{0:T(512)S(1)} %add_rsqrt_fusion.3) | copy-start | bytes 6148
  373.4 140.6 %all-gather.39.cloned.1.call-start = ((), (), s32[]{:S(2)}) async-start(), calls=%async_computation.41 | async-start | bytes 1310720 | tf_op jit(solution)/shard_map/all_gather | solution.py:32
  374.3 297.1 %reduce-scatter.19.cloned.1.call-start = ((), (), s32[]{:S(2)}) async-start(), calls=%async_computation.19 | async-start | bytes 9437184 | tf_op jit(solution)/shard_map/reduce_scatter | solution.py:48
  375.0 133.0 %copy-start.98 = (f32[1,512]{1,0:T(1,128)}, f32[1,512]{1,0:T(1,128)S(1)}, u32[]{:S(2)}) copy-start(f32[1,512]{1,0:T(1,128)S(1)} %get-tuple-element.1000) | copy-start | bytes 6148
  524.3 276.2 %all-gather.25.cloned.1.call-start = ((), (), s32[]{:S(2)}) async-start(), calls=%async_computation.20 | async-start | bytes 9437184 | tf_op jit(solution)/shard_map/all_gather | solution.py:20
  526.2 147.9 %copy-start.56 = (f32[1,1024]{1,0:T(1,128)}, f32[1,1024]{1,0:T(1,128)S(1)}, u32[]{:S(2)}) copy-start(f32[1,1024]{1,0:T(1,128)S(1)} %get-tuple-element.988) | copy-start | bytes 12292
  526.8 147.3 %copy-start.72 = (f32[1,1024]{1,0:T(1,128)}, f32[1,1024]{1,0:T(1,128)S(1)}, u32[]{:S(2)}) copy-start(f32[1,1024]{1,0:T(1,128)S(1)} %get-tuple-element.990) | copy-start | bytes 12292
  676.4 355.0 %reduce-scatter.21.cloned.1.call-start = ((), (), s32[]{:S(2)}) async-start(), calls=%async_computation.21 | async-start | bytes 9437184 | tf_op jit(solution)/shard_map/reduce_scatter | solution.py:48
  691.5 115.2 %copy-start.45 = (bf16[1,1024,384]{2,1,0:T(8,128)(2,1)}, bf16[1,1024,384]{2,1,0:T(8,128)(2,1)S(1)}, u32[]{:S(2)}) copy-start(bf16[1,1024,384]{2,1,0:T(8,128)(2,1)S(1)} %all-gather.4) | copy-start | bytes 2359300
  886.0 145.3 %copy-start.9 = (f32[512,1024]{1,0:T(8,128)S(1)}, f32[512,1024]{1,0:T(8,128)}, u32[]{:S(2)}) copy-start(f32[512,1024]{1,0:T(8,128)} %copy-done.8) | copy-start | bytes 6291460
  886.0 145.4 %copy-start.57 = (f32[1,1024]{1,0:T(1,128)S(1)}, f32[1,1024]{1,0:T(1,128)}, u32[]{:S(2)}) copy-start(f32[1,1024]{1,0:T(1,128)} %copy-done.56) | copy-start | bytes 12292
  886.0 145.4 %copy-start.63 = (f32[512]{0:T(512)S(1)}, f32[512]{0:T(512)}, u32[]{:S(2)}) copy-start(f32[512]{0:T(512)} %copy-done.62) | copy-start | bytes 6148
  886.0 145.3 %copy-start.68 = (f32[512]{0:T(512)S(1)}, f32[512]{0:T(512)}, u32[]{:S(2)}) copy-start(f32[512]{0:T(512)} %copy-done.67) | copy-start | bytes 6148
  886.0 145.3 %copy-start.73 = (f32[1,1024]{1,0:T(1,128)S(1)}, f32[1,1024]{1,0:T(1,128)}, u32[]{:S(2)}) copy-start(f32[1,1024]{1,0:T(1,128)} %copy-done.72) | copy-start | bytes 12292
  886.0 145.3 %copy-start.83 = (f32[1,1024]{1,0:T(1,128)S(1)}, f32[1,1024]{1,0:T(1,128)}, u32[]{:S(2)}) copy-start(f32[1,1024]{1,0:T(1,128)} %get-tuple-element.996) | copy-start | bytes 12292
  886.1 163.2 %all-gather.41.cloned.1.call-start = ((), (), s32[]{:S(2)}) async-start(), calls=%async_computation.42 | async-start | bytes 1310720 | tf_op jit(solution)/shard_map/all_gather | solution.py:28
  886.8 289.8 %all-gather.27.cloned.1.call-start = ((), (), s32[]{:S(2)}) async-start(), calls=%async_computation.22 | async-start | bytes 9437184 | tf_op jit(solution)/shard_map/all_gather | solution.py:20
  1033.4 143.2 %copy-start.101 = (f32[1,512]{1,0:T(1,128)S(1)}, f32[1,512]{1,0:T(1,128)}, u32[]{:S(2)}) copy-start(f32[1,512]{1,0:T(1,128)} %get-tuple-element.999) | copy-start | bytes 6148
  1036.1 156.9 %all-gather.43.cloned.1.call-start = ((), (), s32[]{:S(2)}) async-start(), calls=%async_computation.43 | async-start | bytes 1310720 | tf_op jit(solution)/shard_map/all_gather | solution.py:32
  1036.7 315.8 %reduce-scatter.23.cloned.1.call-start = ((), (), s32[]{:S(2)}) async-start(), calls=%async_computation.23 | async-start | bytes 9437184 | tf_op jit(solution)/shard_map/reduce_scatter | solution.py:48
  1203.3 149.2 %copy-start.12 = (f32[512,1024]{1,0:T(8,128)S(1)}, f32[512,1024]{1,0:T(8,128)}, u32[]{:S(2)}) copy-start(f32[512,1024]{1,0:T(8,128)} %copy-done.11) | copy-start | bytes 6291460
  1203.3 149.2 %copy-start.84 = (f32[1,1024]{1,0:T(1,128)S(1)}, f32[1,1024]{1,0:T(1,128)}, u32[]{:S(2)}) copy-start(f32[1,1024]{1,0:T(1,128)} %get-tuple-element.998) | copy-start | bytes 12292
  1203.3 281.2 %all-gather.29.cloned.1.call-start = ((), (), s32[]{:S(2)}) async-start(), calls=%async_computation.24 | async-start | bytes 9437184 | tf_op jit(solution)/shard_map/all_gather | solution.py:24
  1360.4 291.2 %reduce-scatter.25.cloned.1.call-start = ((), (), s32[]{:S(2)}) async-start(), calls=%async_computation.25 | async-start | bytes 9437184 | tf_op jit(solution)/shard_map/reduce_scatter | solution.py:48
  1484.5 14.6 copy-start.103
  1506.3 276.2 %all-gather.31.cloned.1.call-start = ((), (), s32[]{:S(2)}) async-start(), calls=%async_computation.26 | async-start | bytes 9437184 | tf_op jit(solution)/shard_map/all_gather | solution.py:24
  1658.3 420.2 %reduce-scatter.27.cloned.1.call-start = ((), (), s32[]{:S(2)}) async-start(), calls=%async_computation.27 | async-start | bytes 9437184 | tf_op jit(solution)/shard_map/reduce_scatter | solution.py:48
  1933.1 145.4 %copy-start.10 = (f32[512,1024]{1,0:T(8,128)S(1)}, f32[512,1024]{1,0:T(8,128)}, u32[]{:S(2)}) copy-start(f32[512,1024]{1,0:T(8,128)} %copy-done.8) | copy-start | bytes 6291460
  1933.1 145.4 %copy-start.58 = (f32[1,1024]{1,0:T(1,128)S(1)}, f32[1,1024]{1,0:T(1,128)}, u32[]{:S(2)}) copy-start(f32[1,1024]{1,0:T(1,128)} %copy-done.56) | copy-start | bytes 12292
  1933.1 145.4 %copy-start.64 = (f32[512]{0:T(512)S(1)}, f32[512]{0:T(512)}, u32[]{:S(2)}) copy-start(f32[512]{0:T(512)} %copy-done.62) | copy-start | bytes 6148
  1933.1 145.4 %copy-start.69 = (f32[512]{0:T(512)S(1)}, f32[512]{0:T(512)}, u32[]{:S(2)}) copy-start(f32[512]{0:T(512)} %copy-done.67) | copy-start | bytes 6148
  1933.2 276.2 %all-gather.33.cloned.1.call-start = ((), (), s32[]{:S(2)}) async-start(), calls=%async_computation.28 | async-start | bytes 9437184 | tf_op jit(solution)/shard_map/all_gather | solution.py:24
  2082.1 127.2 %copy-start.99 = (f32[1,512]{1,0:T(1,128)S(1)}, f32[1,512]{1,0:T(1,128)}, u32[]{:S(2)}) copy-start(f32[1,512]{1,0:T(1,128)} %copy-done.98) | copy-start | bytes 6148
  2085.2 291.1 %reduce-scatter.29.cloned.1.call-start = ((), (), s32[]{:S(2)}) async-start(), calls=%async_computation.29 | async-start | bytes 9437184 | tf_op jit(solution)/shard_map/reduce_scatter | solution.py:48
  2209.4 14.3 copy-start.102
  2230.9 145.4 %copy-start.14 = (bf16[512,1024]{1,0:T(8,128)(2,1)S(1)}, bf16[512,1024]{1,0:T(8,128)(2,1)}, u32[]{:S(2)}) copy-start(bf16[512,1024]{1,0:T(8,128)(2,1)} %param.32) | copy-start | bytes 3145732
  2230.9 145.4 %copy-start.16 = (bf16[512,1024]{1,0:T(8,128)(2,1)S(1)}, bf16[512,1024]{1,0:T(8,128)(2,1)}, u32[]{:S(2)}) copy-start(bf16[512,1024]{1,0:T(8,128)(2,1)} %reduce-scatter.17.cloned.1.call-done) | copy-start | bytes 3145732
  2230.9 145.4 %copy-start.52 = (f32[1,1024]{1,0:T(1,128)S(1)}, f32[1,1024]{1,0:T(1,128)}, u32[]{:S(2)}) copy-start(f32[1,1024]{1,0:T(1,128)} %copy-done.51) | copy-start | bytes 12292
  2230.9 145.4 %copy-start.55 = (f32[1,1024]{1,0:T(1,128)S(1)}, f32[1,1024]{1,0:T(1,128)}, u32[]{:S(2)}) copy-start(f32[1,1024]{1,0:T(1,128)} %copy-done.54) | copy-start | bytes 12292
  2230.9 145.4 %copy-start.61 = (f32[512]{0:T(512)S(1)}, f32[512]{0:T(512)}, u32[]{:S(2)}) copy-start(f32[512]{0:T(512)} %copy-done.60) | copy-start | bytes 6148
  2230.9 145.4 %copy-start.66 = (f32[512]{0:T(512)S(1)}, f32[512]{0:T(512)}, u32[]{:S(2)}) copy-start(f32[512]{0:T(512)} %copy-done.65) | copy-start | bytes 6148
  2231.0 276.7 %all-gather.35.cloned.1.call-start = ((), (), s32[]{:S(2)}) async-start(), calls=%async_computation.30 | async-start | bytes 9437184 | tf_op jit(solution)/shard_map/all_gather | solution.py:24
  2383.5 306.9 %reduce-scatter.47.cloned.1.call-start = ((), (), s32[]{:S(2)}) async-start(), calls=%async_computation.39 | async-start | bytes 1310720 | tf_op jit(solution)/shard_map/reduce_scatter | solution.py:54
  2393.7 296.7 %reduce-scatter.45.cloned.1.call-start = ((), (), s32[]{:S(2)}) async-start(), calls=%async_computation.38 | async-start | bytes 1310720 | tf_op jit(solution)/shard_map/reduce_scatter | solution.py:54
  2403.9 291.2 %reduce-scatter.43.cloned.1.call-start = ((), (), s32[]{:S(2)}) async-start(), calls=%async_computation.37 | async-start | bytes 1310720 | tf_op jit(solution)/shard_map/reduce_scatter | solution.py:54
  2414.5 280.6 %reduce-scatter.41.cloned.1.call-start = ((), (), s32[]{:S(2)}) async-start(), calls=%async_computation.36 | async-start | bytes 1310720 | tf_op jit(solution)/shard_map/reduce_scatter | solution.py:54
  2424.9 327.7 %reduce-scatter.39.cloned.1.call-start = ((), (), s32[]{:S(2)}) async-start(), calls=%async_computation.35 | async-start | bytes 327680 | tf_op jit(solution)/shard_map/reduce_scatter | solution.py:54
  2424.9 82.8 %copy-start.31 = (bf16[4096,128]{1,0:T(8,128)(2,1)S(1)}, bf16[4096,128]{1,0:T(8,128)(2,1)}, u32[]{:S(2)}) copy-start(bf16[4096,128]{1,0:T(8,128)(2,1)} %reshape.318) | copy-start | bytes 3145732
  2431.8 320.7 %reduce-scatter.37.cloned.1.call-start = ((), (), s32[]{:S(2)}) async-start(), calls=%async_computation.34 | async-start | bytes 327680 | tf_op jit(solution)/shard_map/reduce_scatter | solution.py:54
  2514.3 240.0 %reduce-scatter.35.cloned.1.call-start = ((), (), s32[]{:S(2)}) async-start(), calls=%async_computation.33 | async-start | bytes 983040 | tf_op jit(solution)/shard_map/reduce_scatter | solution.py:54
  2523.2 231.1 %reduce-scatter.33.cloned.1.call-start = ((), (), s32[]{:S(2)}) async-start(), calls=%async_computation.32 | async-start | bytes 983040 | tf_op jit(solution)/shard_map/reduce_scatter | solution.py:54
  2672.4 173.7 %reduce-scatter.31.cloned.1.call-start = ((), (), s32[]{:S(2)}) async-start(), calls=%async_computation.31 | async-start | bytes 9437184 | tf_op jit(solution)/shard_map/reduce_scatter | solution.py:48
  2745.5 100.6 %copy-start.30 = (f32[512,1024]{1,0:T(8,128)S(1)}, f32[512,1024]{1,0:T(8,128)}, u32[]{:S(2)}) copy-start(f32[512,1024]{1,0:T(8,128)} %get-tuple-element.948) | copy-start | bytes 6291460
  (138 other events, 519.8 us)
Sparse Core Ops, SparseCore 0:
  11.0 127.6 all-gather.20
  221.0 147.1 reduce-scatter.16
  676.5 123.9 all-gather.24
  1203.5 149.0 reduce-scatter.22
  1360.5 123.9 all-gather.28
  1658.4 124.0 all-gather.30
  2085.3 124.0 all-gather.32
  2383.6 124.0 all-gather.34
Sparse Core Ops, SparseCore 1:
  223.5 14.8 all-gather.36
  373.5 123.5 all-gather.22
  499.1 14.8 all-gather.38
  524.4 147.0 reduce-scatter.18
  886.2 145.1 reduce-scatter.20
  1033.6 15.7 all-gather.40
  1052.1 124.5 all-gather.26
  1178.1 14.8 all-gather.42
  1506.4 145.1 reduce-scatter.24
  1933.3 145.2 reduce-scatter.26
  2231.1 145.2 reduce-scatter.28
  2393.8 23.9 reduce-scatter.46
  2420.2 24.8 reduce-scatter.44
  2447.8 24.8 reduce-scatter.42
  2475.2 24.8 reduce-scatter.40
  2503.2 19.9 reduce-scatter.38
  2525.7 20.0 reduce-scatter.36
  2549.0 23.2 reduce-scatter.34
  2672.4 21.4 reduce-scatter.32
  2698.0 148.0 reduce-scatter.30
where the time goes:
time: 2870 us; the launch traced here: 2860 us
  waiting for transfers between devices  2050 us (71%)
  matrix products  355 us (12%)
  local copies, waits for them, and re-layouts  222 us (8%)
  other arithmetic  128 us (4%)
  blocking collectives  82 us (3%)
    reduce_scatter x8, waiting for transfers between devices, settle(): lax.psum_scatter(partial_value.astype(jnp.bfloat16), 'col', scatter_dimen...  1110 us
    all_gather x4, waiting for transfers between devices, features(): return lax.all_gather(value, 'col', axis=0, tiled=True)  466 us
    all_gather x4, waiting for transfers between devices, grad_features(): return lax.all_gather(value, 'col', axis=0, tiled=True)  448 us
    dot_general x8, matrix products, weight_grad(): lax.dot_general(left, right, (((0,), (0,)), ((), ())), preferred_element_...  69.5 us
    dot_general x8, matrix products, contract_last(): lax.dot_general(left, right, (((1,), (1,)), ((), ())), preferred_element_...  69 us
  transfers between devices with their start and end apart: 28, of which 19 were waited for; matrix products, arithmetic and copies ran while one was open for 10% of the time, Pallas kernels for 0%

commit v1 on v0

v1 whole, which is shorter than its diff:
```python
import functools
import math

import jax
import jax.numpy as jnp
from jax import lax
from jax.experimental import pallas as pl
from jax.experimental.pallas import tpu as pltpu
from jax.sharding import Mesh, PartitionSpec as P

HEADS = 16
HEAD_DIM = 64
LAYERS = 2
DEPTH = 4

EPSILON = 1e-12
NEGATIVE = -1e30
SQRT_HALF = 0.7071067811865476
ROOT_TWO_PI_INV = 0.3989422804014327
FACTOR = 1.0 / math.sqrt(HEAD_DIM)
VMEM = 52 * 1024 * 1024
F32 = jnp.float32
BF16 = jnp.bfloat16
NT = (((1,), (1,)), ((), ()))
NN = (((1,), (0,)), ((), ()))
ANY_AXES = ("y", "core", "z", "x")


def dot(left, right, dims=NN):
    return lax.dot_general(left, right, dims, preferred_element_type=F32)


def pull(value, axis, step):
    size = lax.axis_size(axis)
    return lax.ppermute(value, axis, [(i, (i + step) % size) for i in range(size)])


def push(value, axis, step):
    size = lax.axis_size(axis)
    return lax.ppermute(value, axis, [(i, (i - step) % size) for i in range(size)])


def spread(value, axis):
    return [value] + [pull(value, axis, s) for s in range(1, lax.axis_size(axis))]


def collect(pieces, axis):
    total = pieces[0].astype(F32)
    for s in range(1, lax.axis_size(axis)):
        total = total + push(pieces[s], axis, s).astype(F32)
    return total


def gather_weight(block, order):
    value = jnp.stack(spread(block, "z"))
    value = jnp.stack(spread(value, order[0]))
    own = spread(value, order[1])
    return own + [pull(piece, "core", 1) for piece in own]


def scatter_weight(pieces, order):
    value = collect(pieces, order[1]).astype(BF16)
    value = collect([value[s] for s in range(value.shape[0])], order[0]).astype(BF16)
    return collect([value[s] for s in range(value.shape[0])], "z")


def relative_blocks(value, axes):
    sizes = [lax.axis_size(axis) for axis in axes]
    count = math.prod(sizes)
    width = value.shape[-1] // count
    parts = []
    for place in range(count):
        low = place % sizes[1]
        high = place // sizes[1]
        source = ((lax.axis_index(axes[0]) - high) % sizes[0]) * sizes[1] + (
            lax.axis_index(axes[1]) - low
        ) % sizes[1]
        parts.append(lax.dynamic_slice_in_dim(value, source * width, width, value.ndim - 1))
    return jnp.concatenate(parts, axis=-1)


def tile(refs, order, core, y, x):
    half = len(refs) // 2
    if order[1] == "x":
        return refs[core * half + x][y, 0]
    return refs[core * half + y][x, 0]


def input_slab(refs, order, ys, xs):
    return jnp.concatenate(
        [
            jnp.concatenate([tile(refs, order, core, y, x) for x in range(xs)], axis=1)
            for y in range(ys)
            for core in range(2)
        ],
        axis=0,
    )


def output_slab(refs, order, ys, xs):
    return jnp.concatenate(
        [
            jnp.concatenate(
                [tile(refs, order, core, y, x) for y in range(ys) for core in range(2)], axis=1
            )
            for x in range(xs)
        ],
        axis=0,
    )


def weight_specs(weights):
    return [
        pl.BlockSpec((w.shape[0], 1, w.shape[2], w.shape[3]), lambda z: (0, z, 0, 0))
        for w in weights
    ]


def whole(value):
    return pl.BlockSpec(value.shape, lambda z: (0,) * len(value.shape))


def by_z(rows, columns):
    return pl.BlockSpec((rows, columns // DEPTH), lambda z: (0, z))


def params():
    return pltpu.CompilerParams(vmem_limit_bytes=VMEM, dimension_semantics=("arbitrary",))


def cost(flops, arrays, special=0):
    return pl.CostEstimate(
        flops=flops,
        bytes_accessed=sum(a.size * a.dtype.itemsize for a in arrays),
        transcendentals=special,
    )


def weight_size(weights):
    return sum(w.size for w in weights)


def queries_kernel(order, ys, xs, x_ref, bias_ref, *refs):
    weights, (q_ref, k_ref, v_ref) = (refs[:-3], refs[-3:])
    mixed = dot(x_ref[...], input_slab(weights, order, ys, xs))
    wide = q_ref.shape[1] // xs
    for x in range(xs):
        here = slice(x * wide, (x + 1) * wide)
        start = x * 3 * wide
        q_ref[:, here] = (mixed[:, start : start + wide] + bias_ref[0:1, here]).astype(BF16)
        k_ref[:, here] = mixed[:, start + wide : start + 2 * wide].astype(BF16)
        v_ref[:, here] = (
            mixed[:, start + 2 * wide : start + 3 * wide] + bias_ref[1:2, here]
        ).astype(BF16)


def queries(value, weights, order, bias, ys, xs):
    rows = value.shape[0]
    columns = bias.shape[1]
    out = jax.ShapeDtypeStruct((rows, columns), BF16)
    return pl.pallas_call(
        functools.partial(queries_kernel, order, ys, xs),
        grid=(DEPTH,),
        in_specs=[whole(value), by_z(bias.shape[0], columns)] + weight_specs(weights),
        out_specs=[by_z(rows, columns)] * 3,
        out_shape=[out] * 3,
        compiler_params=params(),
        cost_estimate=cost(2 * rows * weight_size(weights), [value, *weights, out, out, out]),
        name="queries",
    )(value, bias, *weights)


def hidden_kernel(order, ys, xs, x_ref, bias_ref, *refs):
    weights, (active_ref, slope_ref) = (refs[:-2], refs[-2:])
    slab = input_slab(weights, order, ys, xs)
    rows = x_ref.shape[0]
    step = min(128, rows)

    def part(i, carry):
        at = pl.ds(pl.multiple_of(i * step, step), step)
        inner = dot(x_ref[at, :], slab) + bias_ref[0:1, :]
        phi = 0.5 * (1.0 + lax.erf(inner * SQRT_HALF))
        active_ref[at, :] = (inner * phi).astype(BF16)
        slope_ref[at, :] = (
            phi + inner * jnp.exp(-0.5 * inner * inner) * ROOT_TWO_PI_INV
        ).astype(BF16)
        return carry

    lax.fori_loop(0, rows // step, part, 0)


def hidden(value, weights, order, bias, ys, xs):
    rows = value.shape[0]
    columns = bias.shape[1]
    out = jax.ShapeDtypeStruct((rows, columns), BF16)
    return pl.pallas_call(
        functools.partial(hidden_kernel, order, ys, xs),
        grid=(DEPTH,),
        in_specs=[whole(value), by_z(bias.shape[0], columns)] + weight_specs(weights),
        out_specs=[by_z(rows, columns)] * 2,
        out_shape=[out] * 2,
        compiler_params=params(),
        cost_estimate=cost(
            2 * rows * weight_size(weights), [value, *weights, out, out], 2 * rows * columns
        ),
        name="hidden",
    )(value, bias, *weights)


def hidden_back_kernel(order, ys, xs, g_ref, slope_ref, *refs):
    weights, (grad_ref, sums_ref) = (refs[:-2], refs[-2:])
    slab = output_slab(weights, order, ys, xs)
    rows = g_ref.shape[0]
    step = min(128, rows)
    sums_ref[...] = jnp.zeros_like(sums_ref)

    def part(i, carry):
        at = pl.ds(pl.multiple_of(i * step, step), step)
        grad = (dot(g_ref[at, :], slab, NT) * slope_ref[at, :].astype(F32)).astype(BF16)
        grad_ref[at, :] = grad
        sums_ref[0:1, :] += jnp.sum(grad.astype(F32), axis=0, keepdims=True)
        return carry

    lax.fori_loop(0, rows // step, part, 0)


def hidden_back(grad, weights, order, slope, ys, xs):
    rows, columns = slope.shape
    out = jax.ShapeDtypeStruct((rows, columns), BF16)
    sums = jax.ShapeDtypeStruct((8, columns), F32)
    return pl.pallas_call(
        functools.partial(hidden_back_kernel, order, ys, xs),
        grid=(DEPTH,),
        in_specs=[whole(grad), by_z(rows, columns)] + weight_specs(weights),
        out_specs=[by_z(rows, columns), by_z(8, columns)],
        out_shape=[out, sums],
        compiler_params=params(),
        cost_estimate=cost(2 * rows * weight_size(weights), [grad, slope, *weights, out]),
        name="hidden_back",
    )(grad, slope, *weights)


def context_back_kernel(order, ys, xs, g_ref, *refs):
    refs[-1][...] = dot(g_ref[...], output_slab(refs[:-1], order, ys, xs), NT).astype(BF16)


def context_back(grad, weights, order, ys, xs):
    rows = grad.shape[0]
    out = jax.ShapeDtypeStruct((rows, HEADS * HEAD_DIM), BF16)
    return pl.pallas_call(
        functools.partial(context_back_kernel, order, ys, xs),
        grid=(DEPTH,),
        in_specs=[whole(grad)] + weight_specs(weights),
        out_specs=by_z(*out.shape),
        out_shape=out,
        compiler_params=params(),
        cost_estimate=cost(2 * rows * weight_size(weights), [grad, *weights, out]),
        name="context_back",
    )(grad, *weights)


def norm_kernel(order, ys, xs, scaled, last, left_ref, base_ref, vec_ref, *refs):
    outs = 4 if last else 3
    weights, results, total = (refs[: -outs - 1], refs[-outs - 1 : -1], refs[-1])
    z = pl.program_id(0)
    product = dot(left_ref[...], output_slab(weights, order, ys, xs))

    @pl.when(z == 0)
    def _():
        total[...] = product

    @pl.when(z > 0)
    def _():
        total[...] += product

    @pl.when(z == DEPTH - 1)
    def _():
        rows = total.shape[0]
        step = min(64, rows)

        def part(i, carry):
            at = pl.ds(pl.multiple_of(i * step, step), step)
            base = base_ref[at, :].astype(F32)
            if scaled:
                base = base * vec_ref[0:1, :] + vec_ref[1:2, :]
            summed = base + (total[at, :] + vec_ref[2:3, :])
            offset = summed - jnp.mean(summed, axis=1, keepdims=True)
            inverse = lax.rsqrt(jnp.mean(offset * offset, axis=1, keepdims=True) + EPSILON)
            normal = offset * inverse
            results[0][at, :] = normal
            results[1][at, :] = jnp.broadcast_to(inverse, (step, 128))
            value = normal * vec_ref[3:4, :] + vec_ref[4:5, :]
            results[2][at, :] = value.astype(BF16)
            if last:
                results[3][at, :] = value
            return carry

        lax.fori_loop(0, rows // step, part, 0)


def norm(left, weights, order, base, vectors, scaled, last, ys, xs):
    rows = left.shape[0]
    width = base.shape[1]
    outs = [
        jax.ShapeDtypeStruct((rows, width), F32),
        jax.ShapeDtypeStruct((rows, 128), F32),
        jax.ShapeDtypeStruct((rows, width), BF16),
    ] + ([jax.ShapeDtypeStruct((rows, width), F32)] if last else [])
    return pl.pallas_call(
        functools.partial(norm_kernel, order, ys, xs, scaled, last),
        grid=(DEPTH,),
        in_specs=[by_z(*left.shape), whole(base), whole(vectors)] + weight_specs(weights),
        out_specs=[whole(o) for o in outs],
        out_shape=outs,
        scratch_shapes=[pltpu.VMEM((rows, width), F32)],
        compiler_params=params(),
        cost_estimate=cost(2 * rows * weight_size(weights), [left, base, *weights, *outs]),
        name="norm",
    )(left, base, vectors, *weights)


def norm_back_rows(upstream, normal, inverse, gain):
    scaled = upstream * gain
    first_mean = jnp.mean(scaled, axis=1, keepdims=True)
    second_mean = jnp.mean(scaled * normal, axis=1, keepdims=True)
    return inverse * (scaled - first_mean - normal * second_mean)


def norm_back_kernel(order, ys, xs, lefts, last, *refs):
    left_refs, rest = (refs[:lefts], refs[lefts:])
    base_ref, rest = (rest[0], rest[1:])
    if not last:
        (normal_ref, inverse_ref, gain_ref), rest = (rest[:3], rest[3:])
    outs = 1 if last else 3
    weights, results, total = (rest[: -outs - 1], rest[-outs - 1 : -1], rest[-1])
    z = pl.program_id(0)
    wide = left_refs[0].shape[1] // xs
    left = jnp.concatenate(
        [ref[:, x * wide : (x + 1) * wide] for x in range(xs) for ref in left_refs], axis=1
    )
    product = dot(left, input_slab(weights, order, ys, xs), NT)

    @pl.when(z == 0)
    def _():
        total[...] = product

    @pl.when(z > 0)
    def _():
        total[...] += product

    @pl.when(z == DEPTH - 1)
    def _():
        if last:
            results[0][...] = base_ref[...] + total[...]
            return
        rows = total.shape[0]
        step = min(64, rows)
        results[2][...] = jnp.zeros_like(results[2])

        def part(i, carry):
            at = pl.ds(pl.multiple_of(i * step, step), step)
            upstream = base_ref[at, :] + total[at, :]
            normal = normal_ref[at, :]
            grad = norm_back_rows(upstream, normal, inverse_ref[at, 0:1], gain_ref[0:1, :])
            low = grad.astype(BF16)
            results[0][at, :] = grad
            results[1][at, :] = low
            results[2][0:1, :] += jnp.sum(upstream, axis=0, keepdims=True)
            results[2][1:2, :] += jnp.sum(upstream * normal, axis=0, keepdims=True)
            results[2][2:3, :] += jnp.sum(low.astype(F32), axis=0, keepdims=True)
            return carry

        lax.fori_loop(0, rows // step, part, 0)


def norm_back(lefts, weights, order, base, saved, ys, xs):
    rows, width = base.shape
    last = saved is None
    outs = [jax.ShapeDtypeStruct((rows, width), F32)]
    if not last:
        outs += [jax.ShapeDtypeStruct((rows, width), BF16), jax.ShapeDtypeStruct((8, width), F32)]
    fixed = [base] + ([] if last else list(saved))
    return pl.pallas_call(
        functools.partial(norm_back_kernel, order, ys, xs, len(lefts), last),
        grid=(DEPTH,),
        in_specs=[by_z(*left.shape) for left in lefts]
        + [whole(v) for v in fixed]
        + weight_specs(weights),
        out_specs=[whole(o) for o in outs],
        out_shape=outs,
        scratch_shapes=[pltpu.VMEM((rows, width), F32)],
        compiler_params=params(),
        cost_estimate=cost(2 * rows * weight_size(weights), [*lefts, *fixed, *weights, *outs]),
        name="norm_back",
    )(*lefts, *fixed, *weights)


def outer_kernel(order, ys, xs, rights, left_ref, other_ref, *refs):
    mine, theirs, rest = (refs[:rights], refs[rights : 2 * rights], refs[2 * rights :])
    outs, turned = (rest[:-1], rest[-1])
    rows = left_ref.shape[0]
    deep = left_ref.shape[1] // (2 * ys)

    @pl.when(pl.program_id(0) == 0)
    def _():
        for y in range(ys):
            turned[y * deep : (y + 1) * deep, :rows] = left_ref[
                :, 2 * y * deep : (2 * y + 1) * deep
            ].T
            turned[y * deep : (y + 1) * deep, rows:] = other_ref[
                :, y * deep : (y + 1) * deep
            ].T

    wide = mine[0].shape[1] // xs
    for x in range(xs):
        here = slice(x * wide, (x + 1) * wide)
        right = jnp.concatenate(
            [
                jnp.concatenate([ref[:, here] for ref in mine], axis=1),
                jnp.concatenate([ref[:, here] for ref in theirs], axis=1),
            ],
            axis=0,
        )
        product = dot(turned[...], right).astype(BF16)
        for y in range(ys):
            block = product[y * deep : (y + 1) * deep]
            if order[1] == "x":
                outs[x][y, 0] = block
            else:
                outs[y][x, 0] = block


def outer(left, other, mine, theirs, order, ys, xs):
    rows, width = left.shape
    deep = width // (2 * ys)
    columns = len(mine) * mine[0].shape[1] // (DEPTH * xs)
    first, second = (xs, ys) if order[1] == "x" else (ys, xs)
    outs = [jax.ShapeDtypeStruct((second, DEPTH, deep, columns), BF16)] * first
    return pl.pallas_call(
        functools.partial(outer_kernel, order, ys, xs, len(mine)),
        grid=(DEPTH,),
        in_specs=[whole(left), whole(other)] + [by_z(*r.shape) for r in [*mine, *theirs]],
        out_specs=[
            pl.BlockSpec((second, 1, deep, columns), lambda z: (0, z, 0, 0)) for _ in outs
        ],
        out_shape=outs,
        scratch_shapes=[pltpu.VMEM((ys * deep, 2 * rows), BF16)],
        compiler_params=params(),
        cost_estimate=cost(
            4 * rows * first * outs[0].size, [left, other, *mine, *theirs, *outs]
        ),
        name="outer",
    )(left, other, *mine, *theirs)


def scores_turned(limits_ref, keys, queries_here):
    pieces = []
    for j, key in enumerate(keys):
        score = dot(key, queries_here, NT) * FACTOR
        place = lax.broadcasted_iota(jnp.int32, score.shape, 0)
        pieces.append(jnp.where(place < limits_ref[j], score, NEGATIVE))
    highest = functools.reduce(
        jnp.maximum, [jnp.max(p, axis=0, keepdims=True) for p in pieces]
    )
    raised = [jnp.exp(p - highest) for p in pieces]
    total = functools.reduce(jnp.add, [jnp.sum(r, axis=0, keepdims=True) for r in raised])
    share = 1.0 / total
    return [r * share for r in raised]


def attend_kernel(parts, limits_ref, q_ref, *refs):
    k_refs, v_refs, out_ref = (refs[:parts], refs[parts : 2 * parts], refs[2 * parts])
    rows = q_ref.shape[0]
    step = min(256, rows)
    for pair in range(q_ref.shape[1] // 128):

        def part(i, carry):
            at = pl.ds(pl.multiple_of(i * step, step), step)
            done = []
            for head in (2 * pair, 2 * pair + 1):
                here = slice(head * HEAD_DIM, (head + 1) * HEAD_DIM)
                probs = scores_turned(
                    limits_ref, [k[:, here] for k in k_refs], q_ref[at, here]
                )
                context = functools.reduce(
                    jnp.add,
                    [
                        dot(v[:, here].T, p.astype(BF16))
                        for v, p in zip(v_refs, probs, strict=True)
                    ],
                )
                done.append(context)
            out_ref[at, pair * 128 : pair * 128 + 128] = (
                jnp.concatenate(done, axis=0).T.astype(BF16)
            )
            return carry

        lax.fori_loop(0, rows // step, part, 0)


def attend(limits, query, keys, values):
    rows, width = query.shape
    elements = rows * rows * len(keys) * HEADS
    return pl.pallas_call(
        functools.partial(attend_kernel, len(keys)),
        grid=(DEPTH,),
        in_specs=[pl.BlockSpec(memory_space=pltpu.SMEM)]
        + [by_z(rows, width)] * (1 + 2 * len(keys)),
        out_specs=by_z(rows, width),
        out_shape=jax.ShapeDtypeStruct((rows, width), BF16),
        compiler_params=params(),
        cost_estimate=cost(4 * 4 * HEAD_DIM * elements, [query, *keys, *values], elements),
        name="attend",
    )(limits, query, *keys, *values)


def attend_back_kernel(parts, limits_ref, q_ref, g_ref, *refs):
    k_refs, v_refs, rest = (refs[:parts], refs[parts : 2 * parts], refs[2 * parts :])
    dq_ref, dk_refs, dv_refs = (rest[0], rest[1 : 1 + parts], rest[1 + parts :])
    for pair in range(q_ref.shape[1] // 128):
        done_q, done_k, done_v = ([], [], [])
        for head in (2 * pair, 2 * pair + 1):
            here = slice(head * HEAD_DIM, (head + 1) * HEAD_DIM)
            query = q_ref[:, here]
            grad = g_ref[:, here]
            probs = scores_turned(limits_ref, [k[:, here] for k in k_refs], query)
            grad_probs = [dot(v[:, here], grad, NT) for v in v_refs]
            weighted = functools.reduce(
                jnp.add,
                [
                    jnp.sum(p * g, axis=0, keepdims=True)
                    for p, g in zip(probs, grad_probs, strict=True)
                ],
            )
            grad_scores = [
                (p * (g - weighted)).astype(BF16)
                for p, g in zip(probs, grad_probs, strict=True)
            ]
            done_v.append([dot(p.astype(BF16), grad) for p in probs])
            done_k.append([dot(s, query) * FACTOR for s in grad_scores])
            done_q.append(
                functools.reduce(
                    jnp.add,
                    [
                        dot(k[:, here].T, s)
                        for k, s in zip(k_refs, grad_scores, strict=True)
                    ],
                )
                * FACTOR
            )
        cols = slice(pair * 128, pair * 128 + 128)
        dq_ref[:, cols] = jnp.concatenate(done_q, axis=0).T.astype(BF16)
        for j in range(parts):
            dk_refs[j][:, cols] = jnp.concatenate([d[j] for d in done_k], axis=1).astype(BF16)
            dv_refs[j][:, cols] = jnp.concatenate([d[j] for d in done_v], axis=1).astype(BF16)


def attend_back(limits, query, grad, keys, values):
    rows, width = query.shape
    parts = len(keys)
    elements = rows * rows * parts * HEADS
    outs = [jax.ShapeDtypeStruct((rows, width), BF16)] * (1 + 2 * parts)
    return pl.pallas_call(
        functools.partial(attend_back_kernel, parts),
        grid=(DEPTH,),
        in_specs=[pl.BlockSpec(memory_space=pltpu.SMEM)] + [by_z(rows, width)] * (2 + 2 * parts),
        out_specs=[by_z(rows, width)] * (1 + 2 * parts),
        out_shape=outs,
        compiler_params=params(),
        cost_estimate=cost(
            10 * 4 * HEAD_DIM * elements, [query, grad, *keys, *values, *outs], elements
        ),
        name="attend_back",
    )(limits, query, grad, *keys, *values)


ORDER = {
    "project": ("y", "x"),
    "combiner": ("x", "y"),
    "expand": ("x", "y"),
    "shrink": ("y", "x"),
}


def shards(
    hidden_in,
    cotangent,
    seq_lengths,
    slot_of,
    project,
    offsets,
    combiner,
    recenter,
    stretch,
    displace,
    expand,
    uplift,
    shrink,
    lowering,
    restretch,
    redisplace,
):
    ys, xs = (lax.axis_size("y"), lax.axis_size("x"))
    y, core, z, x = (lax.axis_index(axis) for axis in ANY_AXES)
    rows, width = hidden_in.shape
    slots_here = seq_lengths.shape[0] // (2 * ys)
    parts = xs
    heads_here = HEADS // (DEPTH * xs)
    paired = parts == 2
    if paired:
        trade = [(a * xs + b, b * xs + a) for a in range(2) for b in range(xs)]
        axis, place, slot_row = ("core", core, 2 * y + x)
    else:
        axis, place, slot_row = ("x", x, 2 * y + core)

    def regroup(value):
        return lax.ppermute(value, ("core", "x"), trade) if paired else value

    def features(value):
        return relative_blocks(value, ("y", "core"))

    slot = slot_row * slots_here + z
    length = jnp.sum(jnp.where(slot_of == slot, seq_lengths, 0))
    limits = jnp.stack([length - ((place - j) % parts) * rows for j in range(parts)])

    def heads_first(block):
        return (
            block.reshape(-1, heads_here, 3, HEAD_DIM).transpose(0, 2, 1, 3).reshape(block.shape)
        )

    weights = []
    for layer in range(LAYERS):
        weights.append(
            {
                "project": gather_weight(heads_first(project[layer]), ORDER["project"]),
                "combiner": gather_weight(combiner[layer], ORDER["combiner"]),
                "expand": gather_weight(expand[layer], ORDER["expand"]),
                "shrink": gather_weight(shrink[layer], ORDER["shrink"]),
            }
        )
    biases = lax.all_gather(
        jnp.concatenate([offsets.reshape(-1), uplift.reshape(-1)]), ("z", "x"), axis=0
    )
    cut = offsets.size
    offsets_full = biases[:, :cut].reshape(-1, LAYERS, heads_here, 2, HEAD_DIM)
    uplift_full = biases[:, cut:].reshape(-1, LAYERS, uplift.shape[1])

    def hidden_order(value):
        return relative_blocks(value, ("z", "x"))

    query_bias = hidden_order(offsets_full[:, :, :, 0].transpose(1, 0, 2, 3).reshape(LAYERS, -1))
    value_bias = hidden_order(offsets_full[:, :, :, 1].transpose(1, 0, 2, 3).reshape(LAYERS, -1))
    inner_bias = hidden_order(uplift_full.transpose(1, 0, 2).reshape(LAYERS, -1))

    start = features(regroup(hidden_in))
    recenter, stretch, displace, lowering, restretch, redisplace = (
        features(v) for v in (recenter, stretch, displace, lowering, restretch, redisplace)
    )
    nothing = jnp.zeros_like(recenter[0])

    def vectors(*items):
        return jnp.stack(list(items) + [nothing] * (8 - len(items)))

    saved = []
    current_low, base, base_gain, base_shift, scaled = (start, start, nothing, nothing, False)
    finished = None
    for layer in range(LAYERS):
        w = weights[layer]
        query, key, value = queries(
            current_low,
            w["project"],
            ORDER["project"],
            vectors(query_bias[layer], value_bias[layer]),
            ys,
            xs,
        )
        keys = spread(key, axis)
        values = spread(value, axis)
        context = attend(limits, query, keys, values)
        normal_one, inverse_one, normed_low = norm(
            context,
            w["combiner"],
            ORDER["combiner"],
            base,
            vectors(base_gain, base_shift, recenter[layer], stretch[layer], displace[layer]),
            scaled,
            False,
            ys,
            xs,
        )
        active, slope = hidden(
            normed_low,
            w["expand"],
            ORDER["expand"],
            jnp.broadcast_to(inner_bias[layer][None], (8, inner_bias.shape[1])),
            ys,
            xs,
        )
        normal_two, inverse_two, next_low, *finished = norm(
            active,
            w["shrink"],
            ORDER["shrink"],
            normal_one,
            vectors(
                stretch[layer], displace[layer], lowering[layer], restretch[layer], redisplace[layer]
            ),
            True,
            layer == LAYERS - 1,
            ys,
            xs,
        )
        saved.append(
            (
                current_low,
                query,
                keys,
                values,
                context,
                normal_one,
                inverse_one,
                normed_low,
                active,
                slope,
                normal_two,
                inverse_two,
            )
        )
        current_low, base, scaled = (next_low, normal_two, True)
        base_gain, base_shift = (restretch[layer], redisplace[layer])
    hidden_out = regroup(features(finished[0]))

    def other_core(value):
        return pull(value, "core", 1)

    def other_features(value):
        return other_core(value.reshape(rows, ys, 2, -1)[:, :, 1].reshape(rows, -1))

    upstream = features(regroup(cotangent))
    _, _, _, _, _, _, _, _, _, _, normal_two, inverse_two = saved[-1]
    grad_two = norm_back_rows(
        upstream, normal_two, inverse_two[:, 0:1], restretch[LAYERS - 1][None]
    )
    grad_two_low = grad_two.astype(BF16)
    sums_two = jnp.stack(
        [
            jnp.sum(upstream, axis=0),
            jnp.sum(upstream * normal_two, axis=0),
            jnp.sum(grad_two_low.astype(F32), axis=0),
        ]
    )
    grads = {name: [] for name in ORDER}
    small = []
    hidden_grad = None
    for layer in reversed(range(LAYERS)):
        w = weights[layer]
        (
            layer_low,
            query,
            keys,
            values,
            context,
            normal_one,
            inverse_one,
            normed_low,
            active,
            slope,
            _,
            _,
        ) = saved[layer]
        grad_inner, sums_inner = hidden_back(
            grad_two_low, w["shrink"], ORDER["shrink"], slope, ys, xs
        )
        grads["shrink"].append(
            scatter_weight(
                outer(
                    grad_two_low,
                    other_features(grad_two_low),
                    [active],
                    [other_core(active)],
                    ORDER["shrink"],
                    ys,
                    xs,
                ),
                ORDER["shrink"],
            ).T
        )
        grads["expand"].append(
            scatter_weight(
                outer(
                    normed_low,
                    other_features(normed_low),
                    [grad_inner],
                    [other_core(grad_inner)],
                    ORDER["expand"],
                    ys,
                    xs,
                ),
                ORDER["expand"],
            )
        )
        grad_one, grad_one_low, sums_one = norm_back(
            [grad_inner],
            w["expand"],
            ORDER["expand"],
            grad_two,
            (normal_one, inverse_one, vectors(stretch[layer])),
            ys,
            xs,
        )
        grads["combiner"].append(
            scatter_weight(
                outer(
                    grad_one_low,
                    other_features(grad_one_low),
                    [context],
                    [other_core(context)],
                    ORDER["combiner"],
                    ys,
                    xs,
                ),
                ORDER["combiner"],
            ).T
        )
        grad_context = context_back(grad_one_low, w["combiner"], ORDER["combiner"], ys, xs)
        grad_query, *pieces = attend_back(limits, query, grad_context, keys, values)
        grad_key = collect(pieces[:parts], axis).astype(BF16)
        grad_value = collect(pieces[parts:], axis).astype(BF16)
        triple = [grad_query, grad_key, grad_value]
        small.append(
            (
                sums_one,
                sums_two,
                sums_inner[0],
                jnp.sum(grad_query.astype(F32), axis=0),
                jnp.sum(grad_value.astype(F32), axis=0),
            )
        )
        lower = None
        if layer > 0:
            lower = (saved[layer - 1][10], saved[layer - 1][11], vectors(restretch[layer - 1]))
        result = norm_back(triple, w["project"], ORDER["project"], grad_one, lower, ys, xs)
        if layer > 0:
            grad_two, grad_two_low, sums_two = result
        else:
            hidden_grad = regroup(features(result[0]))
        turned = scatter_weight(
            outer(
                layer_low,
                other_features(layer_low),
                triple,
                [other_core(t) for t in triple],
                ORDER["project"],
                ys,
                xs,
            ),
            ORDER["project"],
        )
        grads["project"].append(
            turned.reshape(-1, 3, heads_here, HEAD_DIM)
            .transpose(0, 2, 1, 3)
            .reshape(turned.shape)
        )

    def ordered(items):
        return jnp.stack(items[::-1], axis=0)

    def column(flat):
        return flat.reshape(LAYERS, DEPTH * xs, -1)

    totals = []
    for sums_one, sums_two, sums_inner, sums_query, sums_value in small:
        totals.append(
            lax.psum(
                jnp.concatenate(
                    [features(sums_one[s]) for s in range(3)]
                    + [features(sums_two[s]) for s in range(3)]
                    + [hidden_order(sums_inner), hidden_order(sums_query), hidden_order(sums_value)]
                ),
                ANY_AXES,
            )
        )
    total = ordered(totals)
    norms = total[:, : 6 * width].reshape(LAYERS, 6, width)
    rest = total[:, 6 * width :]
    units = sums_inner.shape[0]
    here = z * xs + x

    def own(flat):
        return lax.dynamic_index_in_dim(column(flat), here, 1, keepdims=False)

    uplift_grad = own(rest[:, :units])
    query_grad = own(rest[:, units : units + width]).reshape(LAYERS, heads_here, HEAD_DIM)
    value_grad = own(rest[:, units + width :]).reshape(LAYERS, heads_here, HEAD_DIM)
    offsets_grad = jnp.stack([query_grad, value_grad], axis=2).reshape(LAYERS, -1)
    return (
        hidden_out,
        hidden_grad,
        ordered(grads["project"]),
        offsets_grad,
        ordered(grads["combiner"]),
        norms[:, 2],
        norms[:, 1],
        norms[:, 0],
        ordered(grads["expand"]),
        uplift_grad,
        ordered(grads["shrink"]),
        norms[:, 5],
        norms[:, 4],
        norms[:, 3],
    )


def solution(mesh):
    rows, columns = (mesh.shape["row"], mesh.shape["col"])
    fine = Mesh(mesh.devices.reshape(rows // 2, 2, DEPTH, columns // DEPTH), ANY_AXES)
    row, col = (("y", "core"), ("z", "x"))
    in_specs = (
        P(ANY_AXES, None),
        P(ANY_AXES, None),
        P(),
        P(),
        P(None, row, col),
        P(None, col),
        P(None, col, row),
        P(),
        P(),
        P(),
        P(None, row, col),
        P(None, col),
        P(None, col, row),
        P(),
        P(),
        P(),
    )
    out_specs = (
        P(ANY_AXES, None),
        P(ANY_AXES, None),
        P(None, row, col),
        P(None, col),
        P(None, col, row),
        P(),
        P(),
        P(),
        P(None, row, col),
        P(None, col),
        P(None, col, row),
        P(),
        P(),
        P(),
    )
    return jax.shard_map(shards, mesh=fine, in_specs=in_specs, out_specs=out_specs, check_vma=False)
```

time: 2870 us -> 1350 us (0.47)
  waiting for transfers between devices: 2050 us -> 520 us
  Pallas kernels: 0 us -> 357 us
  matrix products: 355 us -> 0 us
  starting transfers between devices: 2.17 us -> 200 us
  local copies, waits for them, and re-layouts: 222 us -> 123 us
  blocking collectives: 82 us -> 30.7 us
  other arithmetic: 128 us -> 78.3 us
    reduce_scatter x16 -> x0, waiting for transfers between devices: 1110 us -> none  [the longest x8 1110 us: settle(): lax.psum_scatter(partial_value.astype(jnp.bfloat16), 'col', scatter_dimen...]
    all_gather x12 -> x0, waiting for transfers between devices: 938 us -> none  [the longest x4 466 us: features(): return lax.all_gather(value, 'col', axis=0, tiled=True)]
    ppermute x0 -> x128, waiting for transfers between devices: none -> 408 us  [the longest x44 219 us: push(): lax.ppermute(value, axis, [(i, (i - step) % size) for i in range(size)])]
    pallas_call x0 -> x28, Pallas kernels: none -> 357 us  [the longest x2 68.8 us: attend_back(): pl.pallas_call(functools.partial(attend_back_kernel, parts), grid=(DEPTH,...]
    dot_general x136 -> x0, matrix products: 355 us -> none  [the longest x8 69.5 us: weight_grad(): lax.dot_general(left, right, (((0,), (0,)), ((), ())), preferred_element_...]
    ppermute x0 -> x128, starting transfers between devices: none -> 200 us  [the longest x44 76.1 us: push(): lax.ppermute(value, axis, [(i, (i - step) % size) for i in range(size)])]
    psum x0 -> x1, waiting for transfers between devices: none -> 111 us  [shards(): lax.psum(jnp.concatenate([features(sums_one[s]) for s in range(3)] + [fea...]
    reduce_sum x37 -> x7, other arithmetic: 65.9 us -> 9.8 us  [the longest x2 4.05 us: shards(): jnp.sum(grad_value.astype(F32), axis=0)]
  transfers between devices with their start and end apart: 28 -> 129, of which waited for: 19 -> 37; matrix products, arithmetic and copies ran while one was open for 10% -> 14% of each run, Pallas kernels for 0% -> 27%
where the time goes in v1:
time: 1350 us; the launch traced here: 1330 us
  waiting for transfers between devices  520 us (39%)
  Pallas kernels  357 us (26%)
  starting transfers between devices  200 us (15%)
  local copies, waits for them, and re-layouts  123 us (9%)
  other arithmetic  78.3 us (6%)
  blocking collectives  30.7 us (2%)
  between operations  18.2 us (1%)
    ppermute x44, waiting for transfers between devices, push(): lax.ppermute(value, axis, [(i, (i - step) % size) for i in range(size)])  219 us
    ppermute x80, waiting for transfers between devices, pull(): lax.ppermute(value, axis, [(i, (i + step) % size) for i in range(size)])  189 us
    psum x1, waiting for transfers between devices, shards(): lax.psum(jnp.concatenate([features(sums_one[s]) for s in range(3)] + [fea...  111 us
    ppermute x44, starting transfers between devices, push(): lax.ppermute(value, axis, [(i, (i - step) % size) for i in range(size)])  76.1 us
    pallas_call x2, Pallas kernels, attend_back(): pl.pallas_call(functools.partial(attend_back_kernel, parts), grid=(DEPTH,...  68.8 us
    ppermute x80, starting transfers between devices, pull(): lax.ppermute(value, axis, [(i, (i + step) % size) for i in range(size)])  63 us
    pallas_call x8, Pallas kernels, outer(): pl.pallas_call(functools.partial(outer_kernel, order, ys, xs, len(mine)),...  62.4 us
    ppermute x4, starting transfers between devices, regroup(): return lax.ppermute(value, ('core', 'x'), trade) if paired else value  60.9 us
  transfers between devices with their start and end apart: 129, of which 37 were waited for; matrix products, arithmetic and copies ran while one was open for 14% of the time, Pallas kernels for 27%

profile of v1, /device:TPU:0, one launch (start us, length us, event | category | flops | bytes accessed | tf_op | source)
XLA Modules:
  0.0 1326.7 jit_solution(366649407712197874)
XLA Ops:
  8.2 5.1 collective-permute-start.12
  19.8 30.7 %all-gather.1 = f32[8,1,1536]{2,1,0:T(1,128)S(1)} all-gather(f32[1,1,1536]{2,1,0:T(1,128)S(1)} %reshape.235), channel_id=2, replica_groups=mesh['y'=2,'core'=2,'z'=4,'x'=2] {'z','x'}, dimensions={0}, use_global_device_ids=true | all-gather | bytes 55296 | tf_op jit(solution)/shard_map/all_gather | solution.py:641
  61.0 19.5 %collective-permute-done.41 = bf16[128,256]{1,0:T(8,128)(2,1)S(1)} collective-permute-done((bf16[128,256]{1,0:T(8,128)(2,1)S(1)}, bf16[128,256]{1,0:T(8,128)(2,1)S(1)}, u32[]{:S(2)}, u32[]{:S(2)}) %collective-permute-start.41) | collective-permute-done | bytes 65568 | tf_op jit(solution)/shard_map/ppermute | solution.py:35
  90.4 14.7 %collective-permute-done.32 = bf16[256,384]{1,0:T(8,128)(2,1)S(1)} collective-permute-done((bf16[256,384]{1,0:T(8,128)(2,1)}, bf16[256,384]{1,0:T(8,128)(2,1)S(1)}, u32[]{:S(2)}, u32[]{:S(2)}) %collective-permute-start.32) | collective-permute-done | bytes 196640 | tf_op jit(solution)/shard_map/ppermute | solution.py:35
  107.1 5.9 collective-permute-start.25
  113.1 14.5 %collective-permute-done.18 = bf16[256,512]{1,0:T(8,128)(2,1)S(1)} collective-permute-done((bf16[256,512]{1,0:T(8,128)(2,1)S(1)}, bf16[256,512]{1,0:T(8,128)(2,1)S(1)}, u32[]{:S(2)}, u32[]{:S(2)}) %collective-permute-start.18) | collective-permute-done | bytes 262176 | tf_op jit(solution)/shard_map/ppermute | solution.py:35
  140.9 12.0 collective-permute-done.25
  158.2 8.1 collective-permute-done.48
  172.5 9.6 collective-permute-start
  197.1 8.0 collective-permute-done.34
  208.5 9.4 collective-permute-done.20
  227.6 12.8 collective-permute-done.50
  243.7 6.4 collective-permute-done.57
  253.0 21.2 %collective-permute-done.5.refs_1_.refs_5_ = bf16[2,4,256,384]{3,2,1,0:T(8,128)(2,1)} collective-permute-done((bf16[2,4,256,384]{3,2,1,0:T(8,128)(2,1)}, bf16[2,4,256,384]{3,2,1,0:T(8,128)(2,1)}, u32[]{:S(2)}, u32[]{:S(2)}) %collective-permute-start.5) | collective-permute-done | bytes 1572896 | tf_op jit(solution)/shard_map/ppermute | solution.py:35
  279.3 28.6 %collective-permute-done.35.refs_1_.refs_8_ = bf16[2,4,256,384]{3,2,1,0:T(8,128)(2,1)} collective-permute-done((bf16[2,4,256,384]{3,2,1,0:T(8,128)(2,1)}, bf16[2,4,256,384]{3,2,1,0:T(8,128)(2,1)}, u32[]{:S(2)}, u32[]{:S(2)}) %collective-permute-start.35) | collective-permute-done | bytes 1572896 | tf_op jit(solution)/shard_map/ppermute | solution.py:35
  314.1 7.4 queries.2
  324.7 24.7 %collective-permute-done.28.refs_1_ = bf16[2,4,512,256]{3,2,1,0:T(8,128)(2,1)} collective-permute-done((bf16[2,4,512,256]{3,2,1,0:T(8,128)(2,1)}, bf16[2,4,512,256]{3,2,1,0:T(8,128)(2,1)}, u32[]{:S(2)}, u32[]{:S(2)}) %collective-permute-start.28) | collective-permute-done | bytes 2097184 | tf_op jit(solution)/shard_map/ppermute | solution.py:35
  357.7 17.1 %collective-permute-start.62 = (f32[512,1024]{1,0:T(8,128)}, f32[512,1024]{1,0:T(8,128)}, u32[]{:S(2)}, u32[]{:S(2)}) collective-permute-start(f32[512,1024]{1,0:T(8,128)} %param.17), channel_id=1, source_target_pairs={{0,0},{1,8},{8,1},{9,9},{2,2},{3,10},{10,3},{11,11},{4,4},{5,12},{... | collective-permute-start | bytes 6291464 | tf_op jit(solution)/shard_map/ppermute | solution.py:617
  376.3 27.1 %attend.2.left_ref.refs_0_ = bf16[512,1024]{1,0:T(8,128)(2,1)} custom-call(s32[2]{0:T(128)S(1)} %pad_add_fusion.limits_ref, bf16[512,1024]{1,0:T(8,128)(2,1)} %copy-done.40, bf16[512,1024]{1,0:T(8,128)(2,1)} %get-tuple-element.76.refs_0_, bf16[512,1024]{1,0:T(8,128)(2,1)} %collective-permute-done.8.refs_1_, bf16[512,1024]{1,0:T(8,128)(2,1)} %get-tuple-element.77.refs_2_, ...), custom_call_target="tpu_custom_call" | custom-call | flops 8589934592 | bytes 5242880 | tf_op jit(solution)/shard_map/attend/pallas_call | solution.py:504
  403.4 7.9 norm.4
  413.5 12.6 hidden.2
  426.6 12.1 norm.5
  440.9 7.4 queries.3
  455.6 4.9 slice_reduce_fusion.7
  466.9 4.9 slice_reduce_fusion.3
  480.3 26.9 %attend.3.left_ref.refs_0_ = bf16[512,1024]{1,0:T(8,128)(2,1)} custom-call(s32[2]{0:T(128)S(1)} %pad_add_fusion.limits_ref, bf16[512,1024]{1,0:T(8,128)(2,1)} %copy-done.41, bf16[512,1024]{1,0:T(8,128)(2,1)} %get-tuple-element.83.refs_0_, bf16[512,1024]{1,0:T(8,128)(2,1)} %collective-permute-done.38.refs_1_, bf16[512,1024]{1,0:T(8,128)(2,1)} %get-tuple-element.84.refs_2_, ...), custom_call_target="tpu_custom_call" | custom-call | flops 8589934592 | bytes 5242880 | tf_op jit(solution)/shard_map/attend/pallas_call | solution.py:504
  508.0 8.6 norm.6
  520.4 12.3 hidden.3
  532.7 13.2 norm.7
  552.4 16.9 %hidden_back.2 = (bf16[512,4096]{1,0:T(8,128)(2,1)}, f32[8,4096]{1,0:T(8,128)S(1)}) custom-call(bf16[512,1024]{1,0:T(8,128)(2,1)S(1)} %get-tuple-element.189.g_ref.left_ref, bf16[512,4096]{1,0:T(8,128)(2,1)} %get-tuple-element.92.slope_ref, bf16[2,4,512,256]{3,2,1,0:T(8,128)(2,1)} %pad_maximum_fusion.3.refs_0_, ...), custom_call_target="tpu_custom_call" | custom-call | flops 4294967296 | bytes 17825792 | tf_op jit(solution)/shard_map/hidden_back/pallas_call | solution.py:231
  570.0 12.8 norm_back.4
  592.2 34.6 %attend_back.2 = (bf16[512,1024]{1,0:T(8,128)(2,1)S(1)}, bf16[512,1024]{1,0:T(8,128)(2,1)}, bf16[512,1024]{1,0:T(8,128)(2,1)}, bf16[512,1024]{1,0:T(8,128)(2,1)}, bf16[512,1024]{1,0:T(8,128)(2,1)}) custom-call(s32[2]{0:T(128)S(1)} %pad_add_fusion.limits_ref, bf16[512,1024]{1,0:T(8,128)(2,1)} %copy-done.41, bf16[512,1024]{1,0:T(8,128)(2,1)} %context_back.2.g_ref, ...), custom_call_target="tpu_custom_call" | custom-call | flops 21474836480 | bytes 11534336 | tf_op jit(solution)/shard_map/attend_back/pallas_call | solution.py:563
  648.5 11.5 norm_back.5
  660.1 17.2 %hidden_back.3 = (bf16[512,4096]{1,0:T(8,128)(2,1)}, f32[8,4096]{1,0:T(8,128)S(1)}) custom-call(bf16[512,1024]{1,0:T(8,128)(2,1)S(1)} %get-tuple-element.103.g_ref.left_ref, bf16[512,4096]{1,0:T(8,128)(2,1)} %get-tuple-element.104.slope_ref, bf16[2,4,512,256]{3,2,1,0:T(8,128)(2,1)} %pad_maximum_fusion.1.refs_0_, ...), custom_call_target="tpu_custom_call" | custom-call | flops 4294967296 | bytes 17825792 | tf_op jit(solution)/shard_map/hidden_back/pallas_call | solution.py:231
  678.0 12.8 norm_back.6
  700.2 34.2 %attend_back.3 = (bf16[512,1024]{1,0:T(8,128)(2,1)S(1)}, bf16[512,1024]{1,0:T(8,128)(2,1)}, bf16[512,1024]{1,0:T(8,128)(2,1)}, bf16[512,1024]{1,0:T(8,128)(2,1)}, bf16[512,1024]{1,0:T(8,128)(2,1)}) custom-call(s32[2]{0:T(128)S(1)} %pad_add_fusion.limits_ref, bf16[512,1024]{1,0:T(8,128)(2,1)} %copy-done.40, bf16[512,1024]{1,0:T(8,128)(2,1)} %context_back.3.g_ref, ...), custom_call_target="tpu_custom_call" | custom-call | flops 21474836480 | bytes 11534336 | tf_op jit(solution)/shard_map/attend_back/pallas_call | solution.py:563
  742.1 5.7 outer.11
  757.1 5.0 collective-permute-done.95
  763.7 6.4 collective-permute-done.96
  775.1 5.0 outer.10
  784.1 17.1 %collective-permute-start.61 = (f32[512,1024]{1,0:T(8,128)}, f32[512,1024]{1,0:T(8,128)}, u32[]{:S(2)}, u32[]{:S(2)}) collective-permute-start(f32[512,1024]{1,0:T(8,128)} %pad_maximum_fusion.4), channel_id=1, source_target_pairs={{0,0},{1,8},{8,1},{9,9},{2,2},{3,10},{10,3},{11,11},{4,4},{5,12},{... | collective-permute-start | bytes 6291464 | tf_op jit(solution)/shard_map/ppermute | solution.py:617
  803.8 9.5 norm_back.7
  814.9 8.2 outer.9
  830.6 6.2 collective-permute-done.89
  850.0 111.4 %all-reduce.3.cloned.1.call-done = (f32[1,12288]{1,0:T(1,128)}, f32[1,12288]{1,0:T(1,128)}) async-done(((f32[1,12288]{1,0:T(1,128)}, f32[1,12288]{1,0:T(1,128)}), (f32[1,12288]{1,0:T(1,128)}, f32[1,12288]{1,0:T(1,128)})) %all-reduce.3.cloned.1.call-update) | async-done | bytes 98320 | tf_op jit(solution)/shard_map/psum | solution.py:873
  963.0 17.1 %collective-permute-start.67 = (f32[512,1024]{1,0:T(8,128)}, f32[512,1024]{1,0:T(8,128)}, u32[]{:S(2)}, u32[]{:S(2)}) collective-permute-start(f32[512,1024]{1,0:T(8,128)} %pad_maximum_fusion.6), channel_id=1, source_target_pairs={{0,0},{1,8},{8,1},{9,9},{2,2},{3,10},{10,3},{11,11},{4,4},{5,12},{... | collective-permute-start | bytes 6291464 | tf_op jit(solution)/shard_map/ppermute | solution.py:617
  983.8 8.3 outer.8
  992.7 8.9 outer.14
  1001.6 22.8 %collective-permute-done.81 = bf16[2,4,256,384]{3,2,1,0:T(8,128)(2,1)} collective-permute-done((bf16[2,4,256,384]{3,2,1,0:T(8,128)(2,1)}, bf16[2,4,256,384]{3,2,1,0:T(8,128)(2,1)}, u32[]{:S(2)}, u32[]{:S(2)}) %collective-permute-start.81) | collective-permute-done | bytes 1572896 | tf_op jit(solution)/shard_map/ppermute | solution.py:40
  1029.5 8.8 outer.13
  1038.4 8.8 outer.15
  1049.0 13.1 collective-permute-done.72
  1065.0 41.9 %collective-permute-done.116 = bf16[2,4,256,512]{3,2,1,0:T(8,128)(2,1)S(1)} collective-permute-done((bf16[2,4,256,512]{3,2,1,0:T(8,128)(2,1)}, bf16[2,4,256,512]{3,2,1,0:T(8,128)(2,1)S(1)}, u32[]{:S(2)}, u32[]{:S(2)}) %collective-permute-start.116) | collective-permute-done | bytes 2097184 | tf_op jit(solution)/shard_map/ppermute | solution.py:40
  1117.5 5.9 collective-permute-done.84
  1131.0 5.3 collective-permute-done.76
  1137.6 8.8 outer.12
  1152.1 5.7 collective-permute-start.120
  1164.8 23.2 %collective-permute-done.109 = bf16[2,4,256,512]{3,2,1,0:T(8,128)(2,1)} collective-permute-done((bf16[2,4,256,512]{3,2,1,0:T(8,128)(2,1)}, bf16[2,4,256,512]{3,2,1,0:T(8,128)(2,1)}, u32[]{:S(2)}, u32[]{:S(2)}) %collective-permute-start.109) | collective-permute-done | bytes 2097184 | tf_op jit(solution)/shard_map/ppermute | solution.py:40
  1191.1 41.9 %collective-permute-done.102 = bf16[2,4,256,512]{3,2,1,0:T(8,128)(2,1)} collective-permute-done((bf16[2,4,256,512]{3,2,1,0:T(8,128)(2,1)}, bf16[2,4,256,512]{3,2,1,0:T(8,128)(2,1)}, u32[]{:S(2)}, u32[]{:S(2)}) %collective-permute-start.102) | collective-permute-done | bytes 2097184 | tf_op jit(solution)/shard_map/ppermute | solution.py:40
  1236.2 13.9 %collective-permute-done.124 = bf16[4,256,512]{2,1,0:T(8,128)(2,1)S(1)} collective-permute-done((bf16[4,256,512]{2,1,0:T(8,128)(2,1)S(1)}, bf16[4,256,512]{2,1,0:T(8,128)(2,1)S(1)}, u32[]{:S(2)}, u32[]{:S(2)}) %collective-permute-start.124) | collective-permute-done | bytes 1048608 | tf_op jit(solution)/shard_map/ppermute | solution.py:40
  1256.1 5.5 collective-permute-done.127
  1261.6 10.5 collective-permute-start.112
  1272.8 11.5 collective-permute-start.111
  1300.5 11.6 collective-permute-done.105
  (857 shorter events, 327.0 us)
Async XLA Ops:
  7.2 954.2 %all-reduce.3.cloned.1.call-start = ((), (), s32[]{:S(2)}) async-start(), calls=%async_computation | async-start | bytes 196608 | tf_op jit(solution)/shard_map/psum | solution.py:873
  8.2 48.2 %collective-permute-start.12 = (bf16[128,256]{1,0:T(8,128)(2,1)S(1)}, bf16[128,256]{1,0:T(8,128)(2,1)S(1)}, u32[]{:S(2)}, u32[]{:S(2)}) collective-permute-start(bf16[128,256]{1,0:T(8,128)(2,1)S(1)} %get-tuple-element.258), channel_id=1, source_target_pairs={{0,6},{2,0},{4,2},{6,4},{1,7},{3,1},{5,3},{7,5},{8,14},{10,8},{12,... | collective-permute-start | bytes 196616 | tf_op jit(solution)/shard_map/ppermute | solution.py:35
  13.3 43.2 %collective-permute-start.11 = (bf16[128,256]{1,0:T(8,128)(2,1)S(1)}, bf16[128,256]{1,0:T(8,128)(2,1)S(1)}, u32[]{:S(2)}, u32[]{:S(2)}) collective-permute-start(bf16[128,256]{1,0:T(8,128)(2,1)S(1)} %get-tuple-element.258), channel_id=1, source_target_pairs={{0,4},{2,6},{4,0},{6,2},{1,5},{3,7},{5,1},{7,3},{8,12},{10,14},{12... | collective-permute-start | bytes 196616 | tf_op jit(solution)/shard_map/ppermute | solution.py:35
  13.3 44.3 %collective-permute-start.10 = (bf16[128,256]{1,0:T(8,128)(2,1)S(1)}, bf16[128,256]{1,0:T(8,128)(2,1)S(1)}, u32[]{:S(2)}, u32[]{:S(2)}) collective-permute-start(bf16[128,256]{1,0:T(8,128)(2,1)S(1)} %get-tuple-element.258), channel_id=1, source_target_pairs={{0,2},{2,4},{4,6},{6,0},{1,3},{3,5},{5,7},{7,1},{8,10},{10,12},{12... | collective-permute-start | bytes 196616 | tf_op jit(solution)/shard_map/ppermute | solution.py:35
  16.4 67.5 %collective-permute-start.3 = (bf16[256,384]{1,0:T(8,128)(2,1)}, bf16[256,384]{1,0:T(8,128)(2,1)S(1)}, u32[]{:S(2)}, u32[]{:S(2)}) collective-permute-start(bf16[256,384]{1,0:T(8,128)(2,1)} %copy.80), channel_id=1, source_target_pairs={{0,6},{2,0},{4,2},{6,4},{1,7},{3,1},{5,3},{7,5},{8,14},{10,8},{12,... | collective-permute-start | bytes 589832 | tf_op jit(solution)/shard_map/ppermute | solution.py:35
  19.2 40.3 %collective-permute-start.42 = (bf16[128,256]{1,0:T(8,128)(2,1)S(1)}, bf16[128,256]{1,0:T(8,128)(2,1)S(1)}, u32[]{:S(2)}, u32[]{:S(2)}) collective-permute-start(bf16[128,256]{1,0:T(8,128)(2,1)S(1)} %get-tuple-element.259), channel_id=1, source_target_pairs={{0,6},{2,0},{4,2},{6,4},{1,7},{3,1},{5,3},{7,5},{8,14},{10,8},{12,... | collective-permute-start | bytes 196616 | tf_op jit(solution)/shard_map/ppermute | solution.py:35
  89.0 38.6 %collective-permute-start.18 = (bf16[256,512]{1,0:T(8,128)(2,1)S(1)}, bf16[256,512]{1,0:T(8,128)(2,1)S(1)}, u32[]{:S(2)}, u32[]{:S(2)}) collective-permute-start(bf16[256,512]{1,0:T(8,128)(2,1)S(1)} %get-tuple-element.242), channel_id=1, source_target_pairs={{0,4},{2,6},{4,0},{6,2},{1,5},{3,7},{5,1},{7,3},{8,12},{10,14},{12... | collective-permute-start | bytes 786440 | tf_op jit(solution)/shard_map/ppermute | solution.py:35
  90.4 38.4 %collective-permute-start.17 = (bf16[256,512]{1,0:T(8,128)(2,1)S(1)}, bf16[256,512]{1,0:T(8,128)(2,1)S(1)}, u32[]{:S(2)}, u32[]{:S(2)}) collective-permute-start(bf16[256,512]{1,0:T(8,128)(2,1)S(1)} %get-tuple-element.242), channel_id=1, source_target_pairs={{0,2},{2,4},{4,6},{6,0},{1,3},{3,5},{5,7},{7,1},{8,10},{10,12},{12... | collective-permute-start | bytes 786440 | tf_op jit(solution)/shard_map/ppermute | solution.py:35
  107.1 45.7 %collective-permute-start.25 = (bf16[512,256]{1,0:T(8,128)(2,1)S(1)}, bf16[512,256]{1,0:T(8,128)(2,1)S(1)}, u32[]{:S(2)}, u32[]{:S(2)}) collective-permute-start(bf16[512,256]{1,0:T(8,128)(2,1)S(1)} %get-tuple-element.238), channel_id=1, source_target_pairs={{0,4},{2,6},{4,0},{6,2},{1,5},{3,7},{5,1},{7,3},{8,12},{10,14},{12... | collective-permute-start | bytes 786440 | tf_op jit(solution)/shard_map/ppermute | solution.py:35
  132.7 33.7 %collective-permute-start.48 = (bf16[256,512]{1,0:T(8,128)(2,1)}, bf16[256,512]{1,0:T(8,128)(2,1)}, u32[]{:S(2)}, u32[]{:S(2)}) collective-permute-start(bf16[256,512]{1,0:T(8,128)(2,1)} %get-tuple-element.243), channel_id=1, source_target_pairs={{0,4},{2,6},{4,0},{6,2},{1,5},{3,7},{5,1},{7,3},{8,12},{10,14},{12... | collective-permute-start | bytes 786440 | tf_op jit(solution)/shard_map/ppermute | solution.py:35
  172.5 36.0 %collective-permute-start = (bf16[512,1024]{1,0:T(8,128)(2,1)}, bf16[512,1024]{1,0:T(8,128)(2,1)}, u32[]{:S(2)}, u32[]{:S(2)}) collective-permute-start(bf16[512,1024]{1,0:T(8,128)(2,1)} %param.16), channel_id=1, source_target_pairs={{0,0},{1,8},{8,1},{9,9},{2,2},{3,10},{10,3},{11,11},{4,4},{5,12},{... | collective-permute-start | bytes 3145736 | tf_op jit(solution)/shard_map/ppermute | solution.py:617
  190.7 36.9 %collective-permute-start.27 = (bf16[4,512,256]{2,1,0:T(8,128)(2,1)}, bf16[4,512,256]{2,1,0:T(8,128)(2,1)}, u32[]{:S(2)}, u32[]{:S(2)}) collective-permute-start(bf16[4,512,256]{2,1,0:T(8,128)(2,1)} %get-tuple-element.220), channel_id=1, source_target_pairs={{0,16},{16,0},{1,17},{17,1},{2,18},{18,2},{3,19},{19,3},{4,20},{20... | collective-permute-start | bytes 3145736 | tf_op jit(solution)/shard_map/ppermute | solution.py:35
  191.9 48.6 %collective-permute-start.50 = (bf16[4,256,512]{2,1,0:T(8,128)(2,1)}, bf16[4,256,512]{2,1,0:T(8,128)(2,1)}, u32[]{:S(2)}, u32[]{:S(2)}) collective-permute-start(bf16[4,256,512]{2,1,0:T(8,128)(2,1)} %get-tuple-element.218), channel_id=1, source_target_pairs={{0,1},{1,0},{2,3},{3,2},{4,5},{5,4},{6,7},{7,6},{8,9},{9,8},{10,11... | collective-permute-start | bytes 3145736 | tf_op jit(solution)/shard_map/ppermute | solution.py:35
  205.2 44.9 %collective-permute-start.57 = (bf16[4,512,256]{2,1,0:T(8,128)(2,1)}, bf16[4,512,256]{2,1,0:T(8,128)(2,1)}, u32[]{:S(2)}, u32[]{:S(2)}) collective-permute-start(bf16[4,512,256]{2,1,0:T(8,128)(2,1)} %get-tuple-element.216), channel_id=1, source_target_pairs={{0,16},{16,0},{1,17},{17,1},{2,18},{18,2},{3,19},{19,3},{4,20},{20... | collective-permute-start | bytes 3145736 | tf_op jit(solution)/shard_map/ppermute | solution.py:35
  208.5 65.6 %collective-permute-start.5 = (bf16[2,4,256,384]{3,2,1,0:T(8,128)(2,1)}, bf16[2,4,256,384]{3,2,1,0:T(8,128)(2,1)}, u32[]{:S(2)}, u32[]{:S(2)}) collective-permute-start(bf16[2,4,256,384]{3,2,1,0:T(8,128)(2,1)} %pad_maximum_fusion.7.refs_0_.refs_4_), channel_id=1, source_target_pairs={{0,1},{1,0},{2,3},{3,2},{4,5},{5,4},{6,7},{7,6},{8,9},{9,8},{10,11... | collective-permute-start | bytes 4718600 | tf_op jit(solution)/shard_map/ppermute | solution.py:35
  217.9 59.0 %collective-permute-start.6 = (bf16[2,4,256,384]{3,2,1,0:T(8,128)(2,1)}, bf16[2,4,256,384]{3,2,1,0:T(8,128)(2,1)}, u32[]{:S(2)}, u32[]{:S(2)}) collective-permute-start(bf16[2,4,256,384]{3,2,1,0:T(8,128)(2,1)} %pad_maximum_fusion.7.refs_0_.refs_4_), channel_id=1, source_target_pairs={{0,8},{8,0},{1,9},{9,1},{2,10},{10,2},{3,11},{11,3},{4,12},{12,4},... | collective-permute-start | bytes 4718600 | tf_op jit(solution)/shard_map/ppermute | solution.py:35
  227.6 80.2 %collective-permute-start.35 = (bf16[2,4,256,384]{3,2,1,0:T(8,128)(2,1)}, bf16[2,4,256,384]{3,2,1,0:T(8,128)(2,1)}, u32[]{:S(2)}, u32[]{:S(2)}) collective-permute-start(bf16[2,4,256,384]{3,2,1,0:T(8,128)(2,1)} %pad_maximum_fusion.8.refs_0_.refs_7_), channel_id=1, source_target_pairs={{0,1},{1,0},{2,3},{3,2},{4,5},{5,4},{6,7},{7,6},{8,9},{9,8},{10,11... | collective-permute-start | bytes 4718600 | tf_op jit(solution)/shard_map/ppermute | solution.py:35
  240.4 68.7 %collective-permute-start.21 = (bf16[2,4,256,512]{3,2,1,0:T(8,128)(2,1)}, bf16[2,4,256,512]{3,2,1,0:T(8,128)(2,1)}, u32[]{:S(2)}, u32[]{:S(2)}) collective-permute-start(bf16[2,4,256,512]{3,2,1,0:T(8,128)(2,1)} %pad_maximum_fusion.refs_0_.refs_5_), channel_id=1, source_target_pairs={{0,16},{16,0},{1,17},{17,1},{2,18},{18,2},{3,19},{19,3},{4,20},{20... | collective-permute-start | bytes 6291464 | tf_op jit(solution)/shard_map/ppermute | solution.py:35
  252.8 69.2 %collective-permute-start.22 = (bf16[2,4,256,512]{3,2,1,0:T(8,128)(2,1)}, bf16[2,4,256,512]{3,2,1,0:T(8,128)(2,1)}, u32[]{:S(2)}, u32[]{:S(2)}) collective-permute-start(bf16[2,4,256,512]{3,2,1,0:T(8,128)(2,1)} %pad_maximum_fusion.refs_0_.refs_5_), channel_id=1, source_target_pairs={{0,8},{8,0},{1,9},{9,1},{2,10},{10,2},{3,11},{11,3},{4,12},{12,4},... | collective-permute-start | bytes 6291464 | tf_op jit(solution)/shard_map/ppermute | solution.py:35
  274.1 39.9 %collective-permute-start.7 = (bf16[2,4,256,384]{3,2,1,0:T(8,128)(2,1)}, bf16[2,4,256,384]{3,2,1,0:T(8,128)(2,1)}, u32[]{:S(2)}, u32[]{:S(2)}) collective-permute-start(bf16[2,4,256,384]{3,2,1,0:T(8,128)(2,1)} %collective-permute-done.5.refs_1_.refs_5_), channel_id=1, source_target_pairs={{0,8},{8,0},{1,9},{9,1},{2,10},{10,2},{3,11},{11,3},{4,12},{12,4},... | collective-permute-start | bytes 4718600 | tf_op jit(solution)/shard_map/ppermute | solution.py:35
  276.9 72.5 %collective-permute-start.28 = (bf16[2,4,512,256]{3,2,1,0:T(8,128)(2,1)}, bf16[2,4,512,256]{3,2,1,0:T(8,128)(2,1)}, u32[]{:S(2)}, u32[]{:S(2)}) collective-permute-start(bf16[2,4,512,256]{3,2,1,0:T(8,128)(2,1)} %pad_maximum_fusion.1.refs_0_), channel_id=1, source_target_pairs={{0,1},{1,0},{2,3},{3,2},{4,5},{5,4},{6,7},{7,6},{8,9},{9,8},{10,11... | collective-permute-start | bytes 6291464 | tf_op jit(solution)/shard_map/ppermute | solution.py:35
  309.1 48.6 %collective-permute-start.29 = (bf16[2,4,512,256]{3,2,1,0:T(8,128)(2,1)}, bf16[2,4,512,256]{3,2,1,0:T(8,128)(2,1)}, u32[]{:S(2)}, u32[]{:S(2)}) collective-permute-start(bf16[2,4,512,256]{3,2,1,0:T(8,128)(2,1)} %pad_maximum_fusion.1.refs_0_), channel_id=1, source_target_pairs={{0,8},{8,0},{1,9},{9,1},{2,10},{10,2},{3,11},{11,3},{4,12},{12,4},... | collective-permute-start | bytes 6291464 | tf_op jit(solution)/shard_map/ppermute | solution.py:35
  314.0 97.3 %collective-permute-start.23 = (bf16[2,4,256,512]{3,2,1,0:T(8,128)(2,1)}, bf16[2,4,256,512]{3,2,1,0:T(8,128)(2,1)}, u32[]{:S(2)}, u32[]{:S(2)}) collective-permute-start(bf16[2,4,256,512]{3,2,1,0:T(8,128)(2,1)} %collective-permute-done.21.refs_1_.refs_6_), channel_id=1, source_target_pairs={{0,8},{8,0},{1,9},{9,1},{2,10},{10,2},{3,11},{11,3},{4,12},{12,4},... | collective-permute-start | bytes 6291464 | tf_op jit(solution)/shard_map/ppermute | solution.py:35
  321.4 53.3 %collective-permute-start.8 = (bf16[512,1024]{1,0:T(8,128)(2,1)}, bf16[512,1024]{1,0:T(8,128)(2,1)}, u32[]{:S(2)}, u32[]{:S(2)}) collective-permute-start(bf16[512,1024]{1,0:T(8,128)(2,1)} %get-tuple-element.76.refs_0_), channel_id=1, source_target_pairs={{0,8},{8,0},{1,9},{9,1},{2,10},{10,2},{3,11},{11,3},{4,12},{12,4},... | collective-permute-start | bytes 3145736 | tf_op jit(solution)/shard_map/ppermute | solution.py:35
  322.0 54.3 %collective-permute-start.9 = (bf16[512,1024]{1,0:T(8,128)(2,1)}, bf16[512,1024]{1,0:T(8,128)(2,1)}, u32[]{:S(2)}, u32[]{:S(2)}) collective-permute-start(bf16[512,1024]{1,0:T(8,128)(2,1)} %get-tuple-element.77.refs_2_), channel_id=1, source_target_pairs={{0,8},{8,0},{1,9},{9,1},{2,10},{10,2},{3,11},{11,3},{4,12},{12,4},... | collective-permute-start | bytes 3145736 | tf_op jit(solution)/shard_map/ppermute | solution.py:35
  349.4 76.7 %collective-permute-start.30 = (bf16[2,4,512,256]{3,2,1,0:T(8,128)(2,1)}, bf16[2,4,512,256]{3,2,1,0:T(8,128)(2,1)}, u32[]{:S(2)}, u32[]{:S(2)}) collective-permute-start(bf16[2,4,512,256]{3,2,1,0:T(8,128)(2,1)} %collective-permute-done.28.refs_1_), channel_id=1, source_target_pairs={{0,8},{8,0},{1,9},{9,1},{2,10},{10,2},{3,11},{11,3},{4,12},{12,4},... | collective-permute-start | bytes 6291464 | tf_op jit(solution)/shard_map/ppermute | solution.py:35
  357.7 97.6 %collective-permute-start.62 = (f32[512,1024]{1,0:T(8,128)}, f32[512,1024]{1,0:T(8,128)}, u32[]{:S(2)}, u32[]{:S(2)}) collective-permute-start(f32[512,1024]{1,0:T(8,128)} %param.17), channel_id=1, source_target_pairs={{0,0},{1,8},{8,1},{9,9},{2,2},{3,10},{10,3},{11,11},{4,4},{5,12},{... | collective-permute-start | bytes 6291464 | tf_op jit(solution)/shard_map/ppermute | solution.py:617
  374.8 78.0 %collective-permute-start.51 = (bf16[2,4,256,512]{3,2,1,0:T(8,128)(2,1)}, bf16[2,4,256,512]{3,2,1,0:T(8,128)(2,1)}, u32[]{:S(2)}, u32[]{:S(2)}) collective-permute-start(bf16[2,4,256,512]{3,2,1,0:T(8,128)(2,1)} %pad_maximum_fusion.2.refs_0_.refs_5_), channel_id=1, source_target_pairs={{0,16},{16,0},{1,17},{17,1},{2,18},{18,2},{3,19},{19,3},{4,20},{20... | collective-permute-start | bytes 6291464 | tf_op jit(solution)/shard_map/ppermute | solution.py:35
  376.3 63.4 %collective-permute-start.37 = (bf16[2,4,256,384]{3,2,1,0:T(8,128)(2,1)}, bf16[2,4,256,384]{3,2,1,0:T(8,128)(2,1)S(1)}, u32[]{:S(2)}, u32[]{:S(2)}) collective-permute-start(bf16[2,4,256,384]{3,2,1,0:T(8,128)(2,1)} %collective-permute-done.35.refs_1_.refs_8_), channel_id=1, source_target_pairs={{0,8},{8,0},{1,9},{9,1},{2,10},{10,2},{3,11},{11,3},{4,12},{12,4},... | collective-permute-start | bytes 4718600 | tf_op jit(solution)/shard_map/ppermute | solution.py:35
  411.3 50.1 %collective-permute-start.58 = (bf16[2,4,512,256]{3,2,1,0:T(8,128)(2,1)}, bf16[2,4,512,256]{3,2,1,0:T(8,128)(2,1)}, u32[]{:S(2)}, u32[]{:S(2)}) collective-permute-start(bf16[2,4,512,256]{3,2,1,0:T(8,128)(2,1)} %pad_maximum_fusion.3.refs_0_), channel_id=1, source_target_pairs={{0,1},{1,0},{2,3},{3,2},{4,5},{5,4},{6,7},{7,6},{8,9},{9,8},{10,11... | collective-permute-start | bytes 6291464 | tf_op jit(solution)/shard_map/ppermute | solution.py:35
  452.4 67.6 %collective-permute-start.52 = (bf16[2,4,256,512]{3,2,1,0:T(8,128)(2,1)}, bf16[2,4,256,512]{3,2,1,0:T(8,128)(2,1)}, u32[]{:S(2)}, u32[]{:S(2)}) collective-permute-start(bf16[2,4,256,512]{3,2,1,0:T(8,128)(2,1)} %pad_maximum_fusion.2.refs_0_.refs_5_), channel_id=1, source_target_pairs={{0,8},{8,0},{1,9},{9,1},{2,10},{10,2},{3,11},{11,3},{4,12},{12,4},... | collective-permute-start | bytes 6291464 | tf_op jit(solution)/shard_map/ppermute | solution.py:35
  452.8 67.6 %collective-permute-start.53 = (bf16[2,4,256,512]{3,2,1,0:T(8,128)(2,1)}, bf16[2,4,256,512]{3,2,1,0:T(8,128)(2,1)}, u32[]{:S(2)}, u32[]{:S(2)}) collective-permute-start(bf16[2,4,256,512]{3,2,1,0:T(8,128)(2,1)} %collective-permute-done.51.refs_1_.refs_6_), channel_id=1, source_target_pairs={{0,8},{8,0},{1,9},{9,1},{2,10},{10,2},{3,11},{11,3},{4,12},{12,4},... | collective-permute-start | bytes 6291464 | tf_op jit(solution)/shard_map/ppermute | solution.py:35
  461.4 71.3 %collective-permute-start.59 = (bf16[2,4,512,256]{3,2,1,0:T(8,128)(2,1)}, bf16[2,4,512,256]{3,2,1,0:T(8,128)(2,1)}, u32[]{:S(2)}, u32[]{:S(2)}) collective-permute-start(bf16[2,4,512,256]{3,2,1,0:T(8,128)(2,1)} %pad_maximum_fusion.3.refs_0_), channel_id=1, source_target_pairs={{0,8},{8,0},{1,9},{9,1},{2,10},{10,2},{3,11},{11,3},{4,12},{12,4},... | collective-permute-start | bytes 6291464 | tf_op jit(solution)/shard_map/ppermute | solution.py:35
  461.6 71.1 %collective-permute-start.60 = (bf16[2,4,512,256]{3,2,1,0:T(8,128)(2,1)}, bf16[2,4,512,256]{3,2,1,0:T(8,128)(2,1)}, u32[]{:S(2)}, u32[]{:S(2)}) collective-permute-start(bf16[2,4,512,256]{3,2,1,0:T(8,128)(2,1)} %collective-permute-done.58.refs_1_), channel_id=1, source_target_pairs={{0,8},{8,0},{1,9},{9,1},{2,10},{10,2},{3,11},{11,3},{4,12},{12,4},... | collective-permute-start | bytes 6291464 | tf_op jit(solution)/shard_map/ppermute | solution.py:35
  507.2 263.1 %collective-permute-start.87 = (bf16[512,1024]{1,0:T(8,128)(2,1)}, bf16[512,1024]{1,0:T(8,128)(2,1)}, u32[]{:S(2)}, u32[]{:S(2)}) collective-permute-start(bf16[512,1024]{1,0:T(8,128)(2,1)} %attend.2.left_ref.refs_0_), channel_id=1, source_target_pairs={{0,8},{8,0},{1,9},{9,1},{2,10},{10,2},{3,11},{11,3},{4,12},{12,4},... | collective-permute-start | bytes 3145736 | tf_op jit(solution)/shard_map/ppermute | solution.py:35
  519.9 222.2 %collective-permute-start.94 = (bf16[512,1024]{1,0:T(8,128)(2,1)}, bf16[512,1024]{1,0:T(8,128)(2,1)}, u32[]{:S(2)}, u32[]{:S(2)}) collective-permute-start(bf16[512,1024]{1,0:T(8,128)(2,1)} %attend.3.left_ref.refs_0_), channel_id=1, source_target_pairs={{0,8},{8,0},{1,9},{9,1},{2,10},{10,2},{3,11},{11,3},{4,12},{12,4},... | collective-permute-start | bytes 3145736 | tf_op jit(solution)/shard_map/ppermute | solution.py:35
  633.6 108.5 %collective-permute-start.93 = (bf16[512,512]{1,0:T(8,128)(2,1)}, bf16[512,512]{1,0:T(8,128)(2,1)}, u32[]{:S(2)}, u32[]{:S(2)}) collective-permute-start(bf16[512,512]{1,0:T(8,128)(2,1)} %bitcast.237), channel_id=1, source_target_pairs={{0,8},{8,0},{1,9},{9,1},{2,10},{10,2},{3,11},{11,3},{4,12},{12,4},... | collective-permute-start | bytes 1572872 | tf_op jit(solution)/shard_map/ppermute | solution.py:35
  734.4 49.8 %collective-permute-start.65 = (bf16[512,1024]{1,0:T(8,128)(2,1)}, bf16[512,1024]{1,0:T(8,128)(2,1)}, u32[]{:S(2)}, u32[]{:S(2)}) collective-permute-start(bf16[512,1024]{1,0:T(8,128)(2,1)} %get-tuple-element.111), channel_id=1, source_target_pairs={{0,8},{8,0},{1,9},{9,1},{2,10},{10,2},{3,11},{11,3},{4,12},{12,4},... | collective-permute-start | bytes 3145736 | tf_op jit(solution)/shard_map/ppermute | solution.py:40
  734.8 46.0 %collective-permute-start.66 = (bf16[512,1024]{1,0:T(8,128)(2,1)}, bf16[512,1024]{1,0:T(8,128)(2,1)}, u32[]{:S(2)}, u32[]{:S(2)}) collective-permute-start(bf16[512,1024]{1,0:T(8,128)(2,1)} %get-tuple-element.113), channel_id=1, source_target_pairs={{0,8},{8,0},{1,9},{9,1},{2,10},{10,2},{3,11},{11,3},{4,12},{12,4},... | collective-permute-start | bytes 3145736 | tf_op jit(solution)/shard_map/ppermute | solution.py:40
  780.1 33.3 %collective-permute-start.77 = (bf16[512,512]{1,0:T(8,128)(2,1)S(1)}, bf16[512,512]{1,0:T(8,128)(2,1)S(1)}, u32[]{:S(2)}, u32[]{:S(2)}) collective-permute-start(bf16[512,512]{1,0:T(8,128)(2,1)S(1)} %bitcast.379), channel_id=1, source_target_pairs={{0,8},{8,0},{1,9},{9,1},{2,10},{10,2},{3,11},{11,3},{4,12},{12,4},... | collective-permute-start | bytes 1572872 | tf_op jit(solution)/shard_map/ppermute | solution.py:35
  780.7 33.6 %collective-permute-start.79 = (bf16[512,1024]{1,0:T(8,128)(2,1)S(1)}, bf16[512,1024]{1,0:T(8,128)(2,1)}, u32[]{:S(2)}, u32[]{:S(2)}) collective-permute-start(bf16[512,1024]{1,0:T(8,128)(2,1)S(1)} %copy-done.57), channel_id=1, source_target_pairs={{0,8},{8,0},{1,9},{9,1},{2,10},{10,2},{3,11},{11,3},{4,12},{12,4},... | collective-permute-start | bytes 3145736 | tf_op jit(solution)/shard_map/ppermute | solution.py:35
  780.9 33.6 %collective-permute-start.80 = (bf16[512,1024]{1,0:T(8,128)(2,1)S(1)}, bf16[512,1024]{1,0:T(8,128)(2,1)}, u32[]{:S(2)}, u32[]{:S(2)}) collective-permute-start(bf16[512,1024]{1,0:T(8,128)(2,1)S(1)} %copy-done.58), channel_id=1, source_target_pairs={{0,8},{8,0},{1,9},{9,1},{2,10},{10,2},{3,11},{11,3},{4,12},{12,4},... | collective-permute-start | bytes 3145736 | tf_op jit(solution)/shard_map/ppermute | solution.py:35
  784.1 56.2 %collective-permute-start.61 = (f32[512,1024]{1,0:T(8,128)}, f32[512,1024]{1,0:T(8,128)}, u32[]{:S(2)}, u32[]{:S(2)}) collective-permute-start(f32[512,1024]{1,0:T(8,128)} %pad_maximum_fusion.4), channel_id=1, source_target_pairs={{0,0},{1,8},{8,1},{9,9},{2,2},{3,10},{10,3},{11,11},{4,4},{5,12},{... | collective-permute-start | bytes 6291464 | tf_op jit(solution)/shard_map/ppermute | solution.py:617
  814.3 177.8 %collective-permute-start.115 = (bf16[512,4096]{1,0:T(8,128)(2,1)}, bf16[512,4096]{1,0:T(8,128)(2,1)}, u32[]{:S(2)}, u32[]{:S(2)}) collective-permute-start(bf16[512,4096]{1,0:T(8,128)(2,1)} %get-tuple-element.79.left_ref.refs_0_), channel_id=1, source_target_pairs={{0,8},{8,0},{1,9},{9,1},{2,10},{10,2},{3,11},{11,3},{4,12},{12,4},... | collective-permute-start | bytes 12582920 | tf_op jit(solution)/shard_map/ppermute | solution.py:35
  836.8 191.7 %collective-permute-start.108 = (bf16[512,4096]{1,0:T(8,128)(2,1)}, bf16[512,4096]{1,0:T(8,128)(2,1)}, u32[]{:S(2)}, u32[]{:S(2)}) collective-permute-start(bf16[512,4096]{1,0:T(8,128)(2,1)} %get-tuple-element.93.refs_0_), channel_id=1, source_target_pairs={{0,8},{8,0},{1,9},{9,1},{2,10},{10,2},{3,11},{11,3},{4,12},{12,4},... | collective-permute-start | bytes 12582920 | tf_op jit(solution)/shard_map/ppermute | solution.py:35
  838.4 200.0 %collective-permute-start.122 = (bf16[512,4096]{1,0:T(8,128)(2,1)}, bf16[512,4096]{1,0:T(8,128)(2,1)}, u32[]{:S(2)}, u32[]{:S(2)}) collective-permute-start(bf16[512,4096]{1,0:T(8,128)(2,1)} %get-tuple-element.87.left_ref.refs_0_), channel_id=1, source_target_pairs={{0,8},{8,0},{1,9},{9,1},{2,10},{10,2},{3,11},{11,3},{4,12},{12,4},... | collective-permute-start | bytes 12582920 | tf_op jit(solution)/shard_map/ppermute | solution.py:35
  848.7 114.3 %collective-permute-start.70 = (bf16[512,1024]{1,0:T(8,128)(2,1)}, bf16[512,1024]{1,0:T(8,128)(2,1)}, u32[]{:S(2)}, u32[]{:S(2)}) collective-permute-start(bf16[512,1024]{1,0:T(8,128)(2,1)} %add_convert_fusion.7.refs_1_), channel_id=1, source_target_pairs={{0,8},{8,0},{1,9},{9,1},{2,10},{10,2},{3,11},{11,3},{4,12},{12,4},... | collective-permute-start | bytes 3145736 | tf_op jit(solution)/shard_map/ppermute | solution.py:35
  850.0 131.0 %collective-permute-start.71 = (bf16[512,1024]{1,0:T(8,128)(2,1)}, bf16[512,1024]{1,0:T(8,128)(2,1)}, u32[]{:S(2)}, u32[]{:S(2)}) collective-permute-start(bf16[512,1024]{1,0:T(8,128)(2,1)} %get-tuple-element.185.refs_2_), channel_id=1, source_target_pairs={{0,8},{8,0},{1,9},{9,1},{2,10},{10,2},{3,11},{11,3},{4,12},{12,4},... | collective-permute-start | bytes 3145736 | tf_op jit(solution)/shard_map/ppermute | solution.py:35
  963.0 63.4 %collective-permute-start.67 = (f32[512,1024]{1,0:T(8,128)}, f32[512,1024]{1,0:T(8,128)}, u32[]{:S(2)}, u32[]{:S(2)}) collective-permute-start(f32[512,1024]{1,0:T(8,128)} %pad_maximum_fusion.6), channel_id=1, source_target_pairs={{0,0},{1,8},{8,1},{9,9},{2,2},{3,10},{10,3},{11,11},{4,4},{5,12},{... | collective-permute-start | bytes 6291464 | tf_op jit(solution)/shard_map/ppermute | solution.py:617
  980.9 43.5 %collective-permute-start.81 = (bf16[2,4,256,384]{3,2,1,0:T(8,128)(2,1)}, bf16[2,4,256,384]{3,2,1,0:T(8,128)(2,1)}, u32[]{:S(2)}, u32[]{:S(2)}) collective-permute-start(bf16[2,4,256,384]{3,2,1,0:T(8,128)(2,1)} %get-tuple-element.118), channel_id=1, source_target_pairs={{0,1},{1,0},{2,3},{3,2},{4,5},{5,4},{6,7},{7,6},{8,9},{9,8},{10,11... | collective-permute-start | bytes 4718600 | tf_op jit(solution)/shard_map/ppermute | solution.py:40
  992.1 136.4 %collective-permute-start.101 = (bf16[512,4096]{1,0:T(8,128)(2,1)}, bf16[512,4096]{1,0:T(8,128)(2,1)}, u32[]{:S(2)}, u32[]{:S(2)}) collective-permute-start(bf16[512,4096]{1,0:T(8,128)(2,1)} %get-tuple-element.105.refs_0_), channel_id=1, source_target_pairs={{0,8},{8,0},{1,9},{9,1},{2,10},{10,2},{3,11},{11,3},{4,12},{12,4},... | collective-permute-start | bytes 12582920 | tf_op jit(solution)/shard_map/ppermute | solution.py:35
  1024.4 37.6 %collective-permute-start.72 = (bf16[2,4,256,384]{3,2,1,0:T(8,128)(2,1)}, bf16[2,4,256,384]{3,2,1,0:T(8,128)(2,1)}, u32[]{:S(2)}, u32[]{:S(2)}) collective-permute-start(bf16[2,4,256,384]{3,2,1,0:T(8,128)(2,1)} %get-tuple-element.116), channel_id=1, source_target_pairs={{0,1},{1,0},{2,3},{3,2},{4,5},{5,4},{6,7},{7,6},{8,9},{9,8},{10,11... | collective-permute-start | bytes 4718600 | tf_op jit(solution)/shard_map/ppermute | solution.py:40
  1026.4 80.5 %collective-permute-start.116 = (bf16[2,4,256,512]{3,2,1,0:T(8,128)(2,1)}, bf16[2,4,256,512]{3,2,1,0:T(8,128)(2,1)S(1)}, u32[]{:S(2)}, u32[]{:S(2)}) collective-permute-start(bf16[2,4,256,512]{3,2,1,0:T(8,128)(2,1)} %get-tuple-element.133), channel_id=1, source_target_pairs={{0,1},{1,0},{2,3},{3,2},{4,5},{5,4},{6,7},{7,6},{8,9},{9,8},{10,11... | collective-permute-start | bytes 6291464 | tf_op jit(solution)/shard_map/ppermute | solution.py:40
  1038.3 75.5 %collective-permute-start.100 = (bf16[512,512]{1,0:T(8,128)(2,1)S(1)}, bf16[512,512]{1,0:T(8,128)(2,1)S(1)}, u32[]{:S(2)}, u32[]{:S(2)}) collective-permute-start(bf16[512,512]{1,0:T(8,128)(2,1)S(1)} %bitcast.377), channel_id=1, source_target_pairs={{0,8},{8,0},{1,9},{9,1},{2,10},{10,2},{3,11},{11,3},{4,12},{12,4},... | collective-permute-start | bytes 1572872 | tf_op jit(solution)/shard_map/ppermute | solution.py:35
  1047.2 114.4 %collective-permute-start.123 = (bf16[2,4,256,512]{3,2,1,0:T(8,128)(2,1)}, bf16[2,4,256,512]{3,2,1,0:T(8,128)(2,1)}, u32[]{:S(2)}, u32[]{:S(2)}) collective-permute-start(bf16[2,4,256,512]{3,2,1,0:T(8,128)(2,1)} %get-tuple-element.135), channel_id=1, source_target_pairs={{0,1},{1,0},{2,3},{3,2},{4,5},{5,4},{6,7},{7,6},{8,9},{9,8},{10,11... | collective-permute-start | bytes 6291464 | tf_op jit(solution)/shard_map/ppermute | solution.py:40
  1064.0 48.2 %collective-permute-start.73 = (bf16[4,256,384]{2,1,0:T(8,128)(2,1)S(1)}, bf16[4,256,384]{2,1,0:T(8,128)(2,1)S(1)}, u32[]{:S(2)}, u32[]{:S(2)}) collective-permute-start(bf16[4,256,384]{2,1,0:T(8,128)(2,1)S(1)} %slice_bitcast_fusion.10), channel_id=1, source_target_pairs={{0,16},{16,0},{1,17},{17,1},{2,18},{18,2},{3,19},{19,3},{4,20},{20... | collective-permute-start | bytes 2359304 | tf_op jit(solution)/shard_map/ppermute | solution.py:40
  1123.5 64.5 %collective-permute-start.109 = (bf16[2,4,256,512]{3,2,1,0:T(8,128)(2,1)}, bf16[2,4,256,512]{3,2,1,0:T(8,128)(2,1)}, u32[]{:S(2)}, u32[]{:S(2)}) collective-permute-start(bf16[2,4,256,512]{3,2,1,0:T(8,128)(2,1)} %get-tuple-element.131), channel_id=1, source_target_pairs={{0,16},{16,0},{1,17},{17,1},{2,18},{18,2},{3,19},{19,3},{4,20},{20... | collective-permute-start | bytes 6291464 | tf_op jit(solution)/shard_map/ppermute | solution.py:40
  1146.3 86.6 %collective-permute-start.102 = (bf16[2,4,256,512]{3,2,1,0:T(8,128)(2,1)}, bf16[2,4,256,512]{3,2,1,0:T(8,128)(2,1)}, u32[]{:S(2)}, u32[]{:S(2)}) collective-permute-start(bf16[2,4,256,512]{3,2,1,0:T(8,128)(2,1)} %get-tuple-element.129), channel_id=1, source_target_pairs={{0,16},{16,0},{1,17},{17,1},{2,18},{18,2},{3,19},{19,3},{4,20},{20... | collective-permute-start | bytes 6291464 | tf_op jit(solution)/shard_map/ppermute | solution.py:40
  1152.1 38.3 %collective-permute-start.120 = (bf16[256,512]{1,0:T(8,128)(2,1)S(1)}, bf16[256,512]{1,0:T(8,128)(2,1)S(1)}, u32[]{:S(2)}, u32[]{:S(2)}) collective-permute-start(bf16[256,512]{1,0:T(8,128)(2,1)S(1)} %get-tuple-element.204), channel_id=1, source_target_pairs={{0,2},{2,4},{4,6},{6,0},{1,3},{3,5},{5,7},{7,1},{8,10},{10,12},{12... | collective-permute-start | bytes 786440 | tf_op jit(solution)/shard_map/ppermute | solution.py:40
  1188.0 62.1 %collective-permute-start.124 = (bf16[4,256,512]{2,1,0:T(8,128)(2,1)S(1)}, bf16[4,256,512]{2,1,0:T(8,128)(2,1)S(1)}, u32[]{:S(2)}, u32[]{:S(2)}) collective-permute-start(bf16[4,256,512]{2,1,0:T(8,128)(2,1)S(1)} %slice_bitcast_fusion), channel_id=1, source_target_pairs={{0,16},{16,0},{1,17},{17,1},{2,18},{18,2},{3,19},{19,3},{4,20},{20... | collective-permute-start | bytes 3145736 | tf_op jit(solution)/shard_map/ppermute | solution.py:40
  1190.4 64.0 %collective-permute-start.110 = (bf16[4,256,512]{2,1,0:T(8,128)(2,1)S(1)}, bf16[4,256,512]{2,1,0:T(8,128)(2,1)S(1)}, u32[]{:S(2)}, u32[]{:S(2)}) collective-permute-start(bf16[4,256,512]{2,1,0:T(8,128)(2,1)S(1)} %slice_bitcast_fusion.4), channel_id=1, source_target_pairs={{0,1},{1,0},{2,3},{3,2},{4,5},{5,4},{6,7},{7,6},{8,9},{9,8},{10,11... | collective-permute-start | bytes 3145736 | tf_op jit(solution)/shard_map/ppermute | solution.py:40
  1236.2 51.8 %collective-permute-start.103 = (bf16[4,256,512]{2,1,0:T(8,128)(2,1)}, bf16[4,256,512]{2,1,0:T(8,128)(2,1)}, u32[]{:S(2)}, u32[]{:S(2)}) collective-permute-start(bf16[4,256,512]{2,1,0:T(8,128)(2,1)} %slice_bitcast_fusion.6), channel_id=1, source_target_pairs={{0,1},{1,0},{2,3},{3,2},{4,5},{5,4},{6,7},{7,6},{8,9},{9,8},{10,11... | collective-permute-start | bytes 3145736 | tf_op jit(solution)/shard_map/ppermute | solution.py:40
  1255.5 37.2 %collective-permute-start.113 = (bf16[256,512]{1,0:T(8,128)(2,1)}, bf16[256,512]{1,0:T(8,128)(2,1)S(1)}, u32[]{:S(2)}, u32[]{:S(2)}) collective-permute-start(bf16[256,512]{1,0:T(8,128)(2,1)} %get-tuple-element.213), channel_id=1, source_target_pairs={{0,2},{2,4},{4,6},{6,0},{1,3},{3,5},{5,7},{7,1},{8,10},{10,12},{12... | collective-permute-start | bytes 786440 | tf_op jit(solution)/shard_map/ppermute | solution.py:40
  1261.6 33.5 %collective-permute-start.112 = (bf16[256,512]{1,0:T(8,128)(2,1)}, bf16[256,512]{1,0:T(8,128)(2,1)}, u32[]{:S(2)}, u32[]{:S(2)}) collective-permute-start(bf16[256,512]{1,0:T(8,128)(2,1)} %get-tuple-element.214), channel_id=1, source_target_pairs={{0,4},{2,6},{4,0},{6,2},{1,5},{3,7},{5,1},{7,3},{8,12},{10,14},{12... | collective-permute-start | bytes 786440 | tf_op jit(solution)/shard_map/ppermute | solution.py:40
  (224 other events, 4263.3 us)
Sparse Core Ops, SparseCore 0:
  840.5 120.8 all-reduce.2

commit v2 on v0

v2 whole, which is shorter than its diff:
```python
import functools
import math

import jax
import jax.numpy as jnp
from jax import lax
from jax.experimental import pallas as pl
from jax.experimental.pallas import tpu as pltpu
from jax.sharding import Mesh, PartitionSpec as P

HEADS = 16
HEAD_DIM = 64
LAYERS = 2
DEPTH = 4

EPSILON = 1e-12
NEGATIVE = -1e30
SQRT_HALF = 0.7071067811865476
ROOT_TWO_PI_INV = 0.3989422804014327
FACTOR = 1.0 / math.sqrt(HEAD_DIM)
VMEM = 52 * 1024 * 1024
F32 = jnp.float32
BF16 = jnp.bfloat16
NT = (((1,), (1,)), ((), ()))
NN = (((1,), (0,)), ((), ()))
ANY_AXES = ("y", "core", "z", "x")


def dot(left, right, dims=NN):
    return lax.dot_general(left, right, dims, preferred_element_type=F32)


def pull(value, axis, step):
    size = lax.axis_size(axis)
    return lax.ppermute(value, axis, [(i, (i + step) % size) for i in range(size)])


def push(value, axis, step):
    size = lax.axis_size(axis)
    return lax.ppermute(value, axis, [(i, (i - step) % size) for i in range(size)])


def spread(value, axis):
    return [value] + [pull(value, axis, s) for s in range(1, lax.axis_size(axis))]


class Gather:
    def __init__(self, block, order):
        self.order = order
        self.stage = 0
        self.parts = spread(block, "z")

    def advance(self):
        self.stage += 1
        if self.stage <= 2:
            value = jnp.stack(self.parts)
            self.parts = spread(value, self.order[self.stage - 1])
            return [value]
        if self.stage == 3:
            own = self.parts
            self.parts = own + [pull(piece, "core", 1) for piece in own]
            return own[1:]
        return []

    def pieces(self):
        while self.stage < 4:
            self.advance()
        return self.parts


class Scatter:
    def __init__(self, pieces, order):
        self.axes = (order[1], order[0], "z")
        self.stage = 0
        self.own = pieces[0]
        self.parts = send(pieces, self.axes[0])

    def advance(self):
        total = functools.reduce(jnp.add, [p.astype(F32) for p in [self.own] + self.parts])
        self.stage += 1
        if self.stage == 3:
            self.result = total
            return [total]
        total = total.astype(BF16)
        pieces = [total[s] for s in range(total.shape[0])]
        self.own = pieces[0]
        self.parts = send(pieces, self.axes[self.stage])
        return [total]

    def finish(self):
        while self.stage < 3:
            self.advance()
        return self.result


def send(pieces, axis):
    return [push(pieces[s], axis, s) for s in range(1, lax.axis_size(axis))]


def add_over(value, axes):
    for axis in axes:
        value = functools.reduce(jnp.add, spread(value, axis))
    return value


def relative_blocks(value, axes):
    sizes = [lax.axis_size(axis) for axis in axes]
    count = math.prod(sizes)
    width = value.shape[-1] // count
    parts = []
    for place in range(count):
        low = place % sizes[1]
        high = place // sizes[1]
        source = ((lax.axis_index(axes[0]) - high) % sizes[0]) * sizes[1] + (
            lax.axis_index(axes[1]) - low
        ) % sizes[1]
        parts.append(lax.dynamic_slice_in_dim(value, source * width, width, value.ndim - 1))
    return jnp.concatenate(parts, axis=-1)


def tile(refs, order, core, y, x):
    half = len(refs) // 2
    if order[1] == "x":
        return refs[core * half + x][y, 0]
    return refs[core * half + y][x, 0]


def slab(refs, order, ys, xs, span):
    return jnp.concatenate(
        [
            jnp.concatenate(
                [tile(refs, order, core, y, x)[:, span[0] : span[1]] for x in range(xs)], axis=1
            )
            for y in range(ys)
            for core in range(2)
        ],
        axis=0,
    )


def weight_specs(weights):
    return [
        pl.BlockSpec((w.shape[0], 1, w.shape[2], w.shape[3]), lambda z: (0, z, 0, 0))
        for w in weights
    ]


def whole(value):
    return pl.BlockSpec(value.shape, lambda z: (0,) * len(value.shape))


def by_z(rows, columns):
    return pl.BlockSpec((rows, columns // DEPTH), lambda z: (0, z))


ORDERS = (
    (("y", "x"), ("x", "y"), ("y", "x")),
    (("x", "y"), ("y", "x"), ("x", "y")),
)
COST = 1000


def forward_waits(a0, e0, s0, a1, e1, s1):
    return (
        {
            "queries": (e0, s0),
            "attend": (s0,),
            "norm": (e0, a1),
            "hidden": (s0, e1),
            "norm_two": (a1, s1),
        },
        {"queries": (e1,), "attend": (s1,), "norm": (e1,), "hidden": (s1,), "norm_two": ()},
    )


def call(kernel, name, ins, outs, scratch=(), tokens=()):
    skip = len(tokens)

    def body(*refs):
        kernel(*refs[skip:])

    return list(pl.pallas_call(
        body,
        grid=(DEPTH,),
        in_specs=[pl.BlockSpec(memory_space=pl.ANY)] * skip + [spec for _, spec in ins],
        out_specs=[spec for _, spec in outs],
        out_shape=[shape for shape, _ in outs],
        scratch_shapes=list(scratch),
        compiler_params=pltpu.CompilerParams(
            vmem_limit_bytes=VMEM, dimension_semantics=("arbitrary",)
        ),
        cost_estimate=pl.CostEstimate(flops=COST, bytes_accessed=COST, transcendentals=0),
        name=name,
    )(*tokens, *[array for array, _ in ins]))


def shape(rows, columns, dtype=BF16):
    return jax.ShapeDtypeStruct((rows, columns), dtype)


def kept(array):
    return (array, whole(array))


def split(array):
    return (array, by_z(*array.shape))


def weighted(weights):
    return list(zip(weights, weight_specs(weights), strict=True))


def queries(value, weights, order, bias, ys, xs, tokens):
    rows, columns = (value.shape[0], bias.shape[1])
    wide = columns // (DEPTH * xs)

    def kernel(x_ref, bias_ref, *refs):
        q_ref, k_ref, v_ref = refs[-3:]
        mixed = dot(x_ref[...], slab(refs[:-3], order, ys, xs, (0, 3 * wide)))
        for x in range(xs):
            here = slice(x * wide, (x + 1) * wide)
            start = x * 3 * wide
            q_ref[:, here] = (mixed[:, start : start + wide] + bias_ref[0:1, here]).astype(BF16)
            k_ref[:, here] = mixed[:, start + wide : start + 2 * wide].astype(BF16)
            v_ref[:, here] = (
                mixed[:, start + 2 * wide : start + 3 * wide] + bias_ref[1:2, here]
            ).astype(BF16)

    return call(
        kernel,
        "queries",
        [kept(value), split(bias), *weighted(weights)],
        [split(shape(rows, columns))] * 3,
        tokens=tokens,
    )


def hidden(value, weights, order, bias, ys, xs, tokens):
    rows, columns = (value.shape[0], bias.shape[1])
    wide = columns // DEPTH
    step = min(64, rows)

    def kernel(x_ref, bias_ref, *refs):
        active_ref, slope_ref, inner_ref = refs[-3:]
        inner_ref[...] = dot(x_ref[...], slab(refs[:-3], order, ys, xs, (0, wide // xs)))

        def part(i, carry):
            at = pl.ds(pl.multiple_of(i * step, step), step)
            inner = inner_ref[at, :] + bias_ref[0:1, :]
            phi = 0.5 * (1.0 + lax.erf(inner * SQRT_HALF))
            active_ref[at, :] = (inner * phi).astype(BF16)
            slope_ref[at, :] = (
                phi + inner * jnp.exp(-0.5 * inner * inner) * ROOT_TWO_PI_INV
            ).astype(BF16)
            return carry

        lax.fori_loop(0, rows // step, part, 0)

    return call(
        kernel,
        "hidden",
        [kept(value), split(bias), *weighted(weights)],
        [split(shape(rows, columns))] * 2,
        [pltpu.VMEM((rows, wide), F32)],
        tokens,
    )


def hidden_back(grad, weights, order, slope, ys, xs, tokens):
    rows, columns = slope.shape
    wide = columns // DEPTH
    step = min(64, rows)

    def kernel(g_ref, slope_ref, *refs):
        grad_ref, sums_ref, back_ref = refs[-3:]
        back_ref[...] = dot(g_ref[...], slab(refs[:-3], order, ys, xs, (0, wide // xs)))
        sums_ref[...] = jnp.zeros_like(sums_ref)

        def part(i, carry):
            at = pl.ds(pl.multiple_of(i * step, step), step)
            value = (back_ref[at, :] * slope_ref[at, :].astype(F32)).astype(BF16)
            grad_ref[at, :] = value
            sums_ref[0:1, :] += jnp.sum(value.astype(F32), axis=0, keepdims=True)
            return carry

        lax.fori_loop(0, rows // step, part, 0)

    return call(
        kernel,
        "hidden_back",
        [kept(grad), split(slope), *weighted(weights)],
        [split(shape(rows, columns)), split(shape(8, columns, F32))],
        [pltpu.VMEM((rows, wide), F32)],
        tokens,
    )


def context_back(grad, weights, order, ys, xs, tokens):
    rows = grad.shape[0]
    wide = HEADS * HEAD_DIM // (DEPTH * xs)

    def kernel(g_ref, *refs):
        value = dot(g_ref[...], slab(refs[:-1], order, ys, xs, (3 * wide, 4 * wide)))
        refs[-1][...] = value.astype(BF16)

    return call(
        kernel,
        "context_back",
        [kept(grad), *weighted(weights)],
        [split(shape(rows, HEADS * HEAD_DIM))],
        tokens=tokens,
    )[0]


def gathered(total, product):
    z = pl.program_id(0)

    @pl.when(z == 0)
    def _():
        total[...] = product

    @pl.when(z > 0)
    def _():
        total[...] += product


def other_half(value, half_ref, at, ys):
    deep = value.shape[1] // (2 * ys)
    for y in range(ys):
        half_ref[at, y * deep : (y + 1) * deep] = value[:, (2 * y + 1) * deep : (2 * y + 2) * deep]


def norm(left, weights, order, span, base, vectors, scaled, last, ys, xs, tokens):
    rows, width = base.shape
    step = min(64, rows)

    def kernel(left_ref, base_ref, vec_ref, *refs):
        outs = 5 if last else 4
        results, total = (refs[-outs - 1 : -1], refs[-1])
        gathered(
            total, dot(left_ref[...], slab(refs[: -outs - 1], order, ys, xs, span), NT)
        )

        @pl.when(pl.program_id(0) == DEPTH - 1)
        def _():
            def part(i, carry):
                at = pl.ds(pl.multiple_of(i * step, step), step)
                base_here = base_ref[at, :].astype(F32)
                if scaled:
                    base_here = base_here * vec_ref[0:1, :] + vec_ref[1:2, :]
                summed = base_here + (total[at, :] + vec_ref[2:3, :])
                offset = summed - jnp.mean(summed, axis=1, keepdims=True)
                inverse = lax.rsqrt(jnp.mean(offset * offset, axis=1, keepdims=True) + EPSILON)
                normal = offset * inverse
                results[0][at, :] = normal
                results[1][at, :] = jnp.broadcast_to(inverse, (step, 128))
                value = normal * vec_ref[3:4, :] + vec_ref[4:5, :]
                low = value.astype(BF16)
                results[2][at, :] = low
                other_half(low, results[3], at, ys)
                if last:
                    results[4][at, :] = value
                return carry

            lax.fori_loop(0, rows // step, part, 0)

    outs = [
        shape(rows, width, F32),
        shape(rows, 128, F32),
        shape(rows, width),
        shape(rows, width // 2),
    ] + ([shape(rows, width, F32)] if last else [])
    return call(
        kernel,
        "norm",
        [split(left), kept(base), kept(vectors), *weighted(weights)],
        [kept(o) for o in outs],
        [pltpu.VMEM((rows, width), F32)],
        tokens,
    )


def norm_back(lefts, weights, order, span, base, saved, ys, xs, tokens):
    rows, width = base.shape
    step = min(64, rows)
    last = saved is None
    outs = [shape(rows, width, F32)]
    if not last:
        outs += [shape(rows, width), shape(rows, width // 2), shape(8, width, F32)]

    def kernel(*refs):
        left_refs, refs = (refs[: len(lefts)], refs[len(lefts) :])
        base_ref, refs = (refs[0], refs[1:])
        if not last:
            (normal_ref, inverse_ref, gain_ref), refs = (refs[:3], refs[3:])
        results, total = (refs[-len(outs) - 1 : -1], refs[-1])
        if lefts:
            wide = left_refs[0].shape[1] // xs
            left = jnp.concatenate(
                [ref[:, x * wide : (x + 1) * wide] for x in range(xs) for ref in left_refs],
                axis=1,
            )
            tiles = refs[: -len(outs) - 1]
            gathered(total, dot(left, slab(tiles, order, ys, xs, span), NT))

        @pl.when(pl.program_id(0) == DEPTH - 1)
        def _():
            if last:
                results[0][...] = base_ref[...] + total[...]
                return
            results[3][...] = jnp.zeros_like(results[3])

            def part(i, carry):
                at = pl.ds(pl.multiple_of(i * step, step), step)
                upstream = base_ref[at, :]
                if lefts:
                    upstream = upstream + total[at, :]
                normal = normal_ref[at, :]
                scaled = upstream * gain_ref[0:1, :]
                first_mean = jnp.mean(scaled, axis=1, keepdims=True)
                second_mean = jnp.mean(scaled * normal, axis=1, keepdims=True)
                grad = inverse_ref[at, 0:1] * (scaled - first_mean - normal * second_mean)
                low = grad.astype(BF16)
                results[0][at, :] = grad
                results[1][at, :] = low
                other_half(low, results[2], at, ys)
                results[3][0:1, :] += jnp.sum(upstream, axis=0, keepdims=True)
                results[3][1:2, :] += jnp.sum(upstream * normal, axis=0, keepdims=True)
                results[3][2:3, :] += jnp.sum(low.astype(F32), axis=0, keepdims=True)
                return carry

            lax.fori_loop(0, rows // step, part, 0)

    fixed = [base] + ([] if last else list(saved))
    return call(
        kernel,
        "norm_back",
        [split(v) for v in lefts] + [kept(v) for v in fixed] + weighted(weights),
        [kept(o) for o in outs],
        [pltpu.VMEM((rows, width), F32)],
        tokens,
    )


def outer(groups, order, ys, xs, tokens=()):
    rows, width = groups[0][0].shape
    deep = width // (2 * ys)
    widths = [sum(r.shape[1] for r in mine) // (DEPTH * xs) for _, _, mine, _ in groups]
    first, second = (xs, ys) if order[1] == "x" else (ys, xs)
    counts = [2 + 2 * len(mine) for _, _, mine, _ in groups]

    def kernel(*refs):
        inputs, refs = (refs[: sum(counts)], refs[sum(counts) :])
        outs, turned = (refs[:first], refs[first:])
        column = 0
        for g, (_, _, group, _) in enumerate(groups):
            rights = len(group)
            left_ref, other_ref = inputs[:2]
            mine, theirs = (inputs[2 : 2 + rights], inputs[2 + rights : 2 + 2 * rights])
            inputs = inputs[counts[g] :]
            both = turned[g]

            @pl.when(pl.program_id(0) == 0)
            def _(left_ref=left_ref, other_ref=other_ref, both=both):
                for y in range(ys):
                    here = slice(y * deep, (y + 1) * deep)
                    both[here, :rows] = left_ref[:, 2 * y * deep : (2 * y + 1) * deep].T
                    both[here, rows:] = other_ref[:, here].T

            wide = mine[0].shape[1] // xs
            for x in range(xs):
                here = slice(x * wide, (x + 1) * wide)
                right = jnp.concatenate(
                    [
                        jnp.concatenate([ref[:, here] for ref in mine], axis=1),
                        jnp.concatenate([ref[:, here] for ref in theirs], axis=1),
                    ],
                    axis=0,
                )
                product = dot(both[...], right).astype(BF16)
                span = slice(column, column + widths[g])
                for y in range(ys):
                    block = product[y * deep : (y + 1) * deep]
                    if order[1] == "x":
                        outs[x][y, 0, :, span] = block
                    else:
                        outs[y][x, 0, :, span] = block
            column += widths[g]

    spec = pl.BlockSpec((second, 1, deep, sum(widths)), lambda z: (0, z, 0, 0))
    out = jax.ShapeDtypeStruct((second, DEPTH, deep, sum(widths)), BF16)
    ins = []
    for left, other, mine, theirs in groups:
        ins += [kept(left), kept(other)] + [split(r) for r in [*mine, *theirs]]
    return call(
        kernel,
        "outer",
        ins,
        [(out, spec)] * first,
        [pltpu.VMEM((ys * deep, 2 * rows), BF16)] * len(groups),
        tokens,
    )


def probabilities(limits_ref, keys, query):
    pieces = []
    for j, key in enumerate(keys):
        score = dot(key, query, NT) * FACTOR
        place = lax.broadcasted_iota(jnp.int32, score.shape, 0)
        pieces.append(jnp.where(place < limits_ref[j], score, NEGATIVE))
    highest = functools.reduce(
        jnp.maximum, [jnp.max(p, axis=0, keepdims=True) for p in pieces]
    )
    raised = [jnp.exp(p - highest) for p in pieces]
    total = functools.reduce(jnp.add, [jnp.sum(r, axis=0, keepdims=True) for r in raised])
    return raised, 1.0 / total


def total_of(items):
    return functools.reduce(jnp.add, items)


def attend(limits, query, keys, values, tokens):
    rows, _ = query.shape
    parts = len(keys)
    step = min(256, rows)

    def kernel(limits_ref, q_ref, *refs):
        k_refs, v_refs, out_ref = (refs[:parts], refs[parts : 2 * parts], refs[2 * parts])
        for pair in range(q_ref.shape[1] // 128):

            def part(i, carry, pair=pair):
                at = pl.ds(pl.multiple_of(i * step, step), step)
                done = []
                for head in (2 * pair, 2 * pair + 1):
                    here = slice(head * HEAD_DIM, (head + 1) * HEAD_DIM)
                    raised, share = probabilities(
                        limits_ref, [k[:, here] for k in k_refs], q_ref[at, here]
                    )
                    done.append(
                        total_of(
                            dot(v[:, here].T, (r * share).astype(BF16))
                            for v, r in zip(v_refs, raised, strict=True)
                        )
                    )
                out_ref[at, pair * 128 : pair * 128 + 128] = (
                    jnp.concatenate(done, axis=0).T.astype(BF16)
                )
                return carry

            lax.fori_loop(0, rows // step, part, 0)

    return call(
        kernel,
        "attend",
        [(limits, pl.BlockSpec(memory_space=pltpu.SMEM))]
        + [split(v) for v in [query, *keys, *values]],
        [split(query)],
        tokens=tokens,
    )[0]


def attend_back(limits, query, grad, keys, values, tokens):
    parts = len(keys)

    def kernel(limits_ref, q_ref, g_ref, *refs):
        k_refs, v_refs, refs = (refs[:parts], refs[parts : 2 * parts], refs[2 * parts :])
        dq_ref, dk_refs, dv_refs = (refs[0], refs[1 : 1 + parts], refs[1 + parts : 1 + 2 * parts])
        sums_ref = refs[-1]
        sums_ref[...] = jnp.zeros_like(sums_ref)
        for pair in range(q_ref.shape[1] // 128):
            done_q, done_k, done_v = ([], [], [])
            for head in (2 * pair, 2 * pair + 1):
                here = slice(head * HEAD_DIM, (head + 1) * HEAD_DIM)
                query_here = q_ref[:, here]
                grad_here = g_ref[:, here]
                raised, share = probabilities(limits_ref, [k[:, here] for k in k_refs], query_here)
                probs = [r * share for r in raised]
                grad_probs = [dot(v[:, here], grad_here, NT) for v in v_refs]
                mean = total_of(
                    jnp.sum(p * g, axis=0, keepdims=True)
                    for p, g in zip(probs, grad_probs, strict=True)
                )
                grad_scores = [
                    (p * (g - mean)).astype(BF16) for p, g in zip(probs, grad_probs, strict=True)
                ]
                done_v.append([dot(p.astype(BF16), grad_here) for p in probs])
                done_k.append([dot(s, query_here) * FACTOR for s in grad_scores])
                done_q.append(
                    total_of(
                        dot(k[:, here].T, s) for k, s in zip(k_refs, grad_scores, strict=True)
                    )
                    * FACTOR
                )
            cols = slice(pair * 128, pair * 128 + 128)
            low = jnp.concatenate(done_q, axis=0).T.astype(BF16)
            dq_ref[:, cols] = low
            sums_ref[0:1, cols] = jnp.sum(low.astype(F32), axis=0, keepdims=True)
            for j in range(parts):
                dk_refs[j][:, cols] = jnp.concatenate([d[j] for d in done_k], axis=1).astype(BF16)
                grad_value = jnp.concatenate([d[j] for d in done_v], axis=1)
                dv_refs[j][:, cols] = grad_value.astype(BF16)
                sums_ref[1:2, cols] += jnp.sum(grad_value, axis=0, keepdims=True)

    return call(
        kernel,
        "attend_back",
        [(limits, pl.BlockSpec(memory_space=pltpu.SMEM))]
        + [split(v) for v in [query, grad, *keys, *values]],
        [split(query)] * (1 + 2 * parts) + [split(shape(8, query.shape[1], F32))],
        tokens=tokens,
    )


def shards(
    hidden_in,
    cotangent,
    seq_lengths,
    slot_of,
    project,
    offsets,
    combiner,
    recenter,
    stretch,
    displace,
    expand,
    uplift,
    shrink,
    lowering,
    restretch,
    redisplace,
):
    ys, xs = (lax.axis_size("y"), lax.axis_size("x"))
    y, core, z, x = (lax.axis_index(axis) for axis in ANY_AXES)
    rows, width = hidden_in.shape
    slots_here = seq_lengths.shape[0] // (2 * ys)
    parts = xs
    heads_here = HEADS // (DEPTH * xs)
    wide = heads_here * HEAD_DIM
    paired = parts == 2
    if paired:
        trade = [(a * xs + b, b * xs + a) for a in range(2) for b in range(xs) if a != b]
        axis, place, slot_row = ("core", core, 2 * y + x)
    else:
        axis, place, slot_row = ("x", x, 2 * y + core)

    def regroup(value):
        if not paired:
            return value
        return jnp.where(core == x, value, lax.ppermute(value, ("core", "x"), trade))

    def features(value):
        return relative_blocks(value, ("y", "core"))

    slot = slot_row * slots_here + z
    length = jnp.sum(jnp.where(slot_of == slot, seq_lengths, 0))
    limits = jnp.stack([length - ((place - j) % parts) * rows for j in range(parts)])

    def heads_first(block):
        return (
            block.reshape(-1, heads_here, 3, HEAD_DIM).transpose(0, 2, 1, 3).reshape(block.shape)
        )

    start = features(regroup(hidden_in))
    blocks = []
    for layer in range(LAYERS):
        blocks.append(
            (
                jnp.concatenate([heads_first(project[layer]), combiner[layer].T], axis=1),
                expand[layer],
                shrink[layer].T,
            )
        )
    span_project, span_combiner = ((0, 3 * wide), (3 * wide, 4 * wide))
    span_hidden = (0, expand.shape[2])
    gathers = [
        [Gather(b, order) for b, order in zip(blocks[layer], ORDERS[layer], strict=True)]
        for layer in range(LAYERS)
    ]
    biases = jnp.concatenate([offsets.reshape(-1), uplift.reshape(-1)])
    biases = jnp.stack(spread(jnp.stack(spread(biases, "x")), "z"))
    biases = biases.reshape(DEPTH * xs, -1)
    cut = offsets.size
    offsets_full = biases[:, :cut].reshape(-1, LAYERS, heads_here, 2, HEAD_DIM)
    uplift_full = biases[:, cut:].reshape(-1, LAYERS, uplift.shape[1])
    query_bias = offsets_full[:, :, :, 0].transpose(1, 0, 2, 3).reshape(LAYERS, -1)
    value_bias = offsets_full[:, :, :, 1].transpose(1, 0, 2, 3).reshape(LAYERS, -1)
    inner_bias = uplift_full.transpose(1, 0, 2).reshape(LAYERS, -1)

    recenter, stretch, displace, lowering, restretch, redisplace = features(
        jnp.stack([recenter, stretch, displace, lowering, restretch, redisplace])
    )
    nothing = jnp.zeros_like(recenter[0])

    def vectors(*items):
        return jnp.stack(list(items) + [nothing] * (8 - len(items)))

    def other_core(value):
        return pull(value, "core", 1)

    def advance(*flows):
        return sum([flow.advance() for flow in flows], [])

    half = start.reshape(rows, ys, 2, -1)[:, :, 1].reshape(rows, -1)
    saved = []
    current_low, base, base_gain, base_shift, scaled = (start, start, nothing, nothing, False)
    finished = None
    (a0, e0, s0), (a1, e1, s1) = gathers
    waits = forward_waits(a0, e0, s0, a1, e1, s1)
    for layer in range(LAYERS):
        order_a, order_e, order_s = ORDERS[layer]
        gather_a, gather_e, gather_s = gathers[layer]
        weights_a = gather_a.pieces()
        query, key, value = queries(
            current_low,
            weights_a,
            order_a,
            vectors(query_bias[layer], value_bias[layer]),
            ys,
            xs,
            advance(*waits[layer]["queries"]),
        )
        keys = spread(key, axis)
        values = spread(value, axis)
        context = attend(limits, query, keys, values, advance(*waits[layer]["attend"]))
        normal_one, inverse_one, normed_low, normed_half = norm(
            context,
            weights_a,
            order_a,
            span_combiner,
            base,
            vectors(base_gain, base_shift, recenter[layer], stretch[layer], displace[layer]),
            scaled,
            False,
            ys,
            xs,
            advance(*waits[layer]["norm"]),
        )
        weights_e = gather_e.pieces()
        active, slope = hidden(
            normed_low,
            weights_e,
            order_e,
            jnp.broadcast_to(inner_bias[layer][None], (8, inner_bias.shape[1])),
            ys,
            xs,
            advance(*waits[layer]["hidden"]),
        )
        weights_s = gather_s.pieces()
        normal_two, inverse_two, next_low, next_half, *finished = norm(
            active,
            weights_s,
            order_s,
            span_hidden,
            normal_one,
            vectors(
                stretch[layer], displace[layer], lowering[layer], restretch[layer], redisplace[layer]
            ),
            True,
            layer == LAYERS - 1,
            ys,
            xs,
            advance(*waits[layer]["norm_two"]),
        )
        saved.append(
            {
                "low": current_low,
                "low_half": other_core(half),
                "query": query,
                "keys": keys,
                "values": values,
                "context": context,
                "context_other": other_core(context),
                "one": (normal_one, inverse_one),
                "normed": normed_low,
                "normed_half": other_core(normed_half),
                "active": active,
                "active_other": other_core(active),
                "slope": slope,
                "two": (normal_two, inverse_two, vectors(restretch[layer])),
                "weights": (weights_a, weights_e, weights_s),
            }
        )
        current_low, half, base, scaled = (next_low, next_half, normal_two, True)
        base_gain, base_shift = (restretch[layer], redisplace[layer])
    hidden_out = regroup(features(finished[0]))

    upstream = features(regroup(cotangent))
    grad_two, low_two, half_two, sums_two = norm_back(
        [], [], None, None, upstream, saved[-1]["two"], ys, xs, []
    )
    flows = {}
    small = []
    hidden_grad = None

    def turn(*names):
        return advance(*[flows[name] for name in names if name in flows])

    for layer in reversed(range(LAYERS)):
        kept_here = saved[layer]
        weights_a, weights_e, weights_s = kept_here["weights"]
        order_a, order_e, order_s = ORDERS[layer]
        above = layer + 1
        grad_inner, sums_inner = hidden_back(
            low_two,
            weights_s,
            order_s,
            kept_here["slope"],
            ys,
            xs,
            turn(("s", above)),
        )
        out_s = outer(
            [(low_two, other_core(half_two), [kept_here["active"]], [kept_here["active_other"]])],
            order_s,
            ys,
            xs,
            turn(("e", above)),
        )
        flows["s", layer] = Scatter(out_s, order_s)
        grad_one, low_one, half_one, sums_one = norm_back(
            [grad_inner],
            weights_e,
            order_e,
            span_hidden,
            grad_two,
            (*kept_here["one"], vectors(stretch[layer])),
            ys,
            xs,
            out_s + turn(("p", above)),
        )
        out_e = outer(
            [
                (
                    kept_here["normed"],
                    kept_here["normed_half"],
                    [grad_inner],
                    [other_core(grad_inner)],
                ),
                (
                    low_one,
                    other_core(half_one),
                    [kept_here["context"]],
                    [kept_here["context_other"]],
                ),
            ],
            order_e,
            ys,
            xs,
            turn(("s", above)),
        )
        flows["e", layer] = Scatter(out_e, order_e)
        grad_context = context_back(low_one, weights_a, order_a, ys, xs, out_e)
        grad_query, *pieces, sums_attend = attend_back(
            limits,
            kept_here["query"],
            grad_context,
            kept_here["keys"],
            kept_here["values"],
            turn(("e", above), ("p", above)),
        )
        grad_key = total_of(
            p.astype(F32) for p in [pieces[0]] + send(pieces[:parts], axis)
        ).astype(BF16)
        grad_value = total_of(
            p.astype(F32) for p in [pieces[parts]] + send(pieces[parts:], axis)
        ).astype(BF16)
        triple = [grad_query, grad_key, grad_value]
        small.append((sums_one, sums_two, sums_inner, sums_attend))
        result = norm_back(
            triple,
            weights_a,
            order_a,
            span_project,
            grad_one,
            saved[layer - 1]["two"] if layer > 0 else None,
            ys,
            xs,
            turn(("s", layer), ("p", above)),
        )
        if layer > 0:
            grad_two, low_two, half_two, sums_two = result
        else:
            hidden_grad = regroup(features(result[0]))
        out_p = outer(
            [
                (
                    kept_here["low"],
                    kept_here["low_half"],
                    triple,
                    [other_core(t) for t in triple],
                )
            ],
            order_a,
            ys,
            xs,
            turn(("e", layer)),
        )
        flows["p", layer] = Scatter(out_p, order_a)

    def ordered(items):
        return jnp.stack(items, axis=0)

    def hidden_order(value):
        return relative_blocks(value, ("z", "x"))

    totals = []
    for sums_one, sums_two, sums_inner, sums_attend in small[::-1]:
        totals.append(
            add_over(
                jnp.concatenate(
                    [features(sums_one[:3]).reshape(-1), features(sums_two[:3]).reshape(-1)]
                    + [hidden_order(sums_inner[0]), hidden_order(sums_attend[:2]).reshape(-1)]
                ),
                ANY_AXES,
            )
        )
    total = ordered(totals)
    norms = total[:, : 6 * width].reshape(LAYERS, 6, width)
    rest = total[:, 6 * width :]
    units = rest.shape[1] - 2 * width
    here = z * xs + x

    def own(flat):
        columns = flat.reshape(LAYERS, DEPTH * xs, -1)
        return lax.dynamic_index_in_dim(columns, here, 1, keepdims=False)

    uplift_grad = own(rest[:, :units])
    query_grad = own(rest[:, units : units + width]).reshape(LAYERS, heads_here, HEAD_DIM)
    value_grad = own(rest[:, units + width :]).reshape(LAYERS, heads_here, HEAD_DIM)
    offsets_grad = jnp.stack([query_grad, value_grad], axis=2).reshape(LAYERS, -1)

    def heads_last(block):
        return (
            block.reshape(-1, 3, heads_here, HEAD_DIM).transpose(0, 2, 1, 3).reshape(block.shape)
        )

    shrink_grad = ordered([flows["s", layer].finish().T for layer in range(LAYERS)])
    wide_grads = [flows["e", layer].finish() for layer in range(LAYERS)]
    expand_grad = ordered([m[:, : span_hidden[1]] for m in wide_grads])
    combiner_grad = ordered([m[:, span_hidden[1] :].T for m in wide_grads])
    project_grad = ordered([heads_last(flows["p", layer].finish()) for layer in range(LAYERS)])
    return (
        hidden_out,
        hidden_grad,
        project_grad,
        offsets_grad,
        combiner_grad,
        norms[:, 2],
        norms[:, 1],
        norms[:, 0],
        expand_grad,
        uplift_grad,
        shrink_grad,
        norms[:, 5],
        norms[:, 4],
        norms[:, 3],
    )


def solution(mesh):
    rows, columns = (mesh.shape["row"], mesh.shape["col"])
    fine = Mesh(mesh.devices.reshape(rows // 2, 2, DEPTH, columns // DEPTH), ANY_AXES)
    row, col = (("y", "core"), ("z", "x"))
    in_specs = (
        P(ANY_AXES, None),
        P(ANY_AXES, None),
        P(),
        P(),
        P(None, row, col),
        P(None, col),
        P(None, col, row),
        P(),
        P(),
        P(),
        P(None, row, col),
        P(None, col),
        P(None, col, row),
        P(),
        P(),
        P(),
    )
    out_specs = (
        P(ANY_AXES, None),
        P(ANY_AXES, None),
        P(None, row, col),
        P(None, col),
        P(None, col, row),
        P(),
        P(),
        P(),
        P(None, row, col),
        P(None, col),
        P(None, col, row),
        P(),
        P(),
        P(),
    )
    return jax.shard_map(shards, mesh=fine, in_specs=in_specs, out_specs=out_specs, check_vma=False)
```

time: 2870 us -> 971 us (0.34)
  waiting for transfers between devices: 2050 us -> 353 us
  matrix products: 355 us -> 0 us
  Pallas kernels: 0 us -> 351 us
  local copies, waits for them, and re-layouts: 222 us -> 55.4 us
  starting transfers between devices: 2.17 us -> 131 us
  blocking collectives: 82 us -> 0 us
  other arithmetic: 128 us -> 65.8 us
    reduce_scatter x16 -> x0, waiting for transfers between devices: 1110 us -> none  [the longest x8 1110 us: settle(): lax.psum_scatter(partial_value.astype(jnp.bfloat16), 'col', scatter_dimen...]
    all_gather x12 -> x0, waiting for transfers between devices: 938 us -> none  [the longest x4 466 us: features(): return lax.all_gather(value, 'col', axis=0, tiled=True)]
    dot_general x136 -> x0, matrix products: 355 us -> none  [the longest x8 69.5 us: weight_grad(): lax.dot_general(left, right, (((0,), (0,)), ((), ())), preferred_element_...]
    ppermute x0 -> x120, waiting for transfers between devices: none -> 353 us  [the longest x82 224 us: pull(): lax.ppermute(value, axis, [(i, (i + step) % size) for i in range(size)])]
    pallas_call x0 -> x27, Pallas kernels: none -> 351 us  [call(): pl.pallas_call(body, grid=(DEPTH,), in_specs=[pl.BlockSpec(memory_space=p...]
    ppermute x0 -> x120, starting transfers between devices: none -> 131 us  [the longest x82 75 us: pull(): lax.ppermute(value, axis, [(i, (i + step) % size) for i in range(size)])]
    reduce_sum x37 -> x1, other arithmetic: 65.9 us -> 0.63 us  [shards(): length = jnp.sum(jnp.where(slot_of == slot, seq_lengths, 0))]
    psum x2 -> x0, blocking collectives: 50.6 us -> none  [the longest x1 43.6 us: shards(): lax.psum((ordered(grads_recenter), ordered(grads_stretch), ordered(grads_...]
  transfers between devices with their start and end apart: 28 -> 120, of which waited for: 19 -> 32; matrix products, arithmetic and copies ran while one was open for 10% -> 10% of each run, Pallas kernels for 0% -> 37%
where the time goes in v2:
time: 971 us; the launch traced here: 961 us
  waiting for transfers between devices  353 us (36%)
  Pallas kernels  351 us (36%)
  starting transfers between devices  131 us (13%)
  other arithmetic  65.8 us (7%)
  local copies, waits for them, and re-layouts  55.4 us (6%)
    pallas_call x27, Pallas kernels, call(): pl.pallas_call(body, grid=(DEPTH,), in_specs=[pl.BlockSpec(memory_space=p...  351 us
    ppermute x82, waiting for transfers between devices, pull(): lax.ppermute(value, axis, [(i, (i + step) % size) for i in range(size)])  224 us
    ppermute x34, waiting for transfers between devices, push(): lax.ppermute(value, axis, [(i, (i - step) % size) for i in range(size)])  129 us
    ppermute x82, starting transfers between devices, pull(): lax.ppermute(value, axis, [(i, (i + step) % size) for i in range(size)])  75 us
    ppermute x34, starting transfers between devices, push(): lax.ppermute(value, axis, [(i, (i - step) % size) for i in range(size)])  48.7 us
    unnamed x278, local copies, waits for them, and re-layouts  28.1 us
    another operation x14, other arithmetic, advance(): value = jnp.stack(self.parts)  24.4 us
  transfers between devices with their start and end apart: 120, of which 32 were waited for; matrix products, arithmetic and copies ran while one was open for 10% of the time, Pallas kernels for 37%

profile of v2, /device:TPU:0, one launch (start us, length us, event | category | flops | bytes accessed | tf_op | source)
XLA Modules:
  0.0 960.9 jit_solution(11821757742019302506)
XLA Ops:
  3.1 5.1 collective-permute-start.30
  9.2 5.7 collective-permute-done.30
  15.0 15.6 %collective-permute-done.29 = bf16[256,512]{1,0:T(8,128)(2,1)S(1)} collective-permute-done((bf16[256,512]{1,0:T(8,128)(2,1)S(1)}, bf16[256,512]{1,0:T(8,128)(2,1)S(1)}, u32[]{:S(2)}, u32[]{:S(2)}) %collective-permute-start.29) | collective-permute-done | bytes 262176 | tf_op jit(solution)/shard_map/ppermute | solution.py:35
  35.2 2.9 collective-permute-start.1
  41.6 13.4 %collective-permute-done.31 = bf16[4,256,512]{2,1,0:T(8,128)(2,1)} collective-permute-done((bf16[4,256,512]{2,1,0:T(8,128)(2,1)S(1)}, bf16[4,256,512]{2,1,0:T(8,128)(2,1)}, u32[]{:S(2)}, u32[]{:S(2)}) %collective-permute-start.31) | collective-permute-done | bytes 1048608 | tf_op jit(solution)/shard_map/ppermute | solution.py:35
  67.4 3.3 collective-permute-done.21
  70.6 4.3 collective-permute-start.7
  75.0 23.4 %collective-permute-done.20 = bf16[256,512]{1,0:T(8,128)(2,1)S(1)} collective-permute-done((bf16[256,512]{1,0:T(8,128)(2,1)S(1)}, bf16[256,512]{1,0:T(8,128)(2,1)S(1)}, u32[]{:S(2)}, u32[]{:S(2)}) %collective-permute-start.20) | collective-permute-done | bytes 262176 | tf_op jit(solution)/shard_map/ppermute | solution.py:35
  103.4 13.6 %collective-permute-done.6 = bf16[256,512]{1,0:T(8,128)(2,1)} collective-permute-done((bf16[256,512]{1,0:T(8,128)(2,1)}, bf16[256,512]{1,0:T(8,128)(2,1)}, u32[]{:S(2)}, u32[]{:S(2)}) %collective-permute-start.6) | collective-permute-done | bytes 262176 | tf_op jit(solution)/shard_map/ppermute | solution.py:35
  117.0 8.0 collective-permute-start.14
  126.3 18.7 %collective-permute-done.15 = bf16[256,512]{1,0:T(8,128)(2,1)} collective-permute-done((bf16[256,512]{1,0:T(8,128)(2,1)S(1)}, bf16[256,512]{1,0:T(8,128)(2,1)}, u32[]{:S(2)}, u32[]{:S(2)}) %collective-permute-start.15) | collective-permute-done | bytes 262176 | tf_op jit(solution)/shard_map/ppermute | solution.py:35
  149.0 3.0 fusion.33
  158.0 6.7 collective-permute-done.10
  169.3 13.8 %collective-permute-done.3 = bf16[4,256,512]{2,1,0:T(8,128)(2,1)} collective-permute-done((bf16[4,256,512]{2,1,0:T(8,128)(2,1)S(1)}, bf16[4,256,512]{2,1,0:T(8,128)(2,1)}, u32[]{:S(2)}, u32[]{:S(2)}) %collective-permute-start.3) | collective-permute-done | bytes 1048608 | tf_op jit(solution)/shard_map/ppermute | solution.py:35
  187.6 58.2 %collective-permute-done.8 = bf16[4,256,512]{2,1,0:T(8,128)(2,1)S(1)} collective-permute-done((bf16[4,256,512]{2,1,0:T(8,128)(2,1)S(1)}, bf16[4,256,512]{2,1,0:T(8,128)(2,1)S(1)}, u32[]{:S(2)}, u32[]{:S(2)}) %collective-permute-start.8) | collective-permute-done | bytes 1048608 | tf_op jit(solution)/shard_map/ppermute | solution.py:35
  248.8 2.9 pad_maximum_fusion.2.refs_0_.refs_3_.refs_4_.refs_8_
  255.4 8.3 queries.2
  263.7 30.8 %collective-permute-done.18.refs_0_.refs_6_.refs_4_ = bf16[2,4,256,512]{3,2,1,0:T(8,128)(2,1)} collective-permute-done((bf16[2,4,256,512]{3,2,1,0:T(8,128)(2,1)}, bf16[2,4,256,512]{3,2,1,0:T(8,128)(2,1)}, u32[]{:S(2)}, u32[]{:S(2)}) %collective-permute-start.18) | collective-permute-done | bytes 2097184 | tf_op jit(solution)/shard_map/ppermute | solution.py:35
  295.0 5.1 collective-permute-done.42.refs_4_.refs_5_.refs_9_
  310.2 26.2 %attend.2.refs_2_.refs_7_ = bf16[512,1024]{1,0:T(8,128)(2,1)S(1)} custom-call(bf16[2,4,256,512]{3,2,1,0:T(8,128)(2,1)} %pad_maximum_fusion.3.refs_0_.refs_5_.refs_3_, s32[2]{0:T(128)S(1)} %pad_add_fusion.refs_1_.refs_0_.refs_2_, bf16[512,1024]{1,0:T(8,128)(2,1)} %copy-done.11, bf16[512,1024]{1,0:T(8,128)(2,1)} %get-tuple-element.84.refs_3_.refs_5_, ...), custom_call_target="tpu_custom_call" | custom-call | flops 1000 | bytes 1000 | tf_op jit(solution)/shard_map/attend/pallas_call | solution.py:182
  337.4 9.0 norm.4
  348.2 12.6 %hidden.2 = (bf16[512,4096]{1,0:T(8,128)(2,1)}, bf16[512,4096]{1,0:T(8,128)(2,1)}) custom-call(bf16[2,4,256,512]{3,2,1,0:T(8,128)(2,1)} %collective-permute-done.18.refs_0_.refs_6_.refs_4_, bf16[4,256,512]{2,1,0:T(8,128)(2,1)S(1)} %get-tuple-element.217.refs_1_, bf16[512,1024]{1,0:T(8,128)(2,1)} %copy-done.5, f32[8,4096]{1,0:T(8,128)S(1)} %broadcast_in_dim.20.refs_3_, ...), custom_call_target="tpu_custom_call" | custom-call | flops 1000 | bytes 1000 | tf_op jit(solution)/shard_map/hidden/pallas_call | solution.py:182
  360.7 12.1 %norm.5 = (f32[512,1024]{1,0:T(8,128)}, f32[512,128]{1,0:T(8,128)S(1)}, bf16[512,1024]{1,0:T(8,128)(2,1)S(1)}, bf16[512,512]{1,0:T(8,128)(2,1)S(1)}) custom-call(bf16[2,4,256,512]{3,2,1,0:T(8,128)(2,1)} %pad_maximum_fusion.2.refs_0_.refs_3_.refs_4_.refs_8_, bf16[4,256,512]{2,1,0:T(8,128)(2,1)} %copy-done.48, ...), custom_call_target="tpu_custom_call" | custom-call | flops 1000 | bytes 1000 | tf_op jit(solution)/shard_map/norm/pallas_call | solution.py:182
  373.9 7.9 queries.3
  389.8 26.4 %attend.3.refs_1_.refs_6_ = bf16[512,1024]{1,0:T(8,128)(2,1)S(1)} custom-call(bf16[2,4,256,512]{3,2,1,0:T(8,128)(2,1)} %pad_maximum_fusion.refs_0_.refs_3_.refs_2_, s32[2]{0:T(128)S(1)} %pad_add_fusion.refs_1_.refs_0_.refs_2_, bf16[512,1024]{1,0:T(8,128)(2,1)} %copy-done.8, bf16[512,1024]{1,0:T(8,128)(2,1)} %get-tuple-element.91.refs_3_, ...), custom_call_target="tpu_custom_call" | custom-call | flops 1000 | bytes 1000 | tf_op jit(solution)/shard_map/attend/pallas_call | solution.py:182
  417.3 9.3 norm.6
  426.6 12.6 %hidden.3 = (bf16[512,4096]{1,0:T(8,128)(2,1)}, bf16[512,4096]{1,0:T(8,128)(2,1)}) custom-call(bf16[2,4,256,512]{3,2,1,0:T(8,128)(2,1)} %collective-permute-done.4.refs_0_.refs_4_.refs_3_, bf16[512,1024]{1,0:T(8,128)(2,1)S(1)} %get-tuple-element.94.refs_1_.refs_0_, f32[8,4096]{1,0:T(8,128)S(1)} %broadcast_in_dim.22.refs_2_, ...), custom_call_target="tpu_custom_call" | custom-call | flops 1000 | bytes 1000 | tf_op jit(solution)/shard_map/hidden/pallas_call | solution.py:182
  443.1 13.4 %norm.7 = (f32[512,1024]{1,0:T(8,128)}, f32[512,128]{1,0:T(8,128)S(1)}, bf16[512,1024]{1,0:T(8,128)(2,1)}, bf16[512,512]{1,0:T(8,128)(2,1)}, f32[512,1024]{1,0:T(8,128)}) custom-call(bf16[512,4096]{1,0:T(8,128)(2,1)} %get-tuple-element.95.refs_0_.refs_2_, f32[512,1024]{1,0:T(8,128)} %get-tuple-element.96.refs_1_.refs_4_, f32[8,1024]{1,0:T(8,128)S(1)} %stack.333.refs_2_, ...), custom_call_target="tpu_custom_call" | custom-call | flops 1000 | bytes 1000 | tf_op jit(solution)/shard_map/norm/pallas_call | solution.py:182
  456.6 5.4 norm_back.5
  461.9 10.6 %hidden_back.2 = (bf16[512,4096]{1,0:T(8,128)(2,1)}, f32[8,4096]{1,0:T(8,128)S(1)}) custom-call(bf16[512,1024]{1,0:T(8,128)(2,1)S(1)} %get-tuple-element.101.refs_0_, bf16[512,4096]{1,0:T(8,128)(2,1)} %get-tuple-element.102.refs_1_, bf16[2,4,256,512]{3,2,1,0:T(8,128)(2,1)} %pad_maximum_fusion.refs_0_.refs_3_.refs_2_, ...), custom_call_target="tpu_custom_call" | custom-call | flops 1000 | bytes 1000 | tf_op jit(solution)/shard_map/hidden_back/pallas_call | solution.py:182
  483.8 9.0 outer.6
  492.8 12.8 %norm_back.6 = (f32[512,1024]{1,0:T(8,128)}, bf16[512,1024]{1,0:T(8,128)(2,1)S(1)}, bf16[512,512]{1,0:T(8,128)(2,1)S(1)}, f32[8,1024]{1,0:T(8,128)S(1)}) custom-call(bf16[2,4,256,512]{3,2,1,0:T(8,128)(2,1)} %get-tuple-element.105.refs_0_, bf16[2,4,256,512]{3,2,1,0:T(8,128)(2,1)} %get-tuple-element.106.refs_1_, bf16[512,4096]{1,0:T(8,128)(2,1)} %get-tuple-element.103.refs_2_, ...), custom_call_target="tpu_custom_call" | custom-call | flops 1000 | bytes 1000 | tf_op jit(solution)/shard_map/norm_back/pallas_call | solution.py:182
  508.5 12.9 %outer.7 = (bf16[2,4,256,640]{3,2,1,0:T(8,128)(2,1)}, bf16[2,4,256,640]{3,2,1,0:T(8,128)(2,1)}) custom-call(bf16[512,1024]{1,0:T(8,128)(2,1)} %copy-done.14, bf16[512,512]{1,0:T(8,128)(2,1)S(1)} %collective-permute-done.52.refs_1_, bf16[512,4096]{1,0:T(8,128)(2,1)} %get-tuple-element.103.refs_2_, bf16[512,4096]{1,0:T(8,128)(2,1)} %collective-permute-done.54.refs_3_, ...), custom_call_target="tpu_custom_call" | custom-call | flops 1000 | bytes 1000 | tf_op jit(solution)/shard_map/outer/pallas_call | solution.py:182
  521.7 5.1 context_back.2.refs_2_
  527.8 34.8 %attend_back.2 = (bf16[512,1024]{1,0:T(8,128)(2,1)S(1)}, bf16[512,1024]{1,0:T(8,128)(2,1)}, bf16[512,1024]{1,0:T(8,128)(2,1)}, bf16[512,1024]{1,0:T(8,128)(2,1)}...) custom-call(s32[2]{0:T(128)S(1)} %pad_add_fusion.refs_1_.refs_0_.refs_2_, bf16[512,1024]{1,0:T(8,128)(2,1)} %copy-done.8, ...), custom_call_target="tpu_custom_call" | custom-call | flops 1000 | bytes 1000 | tf_op jit(solution)/shard_map/attend_back/pallas_call | solution.py:182
  565.2 4.9 slice_reduce_fusion
  575.1 3.0 add_convert_fusion.9.refs_2_.refs_4_
  578.2 2.8 add_convert_fusion.8.refs_3_.refs_5_
  587.3 12.0 %norm_back.7 = (f32[512,1024]{1,0:T(8,128)}, bf16[512,1024]{1,0:T(8,128)(2,1)S(1)}, bf16[512,512]{1,0:T(8,128)(2,1)S(1)}, f32[8,1024]{1,0:T(8,128)S(1)}) custom-call(bf16[2,4,256,512]{3,2,1,0:T(8,128)(2,1)} %copy-done.28, bf16[512,1024]{1,0:T(8,128)(2,1)} %copy-done.6, bf16[512,1024]{1,0:T(8,128)(2,1)} %add_convert_fusion.9.refs_2_.refs_4_, ...), custom_call_target="tpu_custom_call" | custom-call | flops 1000 | bytes 1000 | tf_op jit(solution)/shard_map/norm_back/pallas_call | solution.py:182
  604.1 8.2 outer.9
  615.2 3.0 collective-permute-start.81
  618.2 11.0 %hidden_back.3 = (bf16[512,4096]{1,0:T(8,128)(2,1)}, f32[8,4096]{1,0:T(8,128)S(1)}) custom-call(bf16[4,256,512]{2,1,0:T(8,128)(2,1)S(1)} %fusion.3.refs_0_, bf16[512,1024]{1,0:T(8,128)(2,1)} %copy-done.9, bf16[512,4096]{1,0:T(8,128)(2,1)} %get-tuple-element.128.refs_2_, bf16[2,4,256,512]{3,2,1,0:T(8,128)(2,1)} %pad_maximum_fusion.3.refs_0_.refs_5_.refs_3_, ...), custom_call_target="tpu_custom_call" | custom-call | flops 1000 | bytes 1000 | tf_op jit(solution)/shard_map/hidden_back/pallas_call | solution.py:182
  629.9 3.1 collective-permute-start.80
  633.0 3.2 collective-permute-done.81
  636.1 4.9 collective-permute-done.80
  644.6 3.0 collective-permute-start.77
  647.9 8.9 outer.8
  656.8 9.7 %collective-permute-done.71 = bf16[2,4,256,384]{3,2,1,0:T(8,128)(2,1)S(1)} collective-permute-done((bf16[2,4,256,384]{3,2,1,0:T(8,128)(2,1)}, bf16[2,4,256,384]{3,2,1,0:T(8,128)(2,1)S(1)}, u32[]{:S(2)}, u32[]{:S(2)}) %collective-permute-start.71) | collective-permute-done | bytes 1572896 | tf_op jit(solution)/shard_map/ppermute | solution.py:40
  668.6 12.9 %norm_back.8 = (f32[512,1024]{1,0:T(8,128)}, bf16[512,1024]{1,0:T(8,128)(2,1)S(1)}, bf16[512,512]{1,0:T(8,128)(2,1)S(1)}, f32[8,1024]{1,0:T(8,128)S(1)}) custom-call(bf16[2,4,256,512]{3,2,1,0:T(8,128)(2,1)} %get-tuple-element.122.refs_0_, bf16[2,4,256,512]{3,2,1,0:T(8,128)(2,1)} %get-tuple-element.123.refs_1_, bf16[2,4,256,384]{3,2,1,0:T(8,128)(2,1)} %copy-done.30, ...), custom_call_target="tpu_custom_call" | custom-call | flops 1000 | bytes 1000 | tf_op jit(solution)/shard_map/norm_back/pallas_call | solution.py:182
  694.9 3.0 collective-permute-start.74
  697.9 12.9 %outer.10 = (bf16[2,4,256,640]{3,2,1,0:T(8,128)(2,1)}, bf16[2,4,256,640]{3,2,1,0:T(8,128)(2,1)}) custom-call(f32[256,512]{1,0:T(8,128)S(1)} %fusion.14.refs_0_, bf16[512,1024]{1,0:T(8,128)(2,1)} %copy-done.5, bf16[512,512]{1,0:T(8,128)(2,1)S(1)} %collective-permute-done.83.refs_2_, bf16[512,4096]{1,0:T(8,128)(2,1)} %get-tuple-element.129.refs_3_, ...), custom_call_target="tpu_custom_call" | custom-call | flops 1000 | bytes 1000 | tf_op jit(solution)/shard_map/outer/pallas_call | solution.py:182
  710.7 5.1 context_back.3.refs_4_
  716.8 3.0 collective-permute-start.73
  719.8 34.5 %attend_back.3 = (bf16[512,1024]{1,0:T(8,128)(2,1)}, bf16[512,1024]{1,0:T(8,128)(2,1)}, bf16[512,1024]{1,0:T(8,128)(2,1)}, bf16[512,1024]{1,0:T(8,128)(2,1)}, bf...) custom-call(f32[256,640]{1,0:T(8,128)S(1)} %fusion.9.refs_0_, bf16[4,256,384]{2,1,0:T(8,128)(2,1)S(1)} %fusion.5.refs_1_, ...), custom_call_target="tpu_custom_call" | custom-call | flops 1000 | bytes 1000 | tf_op jit(solution)/shard_map/attend_back/pallas_call | solution.py:182
  765.2 2.9 add_convert_fusion.2.refs_0_
  783.0 66.4 %collective-permute-done.116 = bf16[4,256,512]{2,1,0:T(8,128)(2,1)S(1)} collective-permute-done((bf16[4,256,512]{2,1,0:T(8,128)(2,1)S(1)}, bf16[4,256,512]{2,1,0:T(8,128)(2,1)S(1)}, u32[]{:S(2)}, u32[]{:S(2)}) %collective-permute-start.116) | collective-permute-done | bytes 1048608 | tf_op jit(solution)/shard_map/ppermute | solution.py:40
  856.2 9.5 norm_back.9
  869.0 8.2 outer.11
  888.3 10.4 %collective-permute-done.118 = bf16[256,512]{1,0:T(8,128)(2,1)S(1)} collective-permute-done((bf16[256,512]{1,0:T(8,128)(2,1)S(1)}, bf16[256,512]{1,0:T(8,128)(2,1)S(1)}, u32[]{:S(2)}, u32[]{:S(2)}) %collective-permute-start.118) | collective-permute-done | bytes 262176 | tf_op jit(solution)/shard_map/ppermute | solution.py:40
  903.5 5.9 collective-permute-start.115
  911.9 7.9 collective-permute-done.95
  924.8 8.5 collective-permute-done.114
  933.5 7.3 collective-permute-done.96
  948.8 10.3 %collective-permute-done.98 = bf16[256,384]{1,0:T(8,128)(2,1)S(1)} collective-permute-done((bf16[256,384]{1,0:T(8,128)(2,1)S(1)}, bf16[256,384]{1,0:T(8,128)(2,1)S(1)}, u32[]{:S(2)}, u32[]{:S(2)}) %collective-permute-start.98) | collective-permute-done | bytes 196640 | tf_op jit(solution)/shard_map/ppermute | solution.py:40
  (639 shorter events, 207.7 us)
Async XLA Ops:
  30.7 24.2 %collective-permute-start.31 = (bf16[4,256,512]{2,1,0:T(8,128)(2,1)S(1)}, bf16[4,256,512]{2,1,0:T(8,128)(2,1)}, u32[]{:S(2)}, u32[]{:S(2)}) collective-permute-start(bf16[4,256,512]{2,1,0:T(8,128)(2,1)S(1)} %get-tuple-element.205), channel_id=1, source_target_pairs={{0,16},{16,0},{1,17},{17,1},{2,18},{18,2},{3,19},{19,3},{4,20},{20... | collective-permute-start | bytes 3145736 | tf_op jit(solution)/shard_map/ppermute | solution.py:35
  35.1 30.0 %collective-permute-start.2 = (bf16[256,512]{1,0:T(8,128)(2,1)S(1)}, bf16[256,512]{1,0:T(8,128)(2,1)S(1)}, u32[]{:S(2)}, u32[]{:S(2)}) collective-permute-start(bf16[256,512]{1,0:T(8,128)(2,1)S(1)} %bitcast.329), channel_id=1, source_target_pairs={{0,6},{2,0},{4,2},{6,4},{1,7},{3,1},{5,3},{7,5},{8,14},{10,8},{12,... | collective-permute-start | bytes 786440 | tf_op jit(solution)/shard_map/ppermute | solution.py:35
  35.2 30.0 %collective-permute-start.1 = (bf16[256,512]{1,0:T(8,128)(2,1)S(1)}, bf16[256,512]{1,0:T(8,128)(2,1)S(1)}, u32[]{:S(2)}, u32[]{:S(2)}) collective-permute-start(bf16[256,512]{1,0:T(8,128)(2,1)S(1)} %bitcast.330), channel_id=1, source_target_pairs={{0,4},{2,6},{4,0},{6,2},{1,5},{3,7},{5,1},{7,3},{8,12},{10,14},{12... | collective-permute-start | bytes 786440 | tf_op jit(solution)/shard_map/ppermute | solution.py:35
  58.8 106.7 %collective-permute-start.32 = (bf16[2,4,256,512]{3,2,1,0:T(8,128)(2,1)}, bf16[2,4,256,512]{3,2,1,0:T(8,128)(2,1)}, u32[]{:S(2)}, u32[]{:S(2)}) collective-permute-start(bf16[2,4,256,512]{3,2,1,0:T(8,128)(2,1)} %pad_maximum_fusion.5.refs_4_.refs_5_.refs_3_.refs_6_), channel_id=1, source_target_pairs={{0,1},{1,0},{2,3},{3,2},{4,5},{5,4},{6,7},{7,6},{8,9},{9,8},{10,11... | collective-permute-start | bytes 6291464 | tf_op jit(solution)/shard_map/ppermute | solution.py:35
  63.9 34.5 %collective-permute-start.20 = (bf16[256,512]{1,0:T(8,128)(2,1)S(1)}, bf16[256,512]{1,0:T(8,128)(2,1)S(1)}, u32[]{:S(2)}, u32[]{:S(2)}) collective-permute-start(bf16[256,512]{1,0:T(8,128)(2,1)S(1)} %get-tuple-element.228), channel_id=1, source_target_pairs={{0,4},{2,6},{4,0},{6,2},{1,5},{3,7},{5,1},{7,3},{8,12},{10,14},{12... | collective-permute-start | bytes 786440 | tf_op jit(solution)/shard_map/ppermute | solution.py:35
  65.2 33.2 %collective-permute-start.19 = (bf16[256,512]{1,0:T(8,128)(2,1)S(1)}, bf16[256,512]{1,0:T(8,128)(2,1)S(1)}, u32[]{:S(2)}, u32[]{:S(2)}) collective-permute-start(bf16[256,512]{1,0:T(8,128)(2,1)S(1)} %get-tuple-element.228), channel_id=1, source_target_pairs={{0,2},{2,4},{4,6},{6,0},{1,3},{3,5},{5,7},{7,1},{8,10},{10,12},{12... | collective-permute-start | bytes 786440 | tf_op jit(solution)/shard_map/ppermute | solution.py:35
  65.2 33.4 %collective-permute-start = (bf16[256,512]{1,0:T(8,128)(2,1)S(1)}, bf16[256,512]{1,0:T(8,128)(2,1)S(1)}, u32[]{:S(2)}, u32[]{:S(2)}) collective-permute-start(bf16[256,512]{1,0:T(8,128)(2,1)S(1)} %bitcast.331), channel_id=1, source_target_pairs={{0,2},{2,4},{4,6},{6,0},{1,3},{3,5},{5,7},{7,1},{8,10},{10,12},{12... | collective-permute-start | bytes 786440 | tf_op jit(solution)/shard_map/ppermute | solution.py:35
  70.6 30.1 %collective-permute-start.7 = (bf16[256,512]{1,0:T(8,128)(2,1)}, bf16[256,512]{1,0:T(8,128)(2,1)S(1)}, u32[]{:S(2)}, u32[]{:S(2)}) collective-permute-start(bf16[256,512]{1,0:T(8,128)(2,1)} %get-tuple-element.227), channel_id=1, source_target_pairs={{0,6},{2,0},{4,2},{6,4},{1,7},{3,1},{5,3},{7,5},{8,14},{10,8},{12,... | collective-permute-start | bytes 786440 | tf_op jit(solution)/shard_map/ppermute | solution.py:35
  98.6 56.3 %collective-permute-start.22 = (bf16[4,256,512]{2,1,0:T(8,128)(2,1)S(1)}, bf16[4,256,512]{2,1,0:T(8,128)(2,1)}, u32[]{:S(2)}, u32[]{:S(2)}) collective-permute-start(bf16[4,256,512]{2,1,0:T(8,128)(2,1)S(1)} %get-tuple-element.211.refs_0_), channel_id=1, source_target_pairs={{0,1},{1,0},{2,3},{3,2},{4,5},{5,4},{6,7},{7,6},{8,9},{9,8},{10,11... | collective-permute-start | bytes 3145736 | tf_op jit(solution)/shard_map/ppermute | solution.py:35
  100.7 25.6 %collective-permute-start.16 = (bf16[256,512]{1,0:T(8,128)(2,1)S(1)}, bf16[256,512]{1,0:T(8,128)(2,1)}, u32[]{:S(2)}, u32[]{:S(2)}) collective-permute-start(bf16[256,512]{1,0:T(8,128)(2,1)S(1)} %bitcast.333), channel_id=1, source_target_pairs={{0,6},{2,0},{4,2},{6,4},{1,7},{3,1},{5,3},{7,5},{8,14},{10,8},{12,... | collective-permute-start | bytes 786440 | tf_op jit(solution)/shard_map/ppermute | solution.py:35
  117.0 28.1 %collective-permute-start.15 = (bf16[256,512]{1,0:T(8,128)(2,1)S(1)}, bf16[256,512]{1,0:T(8,128)(2,1)}, u32[]{:S(2)}, u32[]{:S(2)}) collective-permute-start(bf16[256,512]{1,0:T(8,128)(2,1)S(1)} %bitcast.334), channel_id=1, source_target_pairs={{0,4},{2,6},{4,0},{6,2},{1,5},{3,7},{5,1},{7,3},{8,12},{10,14},{12... | collective-permute-start | bytes 786440 | tf_op jit(solution)/shard_map/ppermute | solution.py:35
  117.0 28.1 %collective-permute-start.14 = (bf16[256,512]{1,0:T(8,128)(2,1)S(1)}, bf16[256,512]{1,0:T(8,128)(2,1)}, u32[]{:S(2)}, u32[]{:S(2)}) collective-permute-start(bf16[256,512]{1,0:T(8,128)(2,1)S(1)} %bitcast.335), channel_id=1, source_target_pairs={{0,2},{2,4},{4,6},{6,0},{1,3},{3,5},{5,7},{7,1},{8,10},{10,12},{12... | collective-permute-start | bytes 786440 | tf_op jit(solution)/shard_map/ppermute | solution.py:35
  126.3 25.7 %collective-permute-start.12 = (bf16[256,512]{1,0:T(8,128)(2,1)}, bf16[256,512]{1,0:T(8,128)(2,1)S(1)}, u32[]{:S(2)}, u32[]{:S(2)}) collective-permute-start(bf16[256,512]{1,0:T(8,128)(2,1)} %get-tuple-element.237), channel_id=1, source_target_pairs={{0,6},{2,0},{4,2},{6,4},{1,7},{3,1},{5,3},{7,5},{8,14},{10,8},{12,... | collective-permute-start | bytes 786440 | tf_op jit(solution)/shard_map/ppermute | solution.py:35
  152.0 31.1 %collective-permute-start.3 = (bf16[4,256,512]{2,1,0:T(8,128)(2,1)S(1)}, bf16[4,256,512]{2,1,0:T(8,128)(2,1)}, u32[]{:S(2)}, u32[]{:S(2)}) collective-permute-start(bf16[4,256,512]{2,1,0:T(8,128)(2,1)S(1)} %get-tuple-element.219.refs_1_), channel_id=1, source_target_pairs={{0,1},{1,0},{2,3},{3,2},{4,5},{5,4},{6,7},{7,6},{8,9},{9,8},{10,11... | collective-permute-start | bytes 3145736 | tf_op jit(solution)/shard_map/ppermute | solution.py:35
  153.4 31.3 %collective-permute-start.17 = (bf16[4,256,512]{2,1,0:T(8,128)(2,1)}, bf16[4,256,512]{2,1,0:T(8,128)(2,1)}, u32[]{:S(2)}, u32[]{:S(2)}) collective-permute-start(bf16[4,256,512]{2,1,0:T(8,128)(2,1)} %get-tuple-element.213.refs_1_), channel_id=1, source_target_pairs={{0,16},{16,0},{1,17},{17,1},{2,18},{18,2},{3,19},{19,3},{4,20},{20... | collective-permute-start | bytes 3145736 | tf_op jit(solution)/shard_map/ppermute | solution.py:35
  164.7 87.0 %collective-permute-start.33 = (bf16[2,4,256,512]{3,2,1,0:T(8,128)(2,1)}, bf16[2,4,256,512]{3,2,1,0:T(8,128)(2,1)}, u32[]{:S(2)}, u32[]{:S(2)}) collective-permute-start(bf16[2,4,256,512]{3,2,1,0:T(8,128)(2,1)} %pad_maximum_fusion.5.refs_4_.refs_5_.refs_3_.refs_6_), channel_id=1, source_target_pairs={{0,8},{8,0},{1,9},{9,1},{2,10},{10,2},{3,11},{11,3},{4,12},{12,4},... | collective-permute-start | bytes 6291464 | tf_op jit(solution)/shard_map/ppermute | solution.py:35
  164.7 87.0 %collective-permute-start.37 = (bf16[2,4,256,512]{3,2,1,0:T(8,128)(2,1)}, bf16[2,4,256,512]{3,2,1,0:T(8,128)(2,1)}, u32[]{:S(2)}, u32[]{:S(2)}) collective-permute-start(bf16[2,4,256,512]{3,2,1,0:T(8,128)(2,1)} %pad_maximum_fusion.4.refs_0_.refs_4_.refs_8_), channel_id=1, source_target_pairs={{0,16},{16,0},{1,17},{17,1},{2,18},{18,2},{3,19},{19,3},{4,20},{20... | collective-permute-start | bytes 6291464 | tf_op jit(solution)/shard_map/ppermute | solution.py:35
  165.6 87.8 %collective-permute-start.34 = (bf16[2,4,256,512]{3,2,1,0:T(8,128)(2,1)}, bf16[2,4,256,512]{3,2,1,0:T(8,128)(2,1)}, u32[]{:S(2)}, u32[]{:S(2)}) collective-permute-start(bf16[2,4,256,512]{3,2,1,0:T(8,128)(2,1)} %collective-permute-done.32.refs_5_.refs_6_.refs_4_.refs_7_), channel_id=1, source_target_pairs={{0,8},{8,0},{1,9},{9,1},{2,10},{10,2},{3,11},{11,3},{4,12},{12,4},... | collective-permute-start | bytes 6291464 | tf_op jit(solution)/shard_map/ppermute | solution.py:35
  183.1 62.7 %collective-permute-start.8 = (bf16[4,256,512]{2,1,0:T(8,128)(2,1)S(1)}, bf16[4,256,512]{2,1,0:T(8,128)(2,1)S(1)}, u32[]{:S(2)}, u32[]{:S(2)}) collective-permute-start(bf16[4,256,512]{2,1,0:T(8,128)(2,1)S(1)} %get-tuple-element.217.refs_1_), channel_id=1, source_target_pairs={{0,16},{16,0},{1,17},{17,1},{2,18},{18,2},{3,19},{19,3},{4,20},{20... | collective-permute-start | bytes 3145736 | tf_op jit(solution)/shard_map/ppermute | solution.py:35
  184.6 61.2 %collective-permute-start.13 = (bf16[4,256,512]{2,1,0:T(8,128)(2,1)S(1)}, bf16[4,256,512]{2,1,0:T(8,128)(2,1)S(1)}, u32[]{:S(2)}, u32[]{:S(2)}) collective-permute-start(bf16[4,256,512]{2,1,0:T(8,128)(2,1)S(1)} %get-tuple-element.215.refs_1_), channel_id=1, source_target_pairs={{0,1},{1,0},{2,3},{3,2},{4,5},{5,4},{6,7},{7,6},{8,9},{9,8},{10,11... | collective-permute-start | bytes 3145736 | tf_op jit(solution)/shard_map/ppermute | solution.py:35
  245.8 48.6 %collective-permute-start.38 = (bf16[2,4,256,512]{3,2,1,0:T(8,128)(2,1)}, bf16[2,4,256,512]{3,2,1,0:T(8,128)(2,1)}, u32[]{:S(2)}, u32[]{:S(2)}) collective-permute-start(bf16[2,4,256,512]{3,2,1,0:T(8,128)(2,1)} %pad_maximum_fusion.4.refs_0_.refs_4_.refs_8_), channel_id=1, source_target_pairs={{0,8},{8,0},{1,9},{9,1},{2,10},{10,2},{3,11},{11,3},{4,12},{12,4},... | collective-permute-start | bytes 6291464 | tf_op jit(solution)/shard_map/ppermute | solution.py:35
  246.8 47.6 %collective-permute-start.18 = (bf16[2,4,256,512]{3,2,1,0:T(8,128)(2,1)}, bf16[2,4,256,512]{3,2,1,0:T(8,128)(2,1)}, u32[]{:S(2)}, u32[]{:S(2)}) collective-permute-start(bf16[2,4,256,512]{3,2,1,0:T(8,128)(2,1)} %pad_maximum_fusion.3.refs_0_.refs_5_.refs_3_), channel_id=1, source_target_pairs={{0,1},{1,0},{2,3},{3,2},{4,5},{5,4},{6,7},{7,6},{8,9},{9,8},{10,11... | collective-permute-start | bytes 6291464 | tf_op jit(solution)/shard_map/ppermute | solution.py:35
  251.7 43.2 %collective-permute-start.40 = (bf16[2,4,256,512]{3,2,1,0:T(8,128)(2,1)}, bf16[2,4,256,512]{3,2,1,0:T(8,128)(2,1)}, u32[]{:S(2)}, u32[]{:S(2)}) collective-permute-start(bf16[2,4,256,512]{3,2,1,0:T(8,128)(2,1)} %pad_maximum_fusion.3.refs_0_.refs_5_.refs_3_), channel_id=1, source_target_pairs={{0,8},{8,0},{1,9},{9,1},{2,10},{10,2},{3,11},{11,3},{4,12},{12,4},... | collective-permute-start | bytes 6291464 | tf_op jit(solution)/shard_map/ppermute | solution.py:35
  251.7 48.4 %collective-permute-start.42 = (bf16[2,4,256,512]{3,2,1,0:T(8,128)(2,1)}, bf16[2,4,256,512]{3,2,1,0:T(8,128)(2,1)}, u32[]{:S(2)}, u32[]{:S(2)}) collective-permute-start(bf16[2,4,256,512]{3,2,1,0:T(8,128)(2,1)} %pad_maximum_fusion.2.refs_0_.refs_3_.refs_4_.refs_8_), channel_id=1, source_target_pairs={{0,16},{16,0},{1,17},{17,1},{2,18},{18,2},{3,19},{19,3},{4,20},{20... | collective-permute-start | bytes 6291464 | tf_op jit(solution)/shard_map/ppermute | solution.py:35
  253.3 46.8 %collective-permute-start.39 = (bf16[2,4,256,512]{3,2,1,0:T(8,128)(2,1)}, bf16[2,4,256,512]{3,2,1,0:T(8,128)(2,1)}, u32[]{:S(2)}, u32[]{:S(2)}) collective-permute-start(bf16[2,4,256,512]{3,2,1,0:T(8,128)(2,1)} %collective-permute-done.37.refs_5_.refs_9_), channel_id=1, source_target_pairs={{0,8},{8,0},{1,9},{9,1},{2,10},{10,2},{3,11},{11,3},{4,12},{12,4},... | collective-permute-start | bytes 6291464 | tf_op jit(solution)/shard_map/ppermute | solution.py:35
  295.0 65.8 %collective-permute-start.41 = (bf16[2,4,256,512]{3,2,1,0:T(8,128)(2,1)}, bf16[2,4,256,512]{3,2,1,0:T(8,128)(2,1)}, u32[]{:S(2)}, u32[]{:S(2)}) collective-permute-start(bf16[2,4,256,512]{3,2,1,0:T(8,128)(2,1)} %collective-permute-done.18.refs_0_.refs_6_.refs_4_), channel_id=1, source_target_pairs={{0,8},{8,0},{1,9},{9,1},{2,10},{10,2},{3,11},{11,3},{4,12},{12,4},... | collective-permute-start | bytes 6291464 | tf_op jit(solution)/shard_map/ppermute | solution.py:35
  300.1 73.8 %collective-permute-start.43 = (bf16[2,4,256,512]{3,2,1,0:T(8,128)(2,1)}, bf16[2,4,256,512]{3,2,1,0:T(8,128)(2,1)}, u32[]{:S(2)}, u32[]{:S(2)}) collective-permute-start(bf16[2,4,256,512]{3,2,1,0:T(8,128)(2,1)} %pad_maximum_fusion.2.refs_0_.refs_3_.refs_4_.refs_8_), channel_id=1, source_target_pairs={{0,8},{8,0},{1,9},{9,1},{2,10},{10,2},{3,11},{11,3},{4,12},{12,4},... | collective-permute-start | bytes 6291464 | tf_op jit(solution)/shard_map/ppermute | solution.py:35
  300.1 73.8 %collective-permute-start.44 = (bf16[2,4,256,512]{3,2,1,0:T(8,128)(2,1)}, bf16[2,4,256,512]{3,2,1,0:T(8,128)(2,1)}, u32[]{:S(2)}, u32[]{:S(2)}) collective-permute-start(bf16[2,4,256,512]{3,2,1,0:T(8,128)(2,1)} %collective-permute-done.42.refs_4_.refs_5_.refs_9_), channel_id=1, source_target_pairs={{0,8},{8,0},{1,9},{9,1},{2,10},{10,2},{3,11},{11,3},{4,12},{12,4},... | collective-permute-start | bytes 6291464 | tf_op jit(solution)/shard_map/ppermute | solution.py:35
  302.1 81.2 %collective-permute-start.9 = (bf16[2,4,256,512]{3,2,1,0:T(8,128)(2,1)}, bf16[2,4,256,512]{3,2,1,0:T(8,128)(2,1)}, u32[]{:S(2)}, u32[]{:S(2)}) collective-permute-start(bf16[2,4,256,512]{3,2,1,0:T(8,128)(2,1)} %pad_maximum_fusion.1.refs_0_.refs_3_.refs_7_), channel_id=1, source_target_pairs={{0,1},{1,0},{2,3},{3,2},{4,5},{5,4},{6,7},{7,6},{8,9},{9,8},{10,11... | collective-permute-start | bytes 6291464 | tf_op jit(solution)/shard_map/ppermute | solution.py:35
  306.5 77.3 %collective-permute-start.4 = (bf16[2,4,256,512]{3,2,1,0:T(8,128)(2,1)}, bf16[2,4,256,512]{3,2,1,0:T(8,128)(2,1)}, u32[]{:S(2)}, u32[]{:S(2)}) collective-permute-start(bf16[2,4,256,512]{3,2,1,0:T(8,128)(2,1)} %pad_maximum_fusion.refs_0_.refs_3_.refs_2_), channel_id=1, source_target_pairs={{0,16},{16,0},{1,17},{17,1},{2,18},{18,2},{3,19},{19,3},{4,20},{20... | collective-permute-start | bytes 6291464 | tf_op jit(solution)/shard_map/ppermute | solution.py:35
  383.3 43.2 %collective-permute-start.47 = (bf16[2,4,256,512]{3,2,1,0:T(8,128)(2,1)}, bf16[2,4,256,512]{3,2,1,0:T(8,128)(2,1)}, u32[]{:S(2)}, u32[]{:S(2)}) collective-permute-start(bf16[2,4,256,512]{3,2,1,0:T(8,128)(2,1)} %pad_maximum_fusion.1.refs_0_.refs_3_.refs_7_), channel_id=1, source_target_pairs={{0,8},{8,0},{1,9},{9,1},{2,10},{10,2},{3,11},{11,3},{4,12},{12,4},... | collective-permute-start | bytes 6291464 | tf_op jit(solution)/shard_map/ppermute | solution.py:35
  383.3 43.2 %collective-permute-start.48 = (bf16[2,4,256,512]{3,2,1,0:T(8,128)(2,1)}, bf16[2,4,256,512]{3,2,1,0:T(8,128)(2,1)}, u32[]{:S(2)}, u32[]{:S(2)}) collective-permute-start(bf16[2,4,256,512]{3,2,1,0:T(8,128)(2,1)} %collective-permute-done.9.refs_0_.refs_4_.refs_8_), channel_id=1, source_target_pairs={{0,8},{8,0},{1,9},{9,1},{2,10},{10,2},{3,11},{11,3},{4,12},{12,4},... | collective-permute-start | bytes 6291464 | tf_op jit(solution)/shard_map/ppermute | solution.py:35
  383.9 55.4 %collective-permute-start.53 = (f32[512,1024]{1,0:T(8,128)}, f32[512,1024]{1,0:T(8,128)}, u32[]{:S(2)}, u32[]{:S(2)}) collective-permute-start(f32[512,1024]{1,0:T(8,128)} %param.17), channel_id=1, source_target_pairs={{1,8},{8,1},{3,10},{10,3},{5,12},{12,5},{7,14},{14,7},{17,24},{24,... | collective-permute-start | bytes 6291464 | tf_op jit(solution)/shard_map/ppermute | solution.py:650
  385.8 57.3 %collective-permute-start.49 = (bf16[2,4,256,512]{3,2,1,0:T(8,128)(2,1)}, bf16[2,4,256,512]{3,2,1,0:T(8,128)(2,1)}, u32[]{:S(2)}, u32[]{:S(2)}) collective-permute-start(bf16[2,4,256,512]{3,2,1,0:T(8,128)(2,1)} %pad_maximum_fusion.refs_0_.refs_3_.refs_2_), channel_id=1, source_target_pairs={{0,8},{8,0},{1,9},{9,1},{2,10},{10,2},{3,11},{11,3},{4,12},{12,4},... | collective-permute-start | bytes 6291464 | tf_op jit(solution)/shard_map/ppermute | solution.py:35
  388.7 54.4 %collective-permute-start.50 = (bf16[2,4,256,512]{3,2,1,0:T(8,128)(2,1)}, bf16[2,4,256,512]{3,2,1,0:T(8,128)(2,1)}, u32[]{:S(2)}, u32[]{:S(2)}) collective-permute-start(bf16[2,4,256,512]{3,2,1,0:T(8,128)(2,1)} %collective-permute-done.4.refs_0_.refs_4_.refs_3_), channel_id=1, source_target_pairs={{0,8},{8,0},{1,9},{9,1},{2,10},{10,2},{3,11},{11,3},{4,12},{12,4},... | collective-permute-start | bytes 6291464 | tf_op jit(solution)/shard_map/ppermute | solution.py:35
  439.2 42.7 %collective-permute-start.56 = (bf16[512,4096]{1,0:T(8,128)(2,1)}, bf16[512,4096]{1,0:T(8,128)(2,1)S(1)}, u32[]{:S(2)}, u32[]{:S(2)}) collective-permute-start(bf16[512,4096]{1,0:T(8,128)(2,1)} %get-tuple-element.95.refs_0_.refs_2_), channel_id=1, source_target_pairs={{0,8},{8,0},{1,9},{9,1},{2,10},{10,2},{3,11},{11,3},{4,12},{12,4},... | collective-permute-start | bytes 12582920 | tf_op jit(solution)/shard_map/ppermute | solution.py:35
  472.5 34.7 %collective-permute-start.54 = (bf16[512,4096]{1,0:T(8,128)(2,1)}, bf16[512,4096]{1,0:T(8,128)(2,1)}, u32[]{:S(2)}, u32[]{:S(2)}) collective-permute-start(bf16[512,4096]{1,0:T(8,128)(2,1)} %get-tuple-element.103.refs_2_), channel_id=1, source_target_pairs={{0,8},{8,0},{1,9},{9,1},{2,10},{10,2},{3,11},{11,3},{4,12},{12,4},... | collective-permute-start | bytes 12582920 | tf_op jit(solution)/shard_map/ppermute | solution.py:35
  476.4 94.7 %collective-permute-start.51 = (f32[512,1024]{1,0:T(8,128)}, f32[512,1024]{1,0:T(8,128)}, u32[]{:S(2)}, u32[]{:S(2)}) collective-permute-start(f32[512,1024]{1,0:T(8,128)} %pad_maximum_fusion.6), channel_id=1, source_target_pairs={{1,8},{8,1},{3,10},{10,3},{5,12},{12,5},{7,14},{14,7},{17,24},{24,... | collective-permute-start | bytes 6291464 | tf_op jit(solution)/shard_map/ppermute | solution.py:650
  479.9 27.3 %collective-permute-start.58 = (bf16[512,1024]{1,0:T(8,128)(2,1)S(1)}, bf16[512,1024]{1,0:T(8,128)(2,1)S(1)}, u32[]{:S(2)}, u32[]{:S(2)}) collective-permute-start(bf16[512,1024]{1,0:T(8,128)(2,1)S(1)} %copy-done.4), channel_id=1, source_target_pairs={{0,8},{8,0},{1,9},{9,1},{2,10},{10,2},{3,11},{11,3},{4,12},{12,4},... | collective-permute-start | bytes 3145736 | tf_op jit(solution)/shard_map/ppermute | solution.py:35
  481.5 25.2 %collective-permute-start.52 = (bf16[512,512]{1,0:T(8,128)(2,1)S(1)}, bf16[512,512]{1,0:T(8,128)(2,1)S(1)}, u32[]{:S(2)}, u32[]{:S(2)}) collective-permute-start(bf16[512,512]{1,0:T(8,128)(2,1)S(1)} %get-tuple-element.98), channel_id=1, source_target_pairs={{0,8},{8,0},{1,9},{9,1},{2,10},{10,2},{3,11},{11,3},{4,12},{12,4},... | collective-permute-start | bytes 1572872 | tf_op jit(solution)/shard_map/ppermute | solution.py:35
  506.7 74.4 %collective-permute-start.61 = (bf16[2,4,256,512]{3,2,1,0:T(8,128)(2,1)}, bf16[2,4,256,512]{3,2,1,0:T(8,128)(2,1)}, u32[]{:S(2)}, u32[]{:S(2)}) collective-permute-start(bf16[2,4,256,512]{3,2,1,0:T(8,128)(2,1)} %get-tuple-element.106.refs_1_), channel_id=1, source_target_pairs={{0,16},{16,0},{1,17},{17,1},{2,18},{18,2},{3,19},{19,3},{4,20},{20... | collective-permute-start | bytes 6291464 | tf_op jit(solution)/shard_map/ppermute | solution.py:40
  521.3 64.1 %collective-permute-start.59 = (bf16[2,4,256,640]{3,2,1,0:T(8,128)(2,1)}, bf16[2,4,256,640]{3,2,1,0:T(8,128)(2,1)}, u32[]{:S(2)}, u32[]{:S(2)}) collective-permute-start(bf16[2,4,256,640]{3,2,1,0:T(8,128)(2,1)} %get-tuple-element.112.refs_1_), channel_id=1, source_target_pairs={{0,1},{1,0},{2,3},{3,2},{4,5},{5,4},{6,7},{7,6},{8,9},{9,8},{10,11... | collective-permute-start | bytes 7864328 | tf_op jit(solution)/shard_map/ppermute | solution.py:40
  571.1 73.5 %collective-permute-start.65 = (bf16[512,4096]{1,0:T(8,128)(2,1)}, bf16[512,4096]{1,0:T(8,128)(2,1)}, u32[]{:S(2)}, u32[]{:S(2)}) collective-permute-start(bf16[512,4096]{1,0:T(8,128)(2,1)} %get-tuple-element.87.refs_2_.refs_3_), channel_id=1, source_target_pairs={{0,8},{8,0},{1,9},{9,1},{2,10},{10,2},{3,11},{11,3},{4,12},{12,4},... | collective-permute-start | bytes 12582920 | tf_op jit(solution)/shard_map/ppermute | solution.py:35
  578.1 24.2 %collective-permute-start.68 = (bf16[512,1024]{1,0:T(8,128)(2,1)S(1)}, bf16[512,1024]{1,0:T(8,128)(2,1)}, u32[]{:S(2)}, u32[]{:S(2)}) collective-permute-start(bf16[512,1024]{1,0:T(8,128)(2,1)S(1)} %get-tuple-element.113.refs_1_.refs_3_), channel_id=1, source_target_pairs={{0,8},{8,0},{1,9},{9,1},{2,10},{10,2},{3,11},{11,3},{4,12},{12,4},... | collective-permute-start | bytes 3145736 | tf_op jit(solution)/shard_map/ppermute | solution.py:35
  585.4 28.1 %collective-permute-start.79 = (bf16[4,256,512]{2,1,0:T(8,128)(2,1)}, bf16[4,256,512]{2,1,0:T(8,128)(2,1)}, u32[]{:S(2)}, u32[]{:S(2)}) collective-permute-start(bf16[4,256,512]{2,1,0:T(8,128)(2,1)} %slice_bitcast_fusion.6), channel_id=1, source_target_pairs={{0,1},{1,0},{2,3},{3,2},{4,5},{5,4},{6,7},{7,6},{8,9},{9,8},{10,11... | collective-permute-start | bytes 3145736 | tf_op jit(solution)/shard_map/ppermute | solution.py:40
  602.3 38.9 %collective-permute-start.60 = (bf16[4,256,640]{2,1,0:T(8,128)(2,1)S(1)}, bf16[4,256,640]{2,1,0:T(8,128)(2,1)}, u32[]{:S(2)}, u32[]{:S(2)}) collective-permute-start(bf16[4,256,640]{2,1,0:T(8,128)(2,1)S(1)} %slice_bitcast_fusion.2), channel_id=1, source_target_pairs={{0,16},{16,0},{1,17},{17,1},{2,18},{18,2},{3,19},{19,3},{4,20},{20... | collective-permute-start | bytes 3932168 | tf_op jit(solution)/shard_map/ppermute | solution.py:40
  612.3 54.2 %collective-permute-start.71 = (bf16[2,4,256,384]{3,2,1,0:T(8,128)(2,1)}, bf16[2,4,256,384]{3,2,1,0:T(8,128)(2,1)S(1)}, u32[]{:S(2)}, u32[]{:S(2)}) collective-permute-start(bf16[2,4,256,384]{3,2,1,0:T(8,128)(2,1)} %get-tuple-element.126), channel_id=1, source_target_pairs={{0,16},{16,0},{1,17},{17,1},{2,18},{18,2},{3,19},{19,3},{4,20},{20... | collective-permute-start | bytes 4718600 | tf_op jit(solution)/shard_map/ppermute | solution.py:40
  641.0 56.8 %collective-permute-start.84 = (bf16[512,4096]{1,0:T(8,128)(2,1)}, bf16[512,4096]{1,0:T(8,128)(2,1)}, u32[]{:S(2)}, u32[]{:S(2)}) collective-permute-start(bf16[512,4096]{1,0:T(8,128)(2,1)} %get-tuple-element.129.refs_3_), channel_id=1, source_target_pairs={{0,8},{8,0},{1,9},{9,1},{2,10},{10,2},{3,11},{11,3},{4,12},{12,4},... | collective-permute-start | bytes 12582920 | tf_op jit(solution)/shard_map/ppermute | solution.py:35
  644.0 44.4 %collective-permute-start.78 = (bf16[256,640]{1,0:T(8,128)(2,1)}, bf16[256,640]{1,0:T(8,128)(2,1)}, u32[]{:S(2)}, u32[]{:S(2)}) collective-permute-start(bf16[256,640]{1,0:T(8,128)(2,1)} %get-tuple-element.196), channel_id=1, source_target_pairs={{0,2},{2,4},{4,6},{6,0},{1,3},{3,5},{5,7},{7,1},{8,10},{10,12},{12... | collective-permute-start | bytes 983048 | tf_op jit(solution)/shard_map/ppermute | solution.py:40
  644.6 43.9 %collective-permute-start.77 = (bf16[256,640]{1,0:T(8,128)(2,1)}, bf16[256,640]{1,0:T(8,128)(2,1)}, u32[]{:S(2)}, u32[]{:S(2)}) collective-permute-start(bf16[256,640]{1,0:T(8,128)(2,1)} %get-tuple-element.197), channel_id=1, source_target_pairs={{0,4},{2,6},{4,0},{6,2},{1,5},{3,7},{5,1},{7,3},{8,12},{10,14},{12... | collective-permute-start | bytes 983048 | tf_op jit(solution)/shard_map/ppermute | solution.py:40
  647.6 41.3 %collective-permute-start.76 = (bf16[256,640]{1,0:T(8,128)(2,1)}, bf16[256,640]{1,0:T(8,128)(2,1)}, u32[]{:S(2)}, u32[]{:S(2)}) collective-permute-start(bf16[256,640]{1,0:T(8,128)(2,1)} %get-tuple-element.195), channel_id=1, source_target_pairs={{0,6},{2,0},{4,2},{6,4},{1,7},{3,1},{5,3},{7,5},{8,14},{10,8},{12,... | collective-permute-start | bytes 983048 | tf_op jit(solution)/shard_map/ppermute | solution.py:40
  668.0 25.4 %collective-permute-start.72 = (bf16[4,256,384]{2,1,0:T(8,128)(2,1)}, bf16[4,256,384]{2,1,0:T(8,128)(2,1)}, u32[]{:S(2)}, u32[]{:S(2)}) collective-permute-start(bf16[4,256,384]{2,1,0:T(8,128)(2,1)} %slice_bitcast_fusion.10), channel_id=1, source_target_pairs={{0,1},{1,0},{2,3},{3,2},{4,5},{5,4},{6,7},{7,6},{8,9},{9,8},{10,11... | collective-permute-start | bytes 2359304 | tf_op jit(solution)/shard_map/ppermute | solution.py:40
  689.0 74.8 %collective-permute-start.66 = (bf16[2,4,256,512]{3,2,1,0:T(8,128)(2,1)}, bf16[2,4,256,512]{3,2,1,0:T(8,128)(2,1)}, u32[]{:S(2)}, u32[]{:S(2)}) collective-permute-start(bf16[2,4,256,512]{3,2,1,0:T(8,128)(2,1)} %get-tuple-element.123.refs_1_), channel_id=1, source_target_pairs={{0,1},{1,0},{2,3},{3,2},{4,5},{5,4},{6,7},{7,6},{8,9},{9,8},{10,11... | collective-permute-start | bytes 6291464 | tf_op jit(solution)/shard_map/ppermute | solution.py:40
  694.8 63.9 %collective-permute-start.75 = (bf16[256,384]{1,0:T(8,128)(2,1)S(1)}, bf16[256,384]{1,0:T(8,128)(2,1)S(1)}, u32[]{:S(2)}, u32[]{:S(2)}) collective-permute-start(bf16[256,384]{1,0:T(8,128)(2,1)S(1)} %get-tuple-element.224), channel_id=1, source_target_pairs={{0,2},{2,4},{4,6},{6,0},{1,3},{3,5},{5,7},{7,1},{8,10},{10,12},{12... | collective-permute-start | bytes 589832 | tf_op jit(solution)/shard_map/ppermute | solution.py:40
  694.9 65.2 %collective-permute-start.74 = (bf16[256,384]{1,0:T(8,128)(2,1)S(1)}, bf16[256,384]{1,0:T(8,128)(2,1)S(1)}, u32[]{:S(2)}, u32[]{:S(2)}) collective-permute-start(bf16[256,384]{1,0:T(8,128)(2,1)S(1)} %get-tuple-element.225), channel_id=1, source_target_pairs={{0,4},{2,6},{4,0},{6,2},{1,5},{3,7},{5,1},{7,3},{8,12},{10,14},{12... | collective-permute-start | bytes 589832 | tf_op jit(solution)/shard_map/ppermute | solution.py:40
  716.8 43.4 %collective-permute-start.73 = (bf16[256,384]{1,0:T(8,128)(2,1)S(1)}, bf16[256,384]{1,0:T(8,128)(2,1)S(1)}, u32[]{:S(2)}, u32[]{:S(2)}) collective-permute-start(bf16[256,384]{1,0:T(8,128)(2,1)S(1)} %get-tuple-element.223), channel_id=1, source_target_pairs={{0,6},{2,0},{4,2},{6,4},{1,7},{3,1},{5,3},{7,5},{8,14},{10,8},{12,... | collective-permute-start | bytes 589832 | tf_op jit(solution)/shard_map/ppermute | solution.py:40
  758.7 108.7 %collective-permute-start.91 = (bf16[512,512]{1,0:T(8,128)(2,1)}, bf16[512,512]{1,0:T(8,128)(2,1)S(1)}, u32[]{:S(2)}, u32[]{:S(2)}) collective-permute-start(bf16[512,512]{1,0:T(8,128)(2,1)} %bitcast.203), channel_id=1, source_target_pairs={{0,8},{8,0},{1,9},{9,1},{2,10},{10,2},{3,11},{11,3},{4,12},{12,4},... | collective-permute-start | bytes 1572872 | tf_op jit(solution)/shard_map/ppermute | solution.py:35
  768.2 84.4 %collective-permute-start.90 = (bf16[2,4,256,640]{3,2,1,0:T(8,128)(2,1)S(1)}, bf16[2,4,256,640]{3,2,1,0:T(8,128)(2,1)S(1)}, u32[]{:S(2)}, u32[]{:S(2)}) collective-permute-start(bf16[2,4,256,640]{3,2,1,0:T(8,128)(2,1)S(1)} %copy-done.60), channel_id=1, source_target_pairs={{0,16},{16,0},{1,17},{17,1},{2,18},{18,2},{3,19},{19,3},{4,20},{20... | collective-permute-start | bytes 7864328 | tf_op jit(solution)/shard_map/ppermute | solution.py:40
  779.6 69.8 %collective-permute-start.116 = (bf16[4,256,512]{2,1,0:T(8,128)(2,1)S(1)}, bf16[4,256,512]{2,1,0:T(8,128)(2,1)S(1)}, u32[]{:S(2)}, u32[]{:S(2)}) collective-permute-start(bf16[4,256,512]{2,1,0:T(8,128)(2,1)S(1)} %slice_bitcast_fusion.4), channel_id=1, source_target_pairs={{0,16},{16,0},{1,17},{17,1},{2,18},{18,2},{3,19},{19,3},{4,20},{20... | collective-permute-start | bytes 3145736 | tf_op jit(solution)/shard_map/ppermute | solution.py:40
  780.3 69.4 %collective-permute-start.87 = (bf16[512,1024]{1,0:T(8,128)(2,1)S(1)}, bf16[512,1024]{1,0:T(8,128)(2,1)S(1)}, u32[]{:S(2)}, u32[]{:S(2)}) collective-permute-start(bf16[512,1024]{1,0:T(8,128)(2,1)S(1)} %copy-done.111), channel_id=1, source_target_pairs={{0,8},{8,0},{1,9},{9,1},{2,10},{10,2},{3,11},{11,3},{4,12},{12,4},... | collective-permute-start | bytes 3145736 | tf_op jit(solution)/shard_map/ppermute | solution.py:40
  782.8 67.9 %collective-permute-start.88 = (bf16[512,1024]{1,0:T(8,128)(2,1)S(1)}, bf16[512,1024]{1,0:T(8,128)(2,1)S(1)}, u32[]{:S(2)}, u32[]{:S(2)}) collective-permute-start(bf16[512,1024]{1,0:T(8,128)(2,1)S(1)} %copy-done.110), channel_id=1, source_target_pairs={{0,8},{8,0},{1,9},{9,1},{2,10},{10,2},{3,11},{11,3},{4,12},{12,4},... | collective-permute-start | bytes 3145736 | tf_op jit(solution)/shard_map/ppermute | solution.py:40
  854.7 46.6 %collective-permute-start.112 = (bf16[4,256,640]{2,1,0:T(8,128)(2,1)}, bf16[4,256,640]{2,1,0:T(8,128)(2,1)}, u32[]{:S(2)}, u32[]{:S(2)}) collective-permute-start(bf16[4,256,640]{2,1,0:T(8,128)(2,1)} %slice_bitcast_fusion), channel_id=1, source_target_pairs={{0,1},{1,0},{2,3},{3,2},{4,5},{5,4},{6,7},{7,6},{8,9},{9,8},{10,11... | collective-permute-start | bytes 3932168 | tf_op jit(solution)/shard_map/ppermute | solution.py:40
  877.2 42.5 %collective-permute-start.95 = (bf16[2,4,256,384]{3,2,1,0:T(8,128)(2,1)}, bf16[2,4,256,384]{3,2,1,0:T(8,128)(2,1)}, u32[]{:S(2)}, u32[]{:S(2)}) collective-permute-start(bf16[2,4,256,384]{3,2,1,0:T(8,128)(2,1)} %get-tuple-element.143), channel_id=1, source_target_pairs={{0,1},{1,0},{2,3},{3,2},{4,5},{5,4},{6,7},{7,6},{8,9},{9,8},{10,11... | collective-permute-start | bytes 4718600 | tf_op jit(solution)/shard_map/ppermute | solution.py:40
  880.2 42.8 %collective-permute-start.89 = (f32[512,1024]{1,0:T(8,128)}, f32[512,1024]{1,0:T(8,128)}, u32[]{:S(2)}, u32[]{:S(2)}) collective-permute-start(f32[512,1024]{1,0:T(8,128)} %pad_maximum_fusion.8), channel_id=1, source_target_pairs={{1,8},{8,1},{3,10},{10,3},{5,12},{12,5},{7,14},{14,7},{17,24},{24,... | collective-permute-start | bytes 6291464 | tf_op jit(solution)/shard_map/ppermute | solution.py:650
  (168 other events, 2311.1 us)
